TPU v7x, 128 devices: a whole 4x4x4 slice. The times are simulated.
128 devices in a mesh: tier: 8 (over z, core), member: 16 (over y, x).
Axes of the slice: x: 4, y: 4, z: 4, core: 2. Of those that a mesh axis runs over, the one named last changes fastest.
Arguments:
- density: float32 [1024, 2, 9216], P(('tier', 'member')), may hold values from -6 to 6
- hamiltonian: float32 [96, 96], replicated, may hold values from -4 to 4, as said below
- coupling: float32 [96, 96, 96], replicated, may hold values from -2 to 2, as said below
- decay_rate: float32 [96], replicated, may hold values from 0.3 to 2
- corr_real: float32 [96], replicated, may hold values from 0.3 to 1.5
- corr_imag: float32 [96], replicated, may hold values from -1 to 1
- up_member: int32 [1024, 1], P(('tier', 'member')), may hold values from 0 to 15; in each aligned block of 8 rows (0 to 7, 8 to 15, ...) at most 2 rows name the same one
- up_slot: int32 [1024, 1], P(('tier', 'member')), may hold values from 0 to 7
- up_mode: int32 [1024, 1], P(('tier', 'member')), may hold values from 0 to 95
- down_member: int32 [1024, 1], P(('tier', 'member')), may hold values from 0 to 15; in each aligned block of 8 rows (0 to 7, 8 to 15, ...) at most 2 rows name the same one
- down_slot: int32 [1024, 1], P(('tier', 'member')), may hold values from 0 to 7
- down_mode: int32 [1024, 1], P(('tier', 'member')), may hold values from 0 to 95
Outputs:
- evolved: float32 [1024, 2, 9216], P(('tier', 'member'))
Inputs may be any that keep to these rules, and one draw needn't show every extreme that they name: `up_member`: among the rows of one device no member index is named by more than 2 rows, a bound that some block reaches. `down_member`: among the rows of one device no member index is named by more than 2 rows, a bound that some block reaches. `hamiltonian`: Symmetric. `coupling`: each mode's matrix is symmetric.
All inputs are finite; a program needn't handle non-finite values.
Results may differ from a plain program's by a relative error of at most 0.0003.
Values sent between devices are 32-bit elements; how exact they have to be, the bound alone decides.
No kernel may reach another device: no remote copies, remote signals or barrier semaphores. Data moves between devices by JAX's collectives and lax.ppermute only.
A program may use at most 128 MiB of HBM per device.

v0:
```python
import jax
import jax.numpy as jnp
from jax import lax
from jax.sharding import PartitionSpec as P

LINKS = 1


time_step = 0.08


def passed_along(value, axis, steps):
    count = lax.axis_size(axis)
    first, last = (max(0, -steps), min(count, count - steps))
    return lax.ppermute(value, axis, [(source, source + steps) for source in range(first, last)])


def matprod(left, right):
    return jnp.einsum("...ik,...kj->...ij", left, right, precision=lax.Precision.HIGHEST)


def linksum(left, right):
    return jnp.einsum("slik,slkj->sij", left, right, precision=lax.Precision.HIGHEST)


def own_terms(hamiltonian, states):
    real_part = states[:, 0]
    imag_part = states[:, 1]
    first = matprod(hamiltonian, imag_part) - matprod(imag_part, hamiltonian)
    second = matprod(real_part, hamiltonian) - matprod(hamiltonian, real_part)
    return jnp.stack([first, second], axis=1)


def lift_terms(operators, values):
    real_part = values[:, :, 0]
    imag_part = values[:, :, 1]
    first = linksum(operators, imag_part) - linksum(imag_part, operators)
    second = linksum(real_part, operators) - linksum(operators, real_part)
    return jnp.stack([first, second], axis=1)


def lower_terms(operators, values, coef_real, coef_imag):
    real_part = values[:, :, 0]
    imag_part = values[:, :, 1]
    scale_re = coef_real[:, :, None, None]
    scale_im = coef_imag[:, :, None, None]
    left_re = scale_re * real_part - scale_im * imag_part
    left_im = scale_im * real_part + scale_re * imag_part
    right_re = scale_re * real_part + scale_im * imag_part
    right_im = scale_im * real_part - scale_re * imag_part
    cross_real = linksum(operators, left_re) - linksum(right_re, operators)
    cross_imag = linksum(operators, left_im) + linksum(right_im, operators)
    return jnp.stack([cross_imag, -cross_real], axis=1)


def runge_kutta(states, derivative):
    section_one = derivative(states)
    section_two = derivative(states + 0.5 * time_step * section_one)
    section_three = derivative(states + 0.5 * time_step * section_two)
    section_four = derivative(states + time_step * section_three)
    return states + time_step / 6.0 * (
        section_one + 2.0 * section_two + 2.0 * section_three + section_four
    )


def build_requests(member_ids, slot_ids, mode_ids, member_count, capacity):
    onehot = (member_ids[:, None] == jnp.arange(member_count, dtype=jnp.int32)[None, :]).astype(
        jnp.int32
    )
    before = jnp.cumsum(onehot, axis=0) - onehot
    position = jnp.sum(before * onehot, axis=1)
    placed = onehot[:, :, None] * (
        position[:, None, None] == jnp.arange(capacity, dtype=jnp.int32)[None, None, :]
    ).astype(jnp.int32)
    pairs = jnp.stack([slot_ids, mode_ids], axis=1)
    request_table = jnp.sum(placed[:, :, :, None, None] * pairs[:, None, None, :, :], axis=0)
    return (request_table, member_ids * capacity + position)


def mode_lookup(mode_ids, table):
    mode_hot = (mode_ids[..., None] == jnp.arange(table.shape[0], dtype=jnp.int32)).astype(
        jnp.float32
    )
    return jnp.sum(mode_hot * table, axis=-1)


def shards(
    density,
    hamiltonian,
    coupling,
    decay_rate,
    corr_real,
    corr_imag,
    up_member,
    up_slot,
    up_mode,
    down_member,
    down_slot,
    down_mode,
):
    member_count = lax.axis_size("member")
    matrices = density.shape[0]
    order_size = hamiltonian.shape[0]
    link_count = up_slot.shape[1]
    capacity = max(2, (matrices + member_count - 1) // member_count)
    served = member_count * capacity
    tier_float = lax.axis_index("tier").astype(jnp.float32)
    up_table, up_where = build_requests(up_member[:, 0], up_slot, up_mode, member_count, capacity)
    down_table, down_where = build_requests(
        down_member[:, 0], down_slot, down_mode, member_count, capacity
    )
    up_lifted = passed_along(up_table, "tier", 1)
    down_lifted = passed_along(down_table, "tier", -1)
    up_serve, down_serve = (
        lax.all_to_all(up_lifted, "member", split_axis=0, concat_axis=0, tiled=True),
        lax.all_to_all(down_lifted, "member", split_axis=0, concat_axis=0, tiled=True),
    )
    up_slots = up_serve[:, :, 0, :].reshape(-1)
    down_slots = down_serve[:, :, 0, :].reshape(-1)
    up_modes = up_serve[:, :, 1, :].reshape(served, link_count)
    down_modes = down_serve[:, :, 1, :].reshape(served, link_count)
    up_ops = jnp.take(coupling, up_modes.reshape(-1), axis=0).reshape(
        served, link_count, order_size, order_size
    )
    down_ops = jnp.take(coupling, down_modes.reshape(-1), axis=0).reshape(
        served, link_count, order_size, order_size
    )
    coef_real = mode_lookup(down_modes, corr_real)
    coef_imag = mode_lookup(down_modes, corr_imag)
    damping = (tier_float / LINKS * jnp.sum(mode_lookup(down_mode, decay_rate), axis=1))[
        :, None, None, None
    ]
    up_weight = jnp.sqrt(tier_float + 1.0)
    down_weight = jnp.sqrt(tier_float)

    def derivative(current):
        up_vals = jnp.take(current, up_slots, axis=0).reshape(
            served, link_count, 2, order_size, order_size
        )
        down_vals = jnp.take(current, down_slots, axis=0).reshape(
            served, link_count, 2, order_size, order_size
        )
        up_send = lift_terms(up_ops, up_vals).reshape(
            member_count, capacity, 2, order_size * order_size
        )
        down_send = lower_terms(down_ops, down_vals, coef_real, coef_imag).reshape(
            member_count, capacity, 2, order_size * order_size
        )
        up_mid, down_mid = (
            lax.all_to_all(up_send, "member", split_axis=0, concat_axis=0, tiled=True),
            lax.all_to_all(down_send, "member", split_axis=0, concat_axis=0, tiled=True),
        )
        up_back = passed_along(up_mid, "tier", -1)
        down_back = passed_along(down_mid, "tier", 1)
        lifted = jnp.take(up_back.reshape(served, 2, order_size, order_size), up_where, axis=0)
        lowered = jnp.take(down_back.reshape(served, 2, order_size, order_size), down_where, axis=0)
        return (
            own_terms(hamiltonian, current)
            + up_weight * lifted
            + down_weight * lowered
            - damping * current
        )

    states = density.reshape(matrices, 2, order_size, order_size)
    evolved = runge_kutta(states, derivative)
    return evolved.reshape(matrices, 2, order_size * order_size)


def solution(mesh):
    return jax.shard_map(
        shards,
        mesh=mesh,
        in_specs=(
            P(("tier", "member"), None, None),
            P(),
            P(),
            P(),
            P(),
            P(),
            P(("tier", "member"), None),
            P(("tier", "member"), None),
            P(("tier", "member"), None),
            P(("tier", "member"), None),
            P(("tier", "member"), None),
            P(("tier", "member"), None),
        ),
        out_specs=P(("tier", "member"), None, None),
        check_vma=False,
    )
```

profile of v0, /device:TPU:1, one launch (start us, length us, event | category | flops | bytes accessed | tf_op | source)
XLA Modules:
  0.0 751.8 jit_solution(15328783928678390818)
XLA Ops:
  13.7 6.8 all-to-all-start.2
  56.6 7.0 subtract_negate_fusion.3
  67.5 7.0 fusion.33
  82.3 7.1 all-to-all-start.3
  134.0 26.4 %all-to-all-done.1 = f32[16,2,2,9216]{3,1,2,0:T(2,128)} async-done(((f32[16,2,2,9216]{3,1,2,0:T(2,128)}), f32[16,2,2,9216]{3,1,2,0:T(2,128)}, u32[]{:S(2)}, u32[]{:S(2)}) %all-to-all-start.1) | async-done | bytes 2359328 | tf_op jit(solution)/shard_map/all_to_all | solution.py:150
  235.1 7.1 subtract_negate_fusion.2
  246.2 7.0 fusion.38
  295.9 6.6 all-to-all-start.4
  302.5 8.4 %collective-permute-start.5 = (f32[16,2,2,9216]{3,1,2,0:T(2,128)}, f32[16,2,2,9216]{3,1,2,0:T(2,128)}, u32[]{:S(2)}, u32[]{:S(2)}) collective-permute-start(f32[16,2,2,9216]{3,1,2,0:T(2,128)} %all-to-all-done.5), channel_id=1, source_target_pairs={{0,16},{16,32},{32,48},{48,64},{64,80},{80,96},{96,112},{1,17},{17... | collective-permute-start | bytes 7077896 | tf_op jit(solution)/shard_map/ppermute | solution.py:15
  310.9 20.8 %all-to-all-done.4 = f32[16,2,2,9216]{3,1,2,0:T(2,128)} async-done(((f32[16,2,2,9216]{3,1,2,0:T(2,128)}), f32[16,2,2,9216]{3,1,2,0:T(2,128)}, u32[]{:S(2)}, u32[]{:S(2)}) %all-to-all-start.4) | async-done | bytes 2359328 | tf_op jit(solution)/shard_map/all_to_all | solution.py:150
  354.2 21.2 %collective-permute-done.4 = f32[16,2,2,9216]{3,1,2,0:T(2,128)} collective-permute-done((f32[16,2,2,9216]{3,1,2,0:T(2,128)}, f32[16,2,2,9216]{3,1,2,0:T(2,128)}, u32[]{:S(2)}, u32[]{:S(2)}) %collective-permute-start.4) | collective-permute-done | bytes 2359328 | tf_op jit(solution)/shard_map/ppermute | solution.py:15
  417.0 7.1 subtract_negate_fusion.1
  427.9 7.0 fusion.43
  477.9 6.6 all-to-all-start.6
  484.5 7.9 %collective-permute-start.7 = (f32[16,2,2,9216]{3,1,2,0:T(2,128)}, f32[16,2,2,9216]{3,1,2,0:T(2,128)}, u32[]{:S(2)}, u32[]{:S(2)}) collective-permute-start(f32[16,2,2,9216]{3,1,2,0:T(2,128)} %all-to-all-done.7), channel_id=1, source_target_pairs={{0,16},{16,32},{32,48},{48,64},{64,80},{80,96},{96,112},{1,17},{17... | collective-permute-start | bytes 7077896 | tf_op jit(solution)/shard_map/ppermute | solution.py:15
  492.4 13.7 %all-to-all-done.6 = f32[16,2,2,9216]{3,1,2,0:T(2,128)} async-done(((f32[16,2,2,9216]{3,1,2,0:T(2,128)}), f32[16,2,2,9216]{3,1,2,0:T(2,128)}, u32[]{:S(2)}, u32[]{:S(2)}) %all-to-all-start.6) | async-done | bytes 2359328 | tf_op jit(solution)/shard_map/all_to_all | solution.py:150
  533.2 23.7 %collective-permute-done.6 = f32[16,2,2,9216]{3,1,2,0:T(2,128)} collective-permute-done((f32[16,2,2,9216]{3,1,2,0:T(2,128)}, f32[16,2,2,9216]{3,1,2,0:T(2,128)}, u32[]{:S(2)}, u32[]{:S(2)}) %collective-permute-start.6) | collective-permute-done | bytes 2359328 | tf_op jit(solution)/shard_map/ppermute | solution.py:15
  592.7 7.1 subtract_negate_fusion
  603.8 7.0 fusion.48
  651.0 6.7 all-to-all-start.8
  657.8 10.3 %collective-permute-start.9 = (f32[16,2,2,9216]{3,1,2,0:T(2,128)}, f32[16,2,2,9216]{3,1,2,0:T(2,128)}, u32[]{:S(2)}, u32[]{:S(2)}) collective-permute-start(f32[16,2,2,9216]{3,1,2,0:T(2,128)} %all-to-all-done.9), channel_id=1, source_target_pairs={{0,16},{16,32},{32,48},{48,64},{64,80},{80,96},{96,112},{1,17},{17... | collective-permute-start | bytes 7077896 | tf_op jit(solution)/shard_map/ppermute | solution.py:15
  668.1 11.3 %all-to-all-done.8 = f32[16,2,2,9216]{3,1,2,0:T(2,128)} async-done(((f32[16,2,2,9216]{3,1,2,0:T(2,128)}), f32[16,2,2,9216]{3,1,2,0:T(2,128)}, u32[]{:S(2)}, u32[]{:S(2)}) %all-to-all-start.8) | async-done | bytes 2359328 | tf_op jit(solution)/shard_map/all_to_all | solution.py:150
  684.8 9.3 %collective-permute-done.9 = f32[16,2,2,9216]{3,1,2,0:T(2,128)} collective-permute-done((f32[16,2,2,9216]{3,1,2,0:T(2,128)}, f32[16,2,2,9216]{3,1,2,0:T(2,128)}, u32[]{:S(2)}, u32[]{:S(2)}) %collective-permute-start.9) | collective-permute-done | bytes 2359328 | tf_op jit(solution)/shard_map/ppermute | solution.py:15
  704.3 28.2 %collective-permute-done.8 = f32[16,2,2,9216]{3,1,2,0:T(2,128)} collective-permute-done((f32[16,2,2,9216]{3,1,2,0:T(2,128)}, f32[16,2,2,9216]{3,1,2,0:T(2,128)}, u32[]{:S(2)}, u32[]{:S(2)}) %collective-permute-start.8) | collective-permute-done | bytes 2359328 | tf_op jit(solution)/shard_map/ppermute | solution.py:15
  (255 shorter events, 479.0 us)
Async XLA Ops:
  0.0 168.2 %copy-start = (f32[96,96]{1,0:T(8,128)S(1)}, f32[96,96]{1,0:T(8,128)}, u32[]{:S(2)}) copy-start(f32[96,96]{1,0:T(8,128)} %param.19) | copy-start | bytes 110596
  2.5 10.6 %collective-permute-start.2 = (s32[16,2,2,1]{0,2,3,1:T(2,128)S(1)}, s32[16,2,2,1]{0,2,3,1:T(2,128)S(1)}, u32[]{:S(2)}, u32[]{:S(2)}) collective-permute-start(s32[16,2,2,1]{0,2,3,1:T(2,128)S(1)} %bitcast.364), channel_id=1, source_target_pairs={{16,0},{32,16},{48,32},{64,48},{80,64},{96,80},{112,96},{17,1},{33... | collective-permute-start | bytes 776 | tf_op jit(solution)/shard_map/ppermute | solution.py:15
  8.2 12.6 %collective-permute-start = (s32[16,2,2,1]{0,2,3,1:T(2,128)S(1)}, s32[16,2,2,1]{0,2,3,1:T(2,128)S(1)}, u32[]{:S(2)}, u32[]{:S(2)}) collective-permute-start(s32[16,2,2,1]{0,2,3,1:T(2,128)S(1)} %bitcast.365), channel_id=1, source_target_pairs={{0,16},{16,32},{32,48},{48,64},{64,80},{80,96},{96,112},{1,17},{17... | collective-permute-start | bytes 776 | tf_op jit(solution)/shard_map/ppermute | solution.py:15
  13.7 13.2 %all-to-all-start.2 = ((s32[16,2,2,1]{2,3,1,0:T(1,128)}), s32[16,2,2,1]{2,3,1,0:T(1,128)S(1)}, u32[]{:S(2)}, u32[]{:S(2)}) async-start(s32[16,2,2,1]{2,3,1,0:T(1,128)} %copy.345), calls=%async_computation.2 | async-start | bytes 32768 | tf_op jit(solution)/shard_map/all_to_all | solution.py:116
  26.9 28.2 %all-to-all-start = ((s32[16,2,2,1]{2,3,1,0:T(1,128)}), s32[16,2,2,1]{2,3,1,0:T(1,128)S(1)}, u32[]{:S(2)}, u32[]{:S(2)}) async-start(s32[16,2,2,1]{2,3,1,0:T(1,128)} %copy.338), calls=%async_computation | async-start | bytes 32768 | tf_op jit(solution)/shard_map/all_to_all | solution.py:115
  82.3 41.8 %all-to-all-start.3 = ((f32[16,2,2,9216]{3,1,2,0:T(2,128)}), f32[16,2,2,9216]{3,1,2,0:T(2,128)}, u32[]{:S(2)}, u32[]{:S(2)}) async-start(f32[16,2,2,9216]{3,1,2,0:T(2,128)} %pad_maximum_fusion.1), calls=%async_computation.3 | async-start | bytes 4718592 | tf_op jit(solution)/shard_map/all_to_all | solution.py:151
  124.1 36.3 %all-to-all-start.1 = ((f32[16,2,2,9216]{3,1,2,0:T(2,128)}), f32[16,2,2,9216]{3,1,2,0:T(2,128)}, u32[]{:S(2)}, u32[]{:S(2)}) async-start(f32[16,2,2,9216]{3,1,2,0:T(2,128)} %pad_maximum_fusion), calls=%async_computation.1 | async-start | bytes 4718592 | tf_op jit(solution)/shard_map/all_to_all | solution.py:150
  128.6 39.3 %copy-start.25 = (s32[8,1]{0,1:T(1,128)S(1)}, s32[8,1]{0,1:T(1,128)}, u32[]{:S(2)}) copy-start(s32[8,1]{0,1:T(1,128)} %param.27) | copy-start | bytes 100
  128.6 39.3 %copy-start.29 = (s32[8,1]{0,1:T(1,128)S(1)}, s32[8,1]{0,1:T(1,128)}, u32[]{:S(2)}) copy-start(s32[8,1]{0,1:T(1,128)} %param.29) | copy-start | bytes 100
  128.6 39.3 %copy-start.30 = (f32[96]{0:T(128)S(1)}, f32[96]{0:T(128)}, u32[]{:S(2)}) copy-start(f32[96]{0:T(128)} %param.21) | copy-start | bytes 1156
  128.6 45.8 %collective-permute-start.3 = (f32[16,2,2,9216]{3,1,2,0:T(2,128)}, f32[16,2,2,9216]{3,1,2,0:T(2,128)}, u32[]{:S(2)}, u32[]{:S(2)}) collective-permute-start(f32[16,2,2,9216]{3,1,2,0:T(2,128)} %all-to-all-done.3), channel_id=1, source_target_pairs={{0,16},{16,32},{32,48},{48,64},{64,80},{80,96},{96,112},{1,17},{17... | collective-permute-start | bytes 7077896 | tf_op jit(solution)/shard_map/ppermute | solution.py:15
  160.4 33.4 %collective-permute-start.1 = (f32[16,2,2,9216]{3,1,2,0:T(2,128)}, f32[16,2,2,9216]{3,1,2,0:T(2,128)}, u32[]{:S(2)}, u32[]{:S(2)}) collective-permute-start(f32[16,2,2,9216]{3,1,2,0:T(2,128)} %all-to-all-done.1), channel_id=1, source_target_pairs={{16,0},{32,16},{48,32},{64,48},{80,64},{96,80},{112,96},{17,1},{33... | collective-permute-start | bytes 7077896 | tf_op jit(solution)/shard_map/ppermute | solution.py:15
  261.0 34.9 %all-to-all-start.5 = ((f32[16,2,2,9216]{3,1,2,0:T(2,128)}), f32[16,2,2,9216]{3,1,2,0:T(2,128)}, u32[]{:S(2)}, u32[]{:S(2)}) async-start(f32[16,2,2,9216]{3,1,2,0:T(2,128)} %pad_maximum_fusion.3), calls=%async_computation.5 | async-start | bytes 4718592 | tf_op jit(solution)/shard_map/all_to_all | solution.py:151
  295.9 35.7 %all-to-all-start.4 = ((f32[16,2,2,9216]{3,1,2,0:T(2,128)}), f32[16,2,2,9216]{3,1,2,0:T(2,128)}, u32[]{:S(2)}, u32[]{:S(2)}) async-start(f32[16,2,2,9216]{3,1,2,0:T(2,128)} %pad_maximum_fusion.2), calls=%async_computation.4 | async-start | bytes 4718592 | tf_op jit(solution)/shard_map/all_to_all | solution.py:150
  302.5 36.7 %collective-permute-start.5 = (f32[16,2,2,9216]{3,1,2,0:T(2,128)}, f32[16,2,2,9216]{3,1,2,0:T(2,128)}, u32[]{:S(2)}, u32[]{:S(2)}) collective-permute-start(f32[16,2,2,9216]{3,1,2,0:T(2,128)} %all-to-all-done.5), channel_id=1, source_target_pairs={{0,16},{16,32},{32,48},{48,64},{64,80},{80,96},{96,112},{1,17},{17... | collective-permute-start | bytes 7077896 | tf_op jit(solution)/shard_map/ppermute | solution.py:15
  331.7 43.7 %collective-permute-start.4 = (f32[16,2,2,9216]{3,1,2,0:T(2,128)}, f32[16,2,2,9216]{3,1,2,0:T(2,128)}, u32[]{:S(2)}, u32[]{:S(2)}) collective-permute-start(f32[16,2,2,9216]{3,1,2,0:T(2,128)} %all-to-all-done.4), channel_id=1, source_target_pairs={{16,0},{32,16},{48,32},{64,48},{80,64},{96,80},{112,96},{17,1},{33... | collective-permute-start | bytes 7077896 | tf_op jit(solution)/shard_map/ppermute | solution.py:15
  442.8 35.1 %all-to-all-start.7 = ((f32[16,2,2,9216]{3,1,2,0:T(2,128)}), f32[16,2,2,9216]{3,1,2,0:T(2,128)}, u32[]{:S(2)}, u32[]{:S(2)}) async-start(f32[16,2,2,9216]{3,1,2,0:T(2,128)} %pad_maximum_fusion.5), calls=%async_computation.7 | async-start | bytes 4718592 | tf_op jit(solution)/shard_map/all_to_all | solution.py:151
  477.9 28.2 %all-to-all-start.6 = ((f32[16,2,2,9216]{3,1,2,0:T(2,128)}), f32[16,2,2,9216]{3,1,2,0:T(2,128)}, u32[]{:S(2)}, u32[]{:S(2)}) async-start(f32[16,2,2,9216]{3,1,2,0:T(2,128)} %pad_maximum_fusion.4), calls=%async_computation.6 | async-start | bytes 4718592 | tf_op jit(solution)/shard_map/all_to_all | solution.py:150
  484.5 34.0 %collective-permute-start.7 = (f32[16,2,2,9216]{3,1,2,0:T(2,128)}, f32[16,2,2,9216]{3,1,2,0:T(2,128)}, u32[]{:S(2)}, u32[]{:S(2)}) collective-permute-start(f32[16,2,2,9216]{3,1,2,0:T(2,128)} %all-to-all-done.7), channel_id=1, source_target_pairs={{0,16},{16,32},{32,48},{48,64},{64,80},{80,96},{96,112},{1,17},{17... | collective-permute-start | bytes 7077896 | tf_op jit(solution)/shard_map/ppermute | solution.py:15
  506.2 50.8 %collective-permute-start.6 = (f32[16,2,2,9216]{3,1,2,0:T(2,128)}, f32[16,2,2,9216]{3,1,2,0:T(2,128)}, u32[]{:S(2)}, u32[]{:S(2)}) collective-permute-start(f32[16,2,2,9216]{3,1,2,0:T(2,128)} %all-to-all-done.6), channel_id=1, source_target_pairs={{16,0},{32,16},{48,32},{64,48},{80,64},{96,80},{112,96},{17,1},{33... | collective-permute-start | bytes 7077896 | tf_op jit(solution)/shard_map/ppermute | solution.py:15
  618.5 32.6 %all-to-all-start.9 = ((f32[16,2,2,9216]{3,1,2,0:T(2,128)}), f32[16,2,2,9216]{3,1,2,0:T(2,128)}, u32[]{:S(2)}, u32[]{:S(2)}) async-start(f32[16,2,2,9216]{3,1,2,0:T(2,128)} %pad_maximum_fusion.7), calls=%async_computation.9 | async-start | bytes 4718592 | tf_op jit(solution)/shard_map/all_to_all | solution.py:151
  651.0 28.4 %all-to-all-start.8 = ((f32[16,2,2,9216]{3,1,2,0:T(2,128)}), f32[16,2,2,9216]{3,1,2,0:T(2,128)}, u32[]{:S(2)}, u32[]{:S(2)}) async-start(f32[16,2,2,9216]{3,1,2,0:T(2,128)} %pad_maximum_fusion.6), calls=%async_computation.8 | async-start | bytes 4718592 | tf_op jit(solution)/shard_map/all_to_all | solution.py:150
  657.8 36.4 %collective-permute-start.9 = (f32[16,2,2,9216]{3,1,2,0:T(2,128)}, f32[16,2,2,9216]{3,1,2,0:T(2,128)}, u32[]{:S(2)}, u32[]{:S(2)}) collective-permute-start(f32[16,2,2,9216]{3,1,2,0:T(2,128)} %all-to-all-done.9), channel_id=1, source_target_pairs={{0,16},{16,32},{32,48},{48,64},{64,80},{80,96},{96,112},{1,17},{17... | collective-permute-start | bytes 7077896 | tf_op jit(solution)/shard_map/ppermute | solution.py:15
  679.4 53.1 %collective-permute-start.8 = (f32[16,2,2,9216]{3,1,2,0:T(2,128)}, f32[16,2,2,9216]{3,1,2,0:T(2,128)}, u32[]{:S(2)}, u32[]{:S(2)}) collective-permute-start(f32[16,2,2,9216]{3,1,2,0:T(2,128)} %all-to-all-done.8), channel_id=1, source_target_pairs={{16,0},{32,16},{48,32},{64,48},{80,64},{96,80},{112,96},{17,1},{33... | collective-permute-start | bytes 7077896 | tf_op jit(solution)/shard_map/ppermute | solution.py:15
  (27 other events, 190.5 us)
where the time goes:
time: 765 us; the launch traced here: 752 us
  local copies, waits for them, and re-layouts  228 us (30%)
  waiting for transfers between devices  174 us (23%)
  matrix products  172 us (22%)
  starting transfers between devices  105 us (14%)
  other arithmetic  72.1 us (9%)
    dot_general x32, matrix products, linksum(): jnp.einsum('slik,slkj->sij', left, right, precision=lax.Precision.HIGHEST)  152 us
    ppermute x10, waiting for transfers between devices, passed_along(): lax.ppermute(value, axis, [(source, source + steps) for source in range(f...  92 us
    all_to_all x4, waiting for transfers between devices, derivative(): lax.all_to_all(up_send, 'member', split_axis=0, concat_axis=0, tiled=True)  72.2 us
    ppermute x10, starting transfers between devices, passed_along(): lax.ppermute(value, axis, [(source, source + steps) for source in range(f...  49.9 us
    ppermute x10, local copies, waits for them, and re-layouts, passed_along(): lax.ppermute(value, axis, [(source, source + steps) for source in range(f...  33 us
    another operation x8, local copies, waits for them, and re-layouts, lower_terms(): return jnp.stack([cross_imag, -cross_real], axis=1)  30.1 us
    another operation x8, local copies, waits for them, and re-layouts, lift_terms(): return jnp.stack([first, second], axis=1)  28.9 us
    all_to_all x4, starting transfers between devices, derivative(): lax.all_to_all(up_send, 'member', split_axis=0, concat_axis=0, tiled=True)  24.3 us
  transfers between devices with their start and end apart: 20, of which 12 were waited for; matrix products, arithmetic and copies ran while one was open for 30% of the time, Pallas kernels for 0%

commit v1 on v0

v1 whole, which is shorter than its diff:
```python
import functools

import jax
import jax.numpy as jnp
from jax import lax
from jax.experimental import pallas as pl
from jax.experimental.pallas import tpu as pltpu
from jax.sharding import PartitionSpec as P

STEP = 0.08
N = 96
M = 8
ROWS = 144
HALF = 72
TIERS = 8
SIDE = 4
F32 = jnp.float32
BF16 = jnp.bfloat16
CHUNK = 128
SEND_A, SEND_B, OWN_A, OWN_B, UP_MODE, DOWN_MODE, COUNT = 0, 32, 64, 80, 96, 120, 144


def ring(axis_shift, value):
    rows = value.shape[0] // 2
    back = lax.ppermute(value, "member", axis_shift(1))
    front = lax.ppermute(value, "member", axis_shift(-1))
    first = lax.ppermute(back[:rows], "member", axis_shift(1))
    second = lax.ppermute(front[rows:], "member", axis_shift(-1))
    return jnp.concatenate([value, back, front, first, second], axis=0)


def along_x(step):
    return [(y * SIDE + x, y * SIDE + (x + step) % SIDE) for y in range(SIDE) for x in range(SIDE)]


def along_y(step):
    return [(y * SIDE + x, (y + step) % SIDE * SIDE + x) for y in range(SIDE) for x in range(SIDE)]


def gathered(state):
    first = ring(along_y, ring(along_x, state[:, :HALF]))
    second = ring(along_x, ring(along_y, state[:, HALF:]))
    return first, second


def passed_along(value, steps):
    low, high = max(0, -steps), min(TIERS, TIERS - steps)
    return lax.ppermute(value, "tier", [(source, source + steps) for source in range(low, high)])


def index_kernel(table, place, corr_real, corr_imag, decay, index, scale):
    tier, member_y, member_x = place[0], place[1], place[2]
    member = member_y * SIDE + member_x

    def entry(block, field, slot):
        return table[block * (6 * M) + field * M + slot]

    def block_of(level, who):
        return jnp.clip(level, 0, TIERS - 1) * (SIDE * SIDE) + who

    def spot(distance):
        return jnp.where(distance == 0, 0, jnp.where(distance == 3, 1, jnp.where(distance == 1, 2, 3)))

    def places(who, slot):
        at_y = spot(jnp.bitwise_and(who // SIDE - member_y + SIDE, SIDE - 1))
        at_x = spot(jnp.bitwise_and(jnp.bitwise_and(who, SIDE - 1) - member_x + SIDE, SIDE - 1))
        return (at_y * SIDE + at_x) * M + slot, (at_x * SIDE + at_y) * M + slot

    def put(base_a, base_b, at, pair):
        index[base_a + at] = pair[0]
        index[base_b + at] = pair[1]

    def node(level, block, slot, at, rate):
        mode = entry(block, 5, slot)
        index[UP_MODE + at] = entry(block, 2, slot)
        index[DOWN_MODE + at] = mode
        scale[at] = corr_real[mode]
        scale[3 * M + at] = corr_imag[mode]
        scale[6 * M + at] = rate * decay[mode]

    own, above, below = block_of(tier, member), block_of(tier + 1, member), block_of(tier - 1, member)
    above2, below2 = block_of(tier + 2, member), block_of(tier - 2, member)
    level = tier.astype(F32)

    def one(m, carry):
        up = block_of(tier + 1, entry(own, 0, m))
        up_slot = entry(own, 1, m)
        down = block_of(tier - 1, entry(own, 3, m))
        down_slot = entry(own, 4, m)
        node(tier, own, m, m, STEP * level)
        node(tier + 1, up, up_slot, M + m, STEP * (level + 1.0))
        node(tier - 1, down, down_slot, 2 * M + m, STEP * jnp.maximum(level - 1.0, 0.0))
        put(OWN_A, OWN_B, m, places(entry(up, 3, up_slot), entry(up, 4, up_slot)))
        put(OWN_A, OWN_B, M + m, places(entry(down, 0, down_slot), entry(down, 1, down_slot)))
        put(SEND_A, SEND_B, m, places(entry(below, 0, m), entry(below, 1, m)))
        put(SEND_A, SEND_B, M + m, places(entry(above, 3, m), entry(above, 4, m)))
        middle = block_of(tier - 1, entry(below2, 0, m))
        slot = entry(below2, 1, m)
        put(SEND_A, SEND_B, 2 * M + m, places(entry(middle, 0, slot), entry(middle, 1, slot)))
        middle = block_of(tier + 1, entry(above2, 3, m))
        slot = entry(above2, 4, m)
        put(SEND_A, SEND_B, 3 * M + m, places(entry(middle, 3, slot), entry(middle, 4, slot)))
        return carry

    lax.fori_loop(0, M, one, 0)


def make_index(table, place, corr_real, corr_imag, decay):
    smem = pl.BlockSpec(memory_space=pltpu.SMEM)
    return pl.pallas_call(
        index_kernel,
        in_specs=[smem] * 5,
        out_specs=[smem, smem],
        out_shape=[jax.ShapeDtypeStruct((COUNT,), jnp.int32), jax.ShapeDtypeStruct((9 * M,), F32)],
        name="links",
    )(table, place, corr_real, corr_imag, decay)


def split(value):
    high = value.astype(BF16)
    return high, (value - high.astype(F32)).astype(BF16)


def operator_kernel(index, weight, hamiltonian, up_op, down_op, left, right):
    kind = pl.program_id(0) // M
    left[...] = jnp.zeros_like(left)
    right[...] = jnp.zeros_like(right)
    parts = (STEP * hamiltonian[...], weight[kind] * up_op[0], weight[3 + kind] * down_op[0])
    for place, part in enumerate(parts):
        high, low = split(part)
        for turn, piece in enumerate((high, low, high)):
            left[0, :, (3 * place + turn) * CHUNK : (3 * place + turn) * CHUNK + N] = piece
        for turn, piece in enumerate((high, high, low)):
            right[0, (3 * place + turn) * CHUNK : (3 * place + turn) * CHUNK + N, 0:N] = piece


def make_operators(index, weight, hamiltonian, coupling):
    return pl.pallas_call(
        operator_kernel,
        grid_spec=pltpu.PrefetchScalarGridSpec(
            num_scalar_prefetch=2,
            grid=(3 * M,),
            in_specs=[
                pl.BlockSpec((N, N), lambda n, index, weight: (0, 0)),
                pl.BlockSpec((1, N, N), lambda n, index, weight: (index[UP_MODE + n], 0, 0)),
                pl.BlockSpec((1, N, N), lambda n, index, weight: (index[DOWN_MODE + n], 0, 0)),
            ],
            out_specs=[
                pl.BlockSpec((1, N, 9 * CHUNK), lambda n, index, weight: (n, 0, 0)),
                pl.BlockSpec((1, 9 * CHUNK, CHUNK), lambda n, index, weight: (n, 0, 0)),
            ],
        ),
        out_shape=[
            jax.ShapeDtypeStruct((3 * M, N, 9 * CHUNK), BF16),
            jax.ShapeDtypeStruct((3 * M, 9 * CHUNK, CHUNK), BF16),
        ],
        name="operators",
    )(index, weight, hamiltonian, coupling, coupling)


def pick_kernel(index, first, second, *refs):
    outs, done = refs[:4], refs[4]
    copies = []
    for kind, out in enumerate(outs):
        for m in range(M):
            at = kind * M + m
            copies.append(pltpu.make_async_copy(first.at[index[SEND_A + at]], out.at[m, pl.ds(0, HALF)], done.at[2 * at]))
            copies.append(pltpu.make_async_copy(second.at[index[SEND_B + at]], out.at[m, pl.ds(HALF, HALF)], done.at[2 * at + 1]))
    for copy in copies:
        copy.start()
    for copy in copies:
        copy.wait()


def picked(index, first, second):
    anywhere = pl.BlockSpec(memory_space=pl.ANY)
    return pl.pallas_call(
        pick_kernel,
        in_specs=[pl.BlockSpec(memory_space=pltpu.SMEM), anywhere, anywhere],
        out_specs=[anywhere] * 4,
        out_shape=[jax.ShapeDtypeStruct((M, ROWS, 128), F32)] * 4,
        scratch_shapes=[pltpu.SemaphoreType.DMA((8 * M,))],
        name="pick",
    )(index, first, second)


def unpack(source, target):
    lane = lax.broadcasted_iota(jnp.int32, (24, 128), 1)
    for part in range(2):
        a, b, c = (source[pl.ds(2 * k + part, 24, stride=6), :] for k in range(3))
        target[pl.ds(part * N, 24, stride=4), :] = a
        target[pl.ds(part * N + 1, 24, stride=4), :] = jnp.where(lane < 32, pltpu.roll(a, 32, 1), pltpu.roll(b, 32, 1))
        target[pl.ds(part * N + 2, 24, stride=4), :] = jnp.where(lane < 64, pltpu.roll(b, 64, 1), pltpu.roll(c, 64, 1))
        target[pl.ds(part * N + 3, 24, stride=4), :] = pltpu.roll(c, 96, 1)


def pack(source, target):
    lane = lax.broadcasted_iota(jnp.int32, (24, 128), 1)
    for part in range(2):
        a, b, c, d = (source[pl.ds(part * N + k, 24, stride=4), :] for k in range(4))
        b, c, d = pltpu.roll(b, 96, 1), pltpu.roll(c, 64, 1), pltpu.roll(d, 32, 1)
        target[pl.ds(part, 24, stride=6), :] = jnp.where(lane < 96, a, b)
        target[pl.ds(part + 2, 24, stride=6), :] = jnp.where(lane < 64, b, c)
        target[pl.ds(part + 4, 24, stride=6), :] = jnp.where(lane < 32, c, d)


def applied(own, up, down, left, right, cr, ci, damp):
    def halves(value):
        return value[:N], value[N:]

    xr, xi = halves(own)
    ur, ui = halves(up)
    dr, di = halves(down)
    rr, ri, ir, ii = cr * dr, cr * di, ci * dr, ci * di
    lefts, rights = [], []
    for (ar, ai), (br, bi) in (((xr, xi), (xr, xi)), ((ur, ui), (ur, ui)), ((rr - ii, ir + ri), (rr + ii, ri - ir))):
        high, low = split(jnp.concatenate([ar, ai], axis=1))
        lefts += [high, high, low]
        high, low = split(jnp.concatenate([br, bi], axis=0))
        rights += [high, low, high]
    pad = jnp.zeros((CHUNK - N, 2 * CHUNK), BF16)
    tall = jnp.concatenate([piece for value in lefts for piece in (value, pad)], axis=0)
    wide = jnp.concatenate(rights, axis=1)
    from_left = jnp.dot(left, tall, preferred_element_type=F32)
    from_right = jnp.dot(wide, right, preferred_element_type=F32)
    real = from_left[:, CHUNK:] - from_right[N:] - damp * xr
    imag = from_right[:N] - from_left[:, :CHUNK] - damp * xi
    return jnp.concatenate([real, imag], axis=0)


def stage_kernel(last, index, scale, *refs):
    own, up, down, up2, down2, ud_a, ud_b, du_a, du_b, left, right = refs[:11]
    if last:
        before, result, raw, plain, level1, level2 = refs[11:]
    else:
        result, total, raw, plain, level1, level2 = refs[11:]
    m = pl.program_id(0)
    for place, source in enumerate((own, up, down, up2, down2)):
        unpack(source.at[0], plain.at[place])
    for place, (a, b) in enumerate(((ud_a, ud_b), (du_a, du_b))):
        raw[place, 0:HALF, :] = a[0]
        raw[place, HALF:ROWS, :] = b[0]
        unpack(raw.at[place], plain.at[5 + place])
    for kind, (x, u, d) in enumerate(((0, 1, 2), (1, 3, 5), (2, 6, 4))):
        at = kind * M + m
        level1[kind] = applied(
            plain[x], plain[u], plain[d], left[kind, 0], right[kind, 0], scale[at], scale[3 * M + at], scale[6 * M + at]
        )
    second = applied(
        level1[0], level1[1], level1[2], left[0, 0], right[0, 0], scale[m], scale[3 * M + m], scale[6 * M + m]
    )
    if last:
        level2[...] = before[0] + (1.0 / 6.0) * level1[0] + (1.0 / 24.0) * second
        pack(level2, result.at[0])
    else:
        level2[...] = second
        pack(level2, result.at[0])
        total[0] = plain[0] + level1[0] + 0.5 * second


def stage(index, scale, own, received, first, second, left, right, before):
    last = before is not None
    whole = pl.BlockSpec((1, ROWS, 128), lambda m, index, scale: (m, 0, 0))
    plain = pl.BlockSpec((1, 2 * N, 128), lambda m, index, scale: (m, 0, 0))

    def chosen(base):
        return pl.BlockSpec((1, HALF, 128), lambda m, index, scale: (index[base + m], 0, 0))

    result = jax.ShapeDtypeStruct((M, ROWS, 128), F32)
    sums = jax.ShapeDtypeStruct((M, 2 * N, 128), F32)
    return pl.pallas_call(
        functools.partial(stage_kernel, last),
        grid_spec=pltpu.PrefetchScalarGridSpec(
            num_scalar_prefetch=2,
            grid=(M,),
            in_specs=[whole] * 5
            + [chosen(OWN_A), chosen(OWN_B), chosen(OWN_A + M), chosen(OWN_B + M)]
            + [
                pl.BlockSpec((3, 1, N, 9 * CHUNK), lambda m, index, scale: (0, m, 0, 0)),
                pl.BlockSpec((3, 1, 9 * CHUNK, CHUNK), lambda m, index, scale: (0, m, 0, 0)),
            ]
            + ([plain] if last else []),
            out_specs=[whole] if last else [whole, plain],
            scratch_shapes=[
                pltpu.VMEM((2, ROWS, 128), F32),
                pltpu.VMEM((7, 2 * N, 128), F32),
                pltpu.VMEM((3, 2 * N, 128), F32),
                pltpu.VMEM((2 * N, 128), F32),
            ],
        ),
        out_shape=[result] if last else [result, sums],
        compiler_params=pltpu.CompilerParams(vmem_limit_bytes=48 * 1024 * 1024),
        name="stage",
    )(index, scale, own, *received, first, second, first, second, left, right, *([before] if last else []))


def shards(
    density,
    hamiltonian,
    coupling,
    decay_rate,
    corr_real,
    corr_imag,
    up_member,
    up_slot,
    up_mode,
    down_member,
    down_slot,
    down_mode,
):
    tier, member = lax.axis_index("tier"), lax.axis_index("member")
    fields = jnp.stack([f[:, 0] for f in (up_member, up_slot, up_mode, down_member, down_slot, down_mode)])
    table = lax.all_gather(fields.reshape(-1), ("tier", "member"), tiled=True)
    place = jnp.stack([tier, member // SIDE, member % SIDE]).astype(jnp.int32)
    levels = jnp.stack([tier, tier + 1, tier - 1]).astype(F32)
    ups = jnp.where(levels + 1.0 < TIERS, jnp.sqrt(levels + 1.0), 0.0)
    downs = jnp.sqrt(jnp.maximum(levels, 0.0))
    weight = STEP * jnp.concatenate([ups, downs])
    index, scale = make_index(table, place, corr_real, corr_imag, decay_rate)
    left, right = make_operators(index, weight, hamiltonian, coupling)
    left, right = left.reshape(3, M, N, 9 * CHUNK), right.reshape(3, M, 9 * CHUNK, CHUNK)

    def exchange(state):
        first, second = gathered(state)
        sent = picked(index, first, second)
        return [passed_along(value, steps) for value, steps in zip(sent, (-1, 1, -2, 2))], first, second

    state = density.reshape(M, 2, HALF, 128).transpose(0, 2, 1, 3).reshape(M, ROWS, 128)
    received, first, second = exchange(state)
    state2, total = stage(index, scale, state, received, first, second, left, right, None)
    received, first, second = exchange(state2)
    (result,) = stage(index, scale, state2, received, first, second, left, right, total)
    return result.reshape(M, HALF, 2, 128).transpose(0, 2, 1, 3).reshape(M, 2, N * N)


def solution(mesh):
    return jax.shard_map(
        shards,
        mesh=mesh,
        in_specs=(P(("tier", "member"), None, None),) + (P(),) * 5 + (P(("tier", "member"), None),) * 6,
        out_specs=P(("tier", "member"), None, None),
        check_vma=False,
    )
```

time: 765 us -> 443 us (0.58)
  the two profiles are of different devices: /device:TPU:1 before, /device:TPU:0 now
where the time goes in v1:
time: 443 us; the launch traced here: 438 us
  Pallas kernels  192 us (43%)
  starting transfers between devices  70.8 us (16%)
  waiting for transfers between devices  70.8 us (16%)
  blocking collectives  66.8 us (15%)
  local copies, waits for them, and re-layouts  35.7 us (8%)
    pallas_call x2, Pallas kernels, picked(): pl.pallas_call(pick_kernel, in_specs=[pl.BlockSpec(memory_space=pltpu.SME...  148 us
    unnamed x1, blocking collectives  66.8 us
    ppermute x8, waiting for transfers between devices, ring(): back = lax.ppermute(value, 'member', axis_shift(1))  46.2 us
    unnamed x52, local copies, waits for them, and re-layouts  27.9 us
    pallas_call x2, Pallas kernels, stage(): pl.pallas_call(functools.partial(stage_kernel, last), grid_spec=pltpu.Pre...  25.8 us
    ppermute x8, starting transfers between devices, ring(): front = lax.ppermute(value, 'member', axis_shift(-1))  21.4 us
    ppermute x8, starting transfers between devices, ring(): second = lax.ppermute(front[rows:], 'member', axis_shift(-1))  20.5 us
    ppermute x8, starting transfers between devices, passed_along(): lax.ppermute(value, 'tier', [(source, source + steps) for source in range...  20.5 us
  transfers between devices with their start and end apart: 40, of which 11 were waited for; matrix products, arithmetic and copies ran while one was open for 7% of the time, Pallas kernels for 4%

profile of v1, /device:TPU:0, one launch (start us, length us, event | category | flops | bytes accessed | tf_op | source)
XLA Modules:
  0.0 438.3 jit_solution(5034849371232073115)
XLA Ops:
  8.7 3.6 collective-permute-done.8
  12.7 3.0 collective-permute-start.11
  28.7 3.2 collective-permute-start.5
  32.0 19.3 %collective-permute-done.12 = f32[32,72,128]{2,1,0:T(8,128)S(1)} collective-permute-done((f32[32,72,128]{2,1,0:T(8,128)}, f32[32,72,128]{2,1,0:T(8,128)S(1)}, u32[]{:S(2)}, u32[]{:S(2)}) %collective-permute-start.12) | collective-permute-done | bytes 1179680 | tf_op jit(solution)/shard_map/ppermute | solution.py:25
  55.6 66.8 %all-reduce.table = s32[6144]{0:T(1024)} all-reduce(s32[6144]{0:T(1024)} %dynamic-update-slice), channel_id=1, replica_groups=mesh['tier'=8,'member'=16] {'tier','member'}, use_global_device_ids=true, to_apply=%add | all-reduce | flops 6144 | bytes 49152
  144.3 73.9 %pick.2 = (f32[8,144,128]{2,1,0:T(8,128)}, f32[8,144,128]{2,1,0:T(8,128)}, f32[8,144,128]{2,1,0:T(8,128)}, f32[8,144,128]{2,1,0:T(8,128)}) custom-call(s32[144]{0:T(256)} %get-tuple-element.19.index, f32[128,72,128]{2,1,0:T(8,128)} %constant_dynamic-update-slice_fusion.5.first.refs_5_.refs_7_, ...), custom_call_target="tpu_custom_call" | custom-call | tf_op jit(solution)/shard_map/pick/pallas_call | solution.py:177
  219.5 3.1 collective-permute-start.17
  223.9 4.6 %collective-permute-start.19 = (f32[8,144,128]{2,1,0:T(8,128)}, f32[8,144,128]{2,1,0:T(8,128)S(1)}, u32[]{:S(2)}, u32[]{:S(2)}) collective-permute-start(f32[8,144,128]{2,1,0:T(8,128)} %get-tuple-element.24), channel_id=1, source_target_pairs={{0,32},{16,48},{32,64},{48,80},{64,96},{80,112},{1,33},{17,49},{33... | collective-permute-start | bytes 1769480 | tf_op jit(solution)/shard_map/ppermute | solution.py:48
  229.2 16.0 %operators.1 = (bf16[24,96,1152]{2,1,0:T(8,128)(2,1)}, bf16[24,1152,128]{2,1,0:T(8,128)(2,1)}) custom-call(s32[144]{0:T(256)} %get-tuple-element.19.index, f32[6]{0:T(128)} %maximum_multiply_fusion.weight, f32[96,96]{1,0:T(8,128)} %hamiltonian.1, f32[96,96,96]{2,1,0:T(8,128)} %down_op.1, f32[96,96,96]{2,1,0:T(8,128)} %down_op.1), custom_call_target="tpu_custom_call" | custom-call | tf_op jit(solution)/shard_map/operators/pallas_call | solution.py:138
  249.0 12.5 %stage.2 = (f32[8,144,128]{2,1,0:T(8,128)S(1)}, f32[8,192,128]{2,1,0:T(8,128)S(1)}) custom-call(s32[144]{0:T(256)S(1)} %copy-done.5, f32[72]{0:T(128)S(1)} %copy-done.7, f32[8,144,128]{2,1,0:T(8,128)S(1)} %bitcast.24, f32[8,144,128]{2,1,0:T(8,128)S(1)} %collective-permute-done.16.refs_1_, f32[8,144,128]{2,1,0:T(8,128)S(1)} %collective-permute-done.17.refs_2_, ...), custom_call_target="tpu_custom_call" | custom-call | tf_op jit(solution)/shard_map/stage/pallas_call | solution.py:271
  268.9 3.5 collective-permute-done.28
  272.5 3.3 collective-permute-start.31
  281.0 3.2 collective-permute-start.33
  285.6 3.2 collective-permute-start.25
  288.8 19.2 %collective-permute-done.32 = f32[32,72,128]{2,1,0:T(8,128)S(1)} collective-permute-done((f32[32,72,128]{2,1,0:T(8,128)S(1)}, f32[32,72,128]{2,1,0:T(8,128)S(1)}, u32[]{:S(2)}, u32[]{:S(2)}) %collective-permute-start.32) | collective-permute-done | bytes 1179680 | tf_op jit(solution)/shard_map/ppermute | solution.py:25
  308.2 3.3 collective-permute-start.35
  312.2 3.3 collective-permute-start.27
  317.9 3.6 collective-permute-done.34
  321.6 3.4 collective-permute-done.26
  326.7 74.0 %pick.3 = (f32[8,144,128]{2,1,0:T(8,128)}, f32[8,144,128]{2,1,0:T(8,128)}, f32[8,144,128]{2,1,0:T(8,128)}, f32[8,144,128]{2,1,0:T(8,128)}) custom-call(s32[144]{0:T(256)} %get-tuple-element.19.index, f32[128,72,128]{2,1,0:T(8,128)} %constant_dynamic-update-slice_fusion.33.first.refs_5_.refs_7_, f32[128,72,128]{2,1,0:T(8,128)} %copy-done.8), custom_call_target="tpu_custom_call" | custom-call | tf_op jit(solution)/shard_map/pick/pallas_call | solution.py:177
  402.0 3.1 collective-permute-start.37
  406.4 4.6 %collective-permute-start.39 = (f32[8,144,128]{2,1,0:T(8,128)}, f32[8,144,128]{2,1,0:T(8,128)S(1)}, u32[]{:S(2)}, u32[]{:S(2)}) collective-permute-start(f32[8,144,128]{2,1,0:T(8,128)} %get-tuple-element.31), channel_id=1, source_target_pairs={{0,32},{16,48},{32,64},{48,80},{64,96},{80,112},{1,33},{17,49},{33... | collective-permute-start | bytes 1769480 | tf_op jit(solution)/shard_map/ppermute | solution.py:48
  411.0 14.0 %collective-permute-done.38.refs_3_ = f32[8,144,128]{2,1,0:T(8,128)S(1)} collective-permute-done((f32[8,144,128]{2,1,0:T(8,128)}, f32[8,144,128]{2,1,0:T(8,128)S(1)}, u32[]{:S(2)}, u32[]{:S(2)}) %collective-permute-start.38) | collective-permute-done | bytes 589856 | tf_op jit(solution)/shard_map/ppermute | solution.py:48
  425.0 13.2 %stage.3 = f32[8,144,128]{2,1,0:T(8,128)} custom-call(s32[144]{0:T(256)S(1)} %copy-done.6, f32[72]{0:T(128)S(1)} %copy-done.7, f32[8,144,128]{2,1,0:T(8,128)S(1)} %get-tuple-element.27.refs_0_, f32[8,144,128]{2,1,0:T(8,128)S(1)} %collective-permute-done.36.refs_1_, f32[8,144,128]{2,1,0:T(8,128)S(1)} %collective-permute-done.37.refs_2_, ...), custom_call_target="tpu_custom_call" | custom-call | tf_op jit(solution)/shard_map/stage/pallas_call | solution.py:271
  (145 shorter events, 76.9 us)
Async XLA Ops:
  15.7 11.5 %collective-permute-start.2 = (f32[4,72,128]{2,1,0:T(8,128)S(1)}, f32[4,72,128]{2,1,0:T(8,128)S(1)}, u32[]{:S(2)}, u32[]{:S(2)}) collective-permute-start(f32[4,72,128]{2,1,0:T(8,128)S(1)} %slice.81), channel_id=1, source_target_pairs={{0,1},{1,2},{2,3},{3,0},{4,5},{5,6},{6,7},{7,4},{8,9},{9,10},{10,1... | collective-permute-start | bytes 442376 | tf_op jit(solution)/shard_map/ppermute | solution.py:27
  17.3 10.7 %collective-permute-start.3 = (f32[4,72,128]{2,1,0:T(8,128)S(1)}, f32[4,72,128]{2,1,0:T(8,128)S(1)}, u32[]{:S(2)}, u32[]{:S(2)}) collective-permute-start(f32[4,72,128]{2,1,0:T(8,128)S(1)} %slice.82), channel_id=1, source_target_pairs={{0,3},{1,0},{2,1},{3,2},{4,7},{5,4},{6,5},{7,6},{8,11},{9,8},{10,9... | collective-permute-start | bytes 442376 | tf_op jit(solution)/shard_map/ppermute | solution.py:28
  24.0 27.3 %collective-permute-start.12 = (f32[32,72,128]{2,1,0:T(8,128)}, f32[32,72,128]{2,1,0:T(8,128)S(1)}, u32[]{:S(2)}, u32[]{:S(2)}) collective-permute-start(f32[32,72,128]{2,1,0:T(8,128)} %get-tuple-element.71), channel_id=1, source_target_pairs={{0,1},{1,2},{2,3},{3,0},{4,5},{5,6},{6,7},{7,4},{8,9},{9,10},{10,1... | collective-permute-start | bytes 3538952 | tf_op jit(solution)/shard_map/ppermute | solution.py:25
  24.3 100.9 %collective-permute-start.13 = (f32[32,72,128]{2,1,0:T(8,128)}, f32[32,72,128]{2,1,0:T(8,128)S(1)}, u32[]{:S(2)}, u32[]{:S(2)}) collective-permute-start(f32[32,72,128]{2,1,0:T(8,128)} %get-tuple-element.71), channel_id=1, source_target_pairs={{0,3},{1,0},{2,1},{3,2},{4,7},{5,4},{6,5},{7,6},{8,11},{9,8},{10,9... | collective-permute-start | bytes 3538952 | tf_op jit(solution)/shard_map/ppermute | solution.py:26
  28.7 97.3 %collective-permute-start.4 = (f32[32,72,128]{2,1,0:T(8,128)}, f32[32,72,128]{2,1,0:T(8,128)S(1)}, u32[]{:S(2)}, u32[]{:S(2)}) collective-permute-start(f32[32,72,128]{2,1,0:T(8,128)} %get-tuple-element.75), channel_id=1, source_target_pairs={{0,4},{1,5},{2,6},{3,7},{4,8},{5,9},{6,10},{7,11},{8,12},{9,13},{1... | collective-permute-start | bytes 3538952 | tf_op jit(solution)/shard_map/ppermute | solution.py:25
  28.7 98.5 %collective-permute-start.5 = (f32[32,72,128]{2,1,0:T(8,128)}, f32[32,72,128]{2,1,0:T(8,128)}, u32[]{:S(2)}, u32[]{:S(2)}) collective-permute-start(f32[32,72,128]{2,1,0:T(8,128)} %get-tuple-element.75), channel_id=1, source_target_pairs={{0,12},{1,13},{2,14},{3,15},{4,0},{5,1},{6,2},{7,3},{8,4},{9,5},{1... | collective-permute-start | bytes 3538952 | tf_op jit(solution)/shard_map/ppermute | solution.py:26
  52.1 84.1 %collective-permute-start.14 = (f32[16,72,128]{2,1,0:T(8,128)}, f32[16,72,128]{2,1,0:T(8,128)}, u32[]{:S(2)}, u32[]{:S(2)}) collective-permute-start(f32[16,72,128]{2,1,0:T(8,128)} %slice.88), channel_id=1, source_target_pairs={{0,1},{1,2},{2,3},{3,0},{4,5},{5,6},{6,7},{7,4},{8,9},{9,10},{10,1... | collective-permute-start | bytes 1769480 | tf_op jit(solution)/shard_map/ppermute | solution.py:27
  125.2 14.9 %collective-permute-start.15 = (f32[16,72,128]{2,1,0:T(8,128)S(1)}, f32[16,72,128]{2,1,0:T(8,128)S(1)}, u32[]{:S(2)}, u32[]{:S(2)}) collective-permute-start(f32[16,72,128]{2,1,0:T(8,128)S(1)} %slice.89), channel_id=1, source_target_pairs={{0,3},{1,0},{2,1},{3,2},{4,7},{5,4},{6,5},{7,6},{8,11},{9,8},{10,9... | collective-permute-start | bytes 1769480 | tf_op jit(solution)/shard_map/ppermute | solution.py:28
  126.0 16.1 %collective-permute-start.6 = (f32[16,72,128]{2,1,0:T(8,128)S(1)}, f32[16,72,128]{2,1,0:T(8,128)S(1)}, u32[]{:S(2)}, u32[]{:S(2)}) collective-permute-start(f32[16,72,128]{2,1,0:T(8,128)S(1)} %slice.83), channel_id=1, source_target_pairs={{0,4},{1,5},{2,6},{3,7},{4,8},{5,9},{6,10},{7,11},{8,12},{9,13},{1... | collective-permute-start | bytes 1769480 | tf_op jit(solution)/shard_map/ppermute | solution.py:27
  128.3 15.1 %collective-permute-start.7 = (f32[16,72,128]{2,1,0:T(8,128)S(1)}, f32[16,72,128]{2,1,0:T(8,128)S(1)}, u32[]{:S(2)}, u32[]{:S(2)}) collective-permute-start(f32[16,72,128]{2,1,0:T(8,128)S(1)} %slice.84), channel_id=1, source_target_pairs={{0,12},{1,13},{2,14},{3,15},{4,0},{5,1},{6,2},{7,3},{8,4},{9,5},{1... | collective-permute-start | bytes 1769480 | tf_op jit(solution)/shard_map/ppermute | solution.py:28
  218.2 27.0 %collective-permute-start.16 = (f32[8,144,128]{2,1,0:T(8,128)}, f32[8,144,128]{2,1,0:T(8,128)S(1)}, u32[]{:S(2)}, u32[]{:S(2)}) collective-permute-start(f32[8,144,128]{2,1,0:T(8,128)} %get-tuple-element.21), channel_id=1, source_target_pairs={{16,0},{32,16},{48,32},{64,48},{80,64},{96,80},{112,96},{17,1},{33... | collective-permute-start | bytes 1769480 | tf_op jit(solution)/shard_map/ppermute | solution.py:48
  219.5 25.7 %collective-permute-start.17 = (f32[8,144,128]{2,1,0:T(8,128)}, f32[8,144,128]{2,1,0:T(8,128)S(1)}, u32[]{:S(2)}, u32[]{:S(2)}) collective-permute-start(f32[8,144,128]{2,1,0:T(8,128)} %get-tuple-element.22), channel_id=1, source_target_pairs={{0,16},{16,32},{32,48},{48,64},{64,80},{80,96},{96,112},{1,17},{17... | collective-permute-start | bytes 1769480 | tf_op jit(solution)/shard_map/ppermute | solution.py:48
  222.6 22.6 %collective-permute-start.18 = (f32[8,144,128]{2,1,0:T(8,128)}, f32[8,144,128]{2,1,0:T(8,128)S(1)}, u32[]{:S(2)}, u32[]{:S(2)}) collective-permute-start(f32[8,144,128]{2,1,0:T(8,128)} %get-tuple-element.23), channel_id=1, source_target_pairs={{32,0},{48,16},{64,32},{80,48},{96,64},{112,80},{33,1},{49,17},{65... | collective-permute-start | bytes 1769480 | tf_op jit(solution)/shard_map/ppermute | solution.py:48
  223.9 22.2 %collective-permute-start.19 = (f32[8,144,128]{2,1,0:T(8,128)}, f32[8,144,128]{2,1,0:T(8,128)S(1)}, u32[]{:S(2)}, u32[]{:S(2)}) collective-permute-start(f32[8,144,128]{2,1,0:T(8,128)} %get-tuple-element.24), channel_id=1, source_target_pairs={{0,32},{16,48},{32,64},{48,80},{64,96},{80,112},{1,33},{17,49},{33... | collective-permute-start | bytes 1769480 | tf_op jit(solution)/shard_map/ppermute | solution.py:48
  280.9 27.1 %collective-permute-start.32 = (f32[32,72,128]{2,1,0:T(8,128)S(1)}, f32[32,72,128]{2,1,0:T(8,128)S(1)}, u32[]{:S(2)}, u32[]{:S(2)}) collective-permute-start(f32[32,72,128]{2,1,0:T(8,128)S(1)} %get-tuple-element.63), channel_id=1, source_target_pairs={{0,1},{1,2},{2,3},{3,0},{4,5},{5,6},{6,7},{7,4},{8,9},{9,10},{10,1... | collective-permute-start | bytes 3538952 | tf_op jit(solution)/shard_map/ppermute | solution.py:25
  281.0 27.1 %collective-permute-start.33 = (f32[32,72,128]{2,1,0:T(8,128)S(1)}, f32[32,72,128]{2,1,0:T(8,128)S(1)}, u32[]{:S(2)}, u32[]{:S(2)}) collective-permute-start(f32[32,72,128]{2,1,0:T(8,128)S(1)} %get-tuple-element.63), channel_id=1, source_target_pairs={{0,3},{1,0},{2,1},{3,2},{4,7},{5,4},{6,5},{7,6},{8,11},{9,8},{10,9... | collective-permute-start | bytes 3538952 | tf_op jit(solution)/shard_map/ppermute | solution.py:26
  285.6 26.4 %collective-permute-start.24 = (f32[32,72,128]{2,1,0:T(8,128)S(1)}, f32[32,72,128]{2,1,0:T(8,128)S(1)}, u32[]{:S(2)}, u32[]{:S(2)}) collective-permute-start(f32[32,72,128]{2,1,0:T(8,128)S(1)} %get-tuple-element.67), channel_id=1, source_target_pairs={{0,4},{1,5},{2,6},{3,7},{4,8},{5,9},{6,10},{7,11},{8,12},{9,13},{1... | collective-permute-start | bytes 3538952 | tf_op jit(solution)/shard_map/ppermute | solution.py:25
  285.6 26.5 %collective-permute-start.25 = (f32[32,72,128]{2,1,0:T(8,128)S(1)}, f32[32,72,128]{2,1,0:T(8,128)S(1)}, u32[]{:S(2)}, u32[]{:S(2)}) collective-permute-start(f32[32,72,128]{2,1,0:T(8,128)S(1)} %get-tuple-element.67), channel_id=1, source_target_pairs={{0,12},{1,13},{2,14},{3,15},{4,0},{5,1},{6,2},{7,3},{8,4},{9,5},{1... | collective-permute-start | bytes 3538952 | tf_op jit(solution)/shard_map/ppermute | solution.py:26
  308.0 13.5 %collective-permute-start.34 = (f32[16,72,128]{2,1,0:T(8,128)S(1)}, f32[16,72,128]{2,1,0:T(8,128)S(1)}, u32[]{:S(2)}, u32[]{:S(2)}) collective-permute-start(f32[16,72,128]{2,1,0:T(8,128)S(1)} %slice.96), channel_id=1, source_target_pairs={{0,1},{1,2},{2,3},{3,0},{4,5},{5,6},{6,7},{7,4},{8,9},{9,10},{10,1... | collective-permute-start | bytes 1769480 | tf_op jit(solution)/shard_map/ppermute | solution.py:27
  308.2 13.4 %collective-permute-start.35 = (f32[16,72,128]{2,1,0:T(8,128)S(1)}, f32[16,72,128]{2,1,0:T(8,128)S(1)}, u32[]{:S(2)}, u32[]{:S(2)}) collective-permute-start(f32[16,72,128]{2,1,0:T(8,128)S(1)} %slice.97), channel_id=1, source_target_pairs={{0,3},{1,0},{2,1},{3,2},{4,7},{5,4},{6,5},{7,6},{8,11},{9,8},{10,9... | collective-permute-start | bytes 1769480 | tf_op jit(solution)/shard_map/ppermute | solution.py:28
  312.0 12.9 %collective-permute-start.26 = (f32[16,72,128]{2,1,0:T(8,128)S(1)}, f32[16,72,128]{2,1,0:T(8,128)S(1)}, u32[]{:S(2)}, u32[]{:S(2)}) collective-permute-start(f32[16,72,128]{2,1,0:T(8,128)S(1)} %slice.92), channel_id=1, source_target_pairs={{0,4},{1,5},{2,6},{3,7},{4,8},{5,9},{6,10},{7,11},{8,12},{9,13},{1... | collective-permute-start | bytes 1769480 | tf_op jit(solution)/shard_map/ppermute | solution.py:27
  312.2 13.7 %collective-permute-start.27 = (f32[16,72,128]{2,1,0:T(8,128)S(1)}, f32[16,72,128]{2,1,0:T(8,128)S(1)}, u32[]{:S(2)}, u32[]{:S(2)}) collective-permute-start(f32[16,72,128]{2,1,0:T(8,128)S(1)} %slice.93), channel_id=1, source_target_pairs={{0,12},{1,13},{2,14},{3,15},{4,0},{5,1},{6,2},{7,3},{8,4},{9,5},{1... | collective-permute-start | bytes 1769480 | tf_op jit(solution)/shard_map/ppermute | solution.py:28
  405.1 19.9 %collective-permute-start.38 = (f32[8,144,128]{2,1,0:T(8,128)}, f32[8,144,128]{2,1,0:T(8,128)S(1)}, u32[]{:S(2)}, u32[]{:S(2)}) collective-permute-start(f32[8,144,128]{2,1,0:T(8,128)} %get-tuple-element.30), channel_id=1, source_target_pairs={{32,0},{48,16},{64,32},{80,48},{96,64},{112,80},{33,1},{49,17},{65... | collective-permute-start | bytes 1769480 | tf_op jit(solution)/shard_map/ppermute | solution.py:48
  406.4 18.6 %collective-permute-start.39 = (f32[8,144,128]{2,1,0:T(8,128)}, f32[8,144,128]{2,1,0:T(8,128)S(1)}, u32[]{:S(2)}, u32[]{:S(2)}) collective-permute-start(f32[8,144,128]{2,1,0:T(8,128)} %get-tuple-element.31), channel_id=1, source_target_pairs={{0,32},{16,48},{32,64},{48,80},{64,96},{80,112},{1,33},{17,49},{33... | collective-permute-start | bytes 1769480 | tf_op jit(solution)/shard_map/ppermute | solution.py:48
  (28 other events, 471.1 us)

commit v2 on v0

v2 whole, which is shorter than its diff:
```python
import functools

import jax
import jax.numpy as jnp
from jax import lax
from jax.experimental import pallas as pl
from jax.experimental.pallas import tpu as pltpu
from jax.sharding import PartitionSpec as P

STEP = 0.08
N = 96
M = 8
ROWS = 144
PIECE = 9
MEMBERS = 16
TIERS = 8
WEIGHT = 9 * M
FIELDS = 6 * M
F32 = jnp.float32
BF16 = jnp.bfloat16
CHUNK = 128


def passed_along(value, steps):
    low, high = max(0, -steps), min(TIERS, TIERS - steps)
    return lax.ppermute(value, "tier", [(source, source + steps) for source in range(low, high)])


def entry(table, level, member, field, slot):
    return table[(level * MEMBERS + member) * FIELDS + field * M + slot]


def nodes_kernel(table, place, corr_real, corr_imag, decay, weight, mode, scale):
    tier, member = place[0], place[1]
    level = tier.astype(F32)

    def node(at, where, rate):
        down_mode = entry(table, *where[:2], 5, where[2])
        mode[at] = entry(table, *where[:2], 2, where[2])
        mode[3 * M + at] = down_mode
        scale[at] = corr_real[down_mode]
        scale[3 * M + at] = corr_imag[down_mode]
        scale[6 * M + at] = rate * decay[down_mode]

    def one(m, carry):
        node(m, (0, member, m), STEP * level)
        node(M + m, (1, entry(table, 0, member, 0, m), entry(table, 0, member, 1, m)), STEP * (level + 1.0))
        node(
            2 * M + m,
            (2, entry(table, 0, member, 3, m), entry(table, 0, member, 4, m)),
            STEP * jnp.maximum(level - 1.0, 0.0),
        )
        return carry

    lax.fori_loop(0, M, one, 0)
    for kind in range(6):
        scale[WEIGHT + kind] = weight[kind]


def make_nodes(table, place, corr_real, corr_imag, decay, weight):
    smem = pl.BlockSpec(memory_space=pltpu.SMEM)
    return pl.pallas_call(
        nodes_kernel,
        in_specs=[smem] * 6,
        out_specs=[smem, smem],
        out_shape=[jax.ShapeDtypeStruct((6 * M,), jnp.int32), jax.ShapeDtypeStruct((WEIGHT + 6,), F32)],
        name="nodes",
    )(table, place, corr_real, corr_imag, decay, weight)


def split(value):
    high = value.astype(BF16)
    return high, (value - high.astype(F32)).astype(BF16)


def deal_kernel(state, links, out):
    for member in range(MEMBERS):
        for m in range(M):
            out[member, m * PIECE : (m + 1) * PIECE, :] = state[m, member * PIECE : (member + 1) * PIECE, :]
        out[member, M * PIECE :, :] = links[...]


def dealt(state, links):
    return pl.pallas_call(
        deal_kernel,
        out_shape=jax.ShapeDtypeStruct((MEMBERS, M * PIECE + 8, 128), F32),
        compiler_params=pltpu.CompilerParams(vmem_limit_bytes=16 * 1024 * 1024),
        name="deal",
    )(state, links)


def pick_near_kernel(table, own, out):
    def one(member, carry):
        for m in range(M):
            for kind, first in ((0, 0), (1, 3)):
                who, slot = entry(table, 0, member, first, m), entry(table, 0, member, first + 1, m)
                who, slot = (entry(table, kind + 1, who, 3 - first + field, slot) for field in range(2))
                row = (kind * M + m) * PIECE
                out[member, row : row + PIECE, :] = own[who, pl.ds(slot * PIECE, PIECE), :]
        return carry

    lax.fori_loop(0, MEMBERS, one, 0)


def pick_other_kernel(table, place, mate, cross, above2, below2, out):
    def one(above, below, member, carry):
        for m in range(M):
            for kind, source, source2, first in ((0, above, above2, 0), (1, below, below2, 3)):
                who, slot = entry(table, 0, member, first, m), entry(table, 0, member, first + 1, m)
                row = (m * 4 + kind) * PIECE
                out[member, row : row + PIECE, :] = source[who, pl.ds(slot * PIECE, PIECE), :]
                who, slot = (entry(table, kind + 1, who, first + field, slot) for field in range(2))
                row += 2 * PIECE
                out[member, row : row + PIECE, :] = source2[who, pl.ds(slot * PIECE, PIECE), :]
        return carry

    lower_core = jnp.bitwise_and(place[0], 1) == 0
    pl.when(lower_core)(lambda: lax.fori_loop(0, MEMBERS, functools.partial(one, mate, cross), None))
    pl.when(jnp.logical_not(lower_core))(lambda: lax.fori_loop(0, MEMBERS, functools.partial(one, cross, mate), None))


def picked(kernel, kinds, scalars, blocks):
    return pl.pallas_call(
        kernel,
        in_specs=[pl.BlockSpec(memory_space=pltpu.SMEM)] * len(scalars)
        + [pl.BlockSpec(memory_space=pltpu.VMEM)] * len(blocks),
        out_specs=pl.BlockSpec(memory_space=pltpu.VMEM),
        out_shape=jax.ShapeDtypeStruct((MEMBERS, kinds * M * PIECE, 128), F32),
        compiler_params=pltpu.CompilerParams(vmem_limit_bytes=16 * 1024 * 1024),
        name="pick",
    )(*scalars, *blocks)


def unpack(source, target):
    lane = lax.broadcasted_iota(jnp.int32, (24, 128), 1)
    for part in range(2):
        a, b, c = (source[pl.ds(2 * k + part, 24, stride=6), :] for k in range(3))
        target[pl.ds(part * N, 24, stride=4), :] = a
        target[pl.ds(part * N + 1, 24, stride=4), :] = jnp.where(lane < 32, pltpu.roll(a, 32, 1), pltpu.roll(b, 32, 1))
        target[pl.ds(part * N + 2, 24, stride=4), :] = jnp.where(lane < 64, pltpu.roll(b, 64, 1), pltpu.roll(c, 64, 1))
        target[pl.ds(part * N + 3, 24, stride=4), :] = pltpu.roll(c, 96, 1)


def pack(source, target):
    lane = lax.broadcasted_iota(jnp.int32, (24, 128), 1)
    for part in range(2):
        a, b, c, d = (source[pl.ds(part * N + k, 24, stride=4), :] for k in range(4))
        b, c, d = pltpu.roll(b, 96, 1), pltpu.roll(c, 64, 1), pltpu.roll(d, 32, 1)
        target[pl.ds(part, 24, stride=6), :] = jnp.where(lane < 96, a, b)
        target[pl.ds(part + 2, 24, stride=6), :] = jnp.where(lane < 64, b, c)
        target[pl.ds(part + 4, 24, stride=6), :] = jnp.where(lane < 32, c, d)


def halved(value):
    high, low = split(value)
    return (high[:N], high[N:]), (low[:N], low[N:])


def commuted(*terms):
    lefts, rights, tall, wide = [], [], [], []
    pad = jnp.zeros((CHUNK - N, 2 * CHUNK), BF16)
    thin = pad[:, :CHUNK]
    for operator, a, b in terms:
        high, low = split(operator)
        lefts += [high, low, high]
        rights += [high, thin, high, thin, low, thin]
        high, low = (jnp.concatenate(piece, axis=1) for piece in a)
        tall += [high, pad, high, pad, low, pad]
        high, low = (jnp.concatenate(piece, axis=0) for piece in b)
        wide += [high, low, high]
    from_left = jnp.dot(
        jnp.concatenate(lefts, axis=1), jnp.concatenate(tall, axis=0), preferred_element_type=F32
    )
    from_right = jnp.dot(
        jnp.concatenate(wide, axis=1), jnp.concatenate(rights, axis=0), preferred_element_type=F32
    )
    return jnp.concatenate([from_left[:, CHUNK:] - from_right[N:], from_right[:N] - from_left[:, :CHUNK]], axis=0)


def widened(operator):
    return jnp.concatenate([operator, jnp.zeros((N, CHUNK - N), F32)], axis=1)


def plainly(operator, value):
    pieces = halved(value)
    return operator, pieces, pieces


def with_factor(operator, value, cr, ci):
    dr, di = value[:N], value[N:]
    rr, ri, ir, ii = cr * dr, cr * di, ci * dr, ci * di
    a, b = jnp.concatenate([rr - ii, ir + ri], axis=0), jnp.concatenate([rr + ii, ri - ir], axis=0)
    return operator, halved(a), halved(b)


def assembled(source, row, raw, target):
    for member in range(MEMBERS):
        raw[member * PIECE : (member + 1) * PIECE, :] = source[member, pl.ds(row, PIECE), :]
    unpack(raw, target)


def factor(scale, kind, m):
    return scale[kind * M + m], scale[3 * M + kind * M + m]


def early_kernel(last, mode, scale, state, near, core, *refs):
    ops, refs = refs[: 2 * TOGETHER], refs[2 * TOGETHER :]
    first, first_up, first_down, raw, plain = refs[-5:]
    for turn in range(TOGETHER):
        m = pl.program_id(0) * TOGETHER + turn
        above_op, below_op = ops[2 * turn : 2 * turn + 2]
        if last:
            own = state[turn]
        else:
            unpack(state.at[turn], refs[0].at[turn])
            own = refs[0][turn]
        for kind in range(2):
            assembled(near, (kind * M + m) * PIECE, raw.at[turn, kind], plain.at[turn, kind])
        first[turn] = commuted(plainly(widened(STEP * core[...]), own)) - scale[6 * M + m] * own
        first_up[turn] = commuted(
            with_factor(widened(scale[WEIGHT + 4] * above_op[0]), plain[turn, 0], *factor(scale, 1, m))
        )
        first_down[turn] = commuted(plainly(widened(scale[WEIGHT + 2] * below_op[0]), plain[turn, 1]))


def late_kernel(last, mode, scale, other, core, *refs):
    ops, (base, part, part_up, part_down), refs = refs[: 4 * TOGETHER], refs[4 * TOGETHER :][:4], refs[4 * TOGETHER + 4 :]
    if last:
        result, raw, plain = refs
    else:
        result, following, total, raw, plain = refs
    for turn in range(TOGETHER):
        m = pl.program_id(0) * TOGETHER + turn
        up_op, down_op, above_op, below_op = ops[4 * turn : 4 * turn + 4]
        for kind in range(4):
            assembled(other, (turn * 4 + kind) * PIECE, raw.at[turn, kind], plain.at[turn, kind])
        up, down, up2, down2 = (plain[turn, kind] for kind in range(4))
        hamiltonian = widened(STEP * core[...])
        up_op, down_op = widened(scale[WEIGHT] * up_op[0]), widened(scale[WEIGHT + 3] * down_op[0])
        own_factor = factor(scale, 0, m)
        up_pieces = halved(up)
        first = part[turn] + commuted((up_op, up_pieces, up_pieces), with_factor(down_op, down, *own_factor))
        first_up = (
            part_up[turn]
            + commuted((hamiltonian, up_pieces, up_pieces), plainly(widened(scale[WEIGHT + 1] * above_op[0]), up2))
            - scale[7 * M + m] * up
        )
        first_down = (
            part_down[turn]
            + commuted(
                plainly(hamiltonian, down),
                with_factor(widened(scale[WEIGHT + 5] * below_op[0]), down2, *factor(scale, 2, m)),
            )
            - scale[8 * M + m] * down
        )
        second = (
            commuted(plainly(hamiltonian, first), plainly(up_op, first_up), with_factor(down_op, first_down, *own_factor))
            - scale[6 * M + m] * first
        )
        if last:
            plain[turn, 0] = base[turn] + (1.0 / 6.0) * first + (1.0 / 24.0) * second
            pack(plain.at[turn, 0], result.at[turn])
        else:
            following[turn] = second
            plain[turn, 0] = second
            total[turn] = base[turn] + first + 0.5 * second
            pack(plain.at[turn, 0], raw.at[turn, 0])
            for member in range(MEMBERS):
                result[member, pl.ds(m * PIECE, PIECE), :] = raw[turn, 0, member * PIECE : (member + 1) * PIECE, :]


TOGETHER = 2
PLAIN = pl.BlockSpec((TOGETHER, 2 * N, 128), lambda step, mode, scale: (step, 0, 0))
WHOLE = pl.BlockSpec((TOGETHER, ROWS, 128), lambda step, mode, scale: (step, 0, 0))
SUMS = pltpu.HBM((M, 2 * N, 128), F32)


def all_of(shape):
    return pl.BlockSpec(shape, lambda step, mode, scale: (0,) * len(shape))


def operator_specs(*lists):
    return [
        pl.BlockSpec((1, N, N), lambda step, mode, scale, at=at * M + turn: (mode[step * TOGETHER + at], 0, 0))
        for turn in range(TOGETHER)
        for at in lists
    ]


def by_matrix(kernel, name, in_specs, out_specs, out_shape, raws, plains):
    return pl.pallas_call(
        kernel,
        grid_spec=pltpu.PrefetchScalarGridSpec(
            num_scalar_prefetch=2,
            grid=(M // TOGETHER,),
            in_specs=in_specs,
            out_specs=out_specs,
            scratch_shapes=[pltpu.VMEM((TOGETHER, raws, ROWS, 128), F32), pltpu.VMEM((TOGETHER, plains, 2 * N, 128), F32)],
        ),
        out_shape=out_shape,
        compiler_params=pltpu.CompilerParams(vmem_limit_bytes=32 * 1024 * 1024),
        name=name,
    )


def kept(*values):
    return [pltpu.with_memory_space_constraint(value, pltpu.HBM) for value in values]


def early(nodes, state, near, operators, last):
    hamiltonian, coupling = operators
    specs = [PLAIN if last else WHOLE, all_of(near.shape), all_of(hamiltonian.shape)] + operator_specs(4, 2)
    outs = 3 if last else 4
    call = by_matrix(functools.partial(early_kernel, last), "early", specs, [PLAIN] * outs, [SUMS] * outs, 2, 2)
    return call(*nodes, *kept(state), near, hamiltonian, *kept(*[coupling] * (2 * TOGETHER)))


def late(nodes, other, operators, base, parts, last):
    hamiltonian, coupling = operators
    specs = [pl.BlockSpec((MEMBERS, TOGETHER * 4 * PIECE, 128), lambda step, mode, scale: (0, step, 0))]
    specs += [all_of(hamiltonian.shape)] + operator_specs(0, 3, 1, 5) + [PLAIN] * 4
    if last:
        outs = [WHOLE], [jax.ShapeDtypeStruct((M, ROWS, 128), F32)]
    else:
        blocks = (MEMBERS, M * PIECE, 128)
        outs = [all_of(blocks), PLAIN, PLAIN], [jax.ShapeDtypeStruct(blocks, F32), SUMS, SUMS]
    call = by_matrix(functools.partial(late_kernel, last), "late", specs, *outs, 4, 4)
    return call(*nodes, other, hamiltonian, *kept(*[coupling] * (4 * TOGETHER), base, *parts))


def shards(
    density,
    hamiltonian,
    coupling,
    decay_rate,
    corr_real,
    corr_imag,
    up_member,
    up_slot,
    up_mode,
    down_member,
    down_slot,
    down_mode,
):
    tier, member = lax.axis_index("tier"), lax.axis_index("member")
    fields = jnp.stack([f[:, 0] for f in (up_member, up_slot, up_mode, down_member, down_slot, down_mode)])
    fields = fields.reshape(1, FIELDS).astype(F32)
    links = jnp.pad(fields, ((0, 7), (0, 128 - FIELDS)))
    place = jnp.stack([tier, member]).astype(jnp.int32)
    levels = jnp.stack([tier, tier + 1, tier - 1]).astype(F32)
    ups = jnp.where(levels + 1.0 < TIERS, jnp.sqrt(levels + 1.0), 0.0)
    downs = jnp.sqrt(jnp.maximum(levels, 0.0))
    weight = STEP * jnp.concatenate([ups, downs])

    def swapped(blocks):
        return lax.all_to_all(blocks, "member", split_axis=0, concat_axis=0, tiled=True)

    def link_fields(tier_blocks):
        return tier_blocks[:, M * PIECE, :FIELDS].reshape(-1).astype(jnp.int32)

    def two_steps(own, table, state, operators, nodes, before):
        last = before is not None
        mate = lax.ppermute(own, "tier", [(source, source ^ 1) for source in range(TIERS)])
        above2, below2 = passed_along(own, -2), passed_along(own, 2)
        near = swapped(picked(pick_near_kernel, 2, [table], [own]))
        cross = jnp.where(tier % 2 == 0, above2, below2)
        cross = lax.ppermute(cross, "tier", [(source, source ^ 1) for source in range(TIERS)])
        other = swapped(picked(pick_other_kernel, 4, [table, place], [mate, cross, above2, below2]))
        *base, part, part_up, part_down = early(nodes, state, near, operators, last)
        return late(nodes, other, operators, before if last else base[0], (part, part_up, part_down), last)

    state = density.reshape(M, 2, ROWS // 2, 128).transpose(0, 2, 1, 3).reshape(M, ROWS, 128)
    own = swapped(dealt(state, links))
    table = link_fields(own)
    table = jnp.concatenate([table, passed_along(table, -1), passed_along(table, 1)])
    own, table = lax.optimization_barrier((own, table))
    nodes = make_nodes(table, place, corr_real, corr_imag, decay_rate, weight)
    operators = hamiltonian, coupling
    blocks, state, total = two_steps(own, table, state, operators, nodes, None)
    (result,) = two_steps(swapped(blocks), table, state, operators, nodes, total)
    return result.reshape(M, ROWS // 2, 2, 128).transpose(0, 2, 1, 3).reshape(M, 2, N * N)


def solution(mesh):
    return jax.shard_map(
        shards,
        mesh=mesh,
        in_specs=(P(("tier", "member"), None, None),) + (P(),) * 5 + (P(("tier", "member"), None),) * 6,
        out_specs=P(("tier", "member"), None, None),
        check_vma=False,
    )
```

time: 765 us -> 210 us (0.27)
  the two profiles are of different devices: /device:TPU:1 before, /device:TPU:0 now
where the time goes in v2:
time: 210 us; the launch traced here: 209 us
  waiting for transfers between devices  84.4 us (40%)
  Pallas kernels  44.9 us (21%)
  blocking collectives  35.6 us (17%)
  starting transfers between devices  32.1 us (15%)
  local copies, waits for them, and re-layouts  10.6 us (5%)
    all_to_all x4, waiting for transfers between devices, swapped(): lax.all_to_all(blocks, 'member', split_axis=0, concat_axis=0, tiled=True)  60.1 us
    all_to_all x2, blocking collectives, swapped(): lax.all_to_all(blocks, 'member', split_axis=0, concat_axis=0, tiled=True)  35.6 us
    pallas_call x2, Pallas kernels, late(): call(*nodes, other, hamiltonian, *kept(*[coupling] * (4 * TOGETHER), base...  21.4 us
    ppermute x6, waiting for transfers between devices, passed_along(): lax.ppermute(value, 'tier', [(source, source + steps) for source in range...  20.3 us
    all_to_all x4, starting transfers between devices, swapped(): lax.all_to_all(blocks, 'member', split_axis=0, concat_axis=0, tiled=True)  14.8 us
    ppermute x6, starting transfers between devices, passed_along(): lax.ppermute(value, 'tier', [(source, source + steps) for source in range...  14.4 us
    pallas_call x2, Pallas kernels, early(): call(*nodes, *kept(state), near, hamiltonian, *kept(*[coupling] * (2 * TO...  11.1 us
    pallas_call x4, Pallas kernels, picked(): pl.pallas_call(kernel, in_specs=[pl.BlockSpec(memory_space=pltpu.SMEM)] *...  10.7 us
  transfers between devices with their start and end apart: 14, of which 11 were waited for; matrix products, arithmetic and copies ran while one was open for 1% of the time, Pallas kernels for 11%

profile of v2, /device:TPU:0, one launch (start us, length us, event | category | flops | bytes accessed | tf_op | source)
XLA Modules:
  0.0 209.5 jit_solution(17797957904575390268)
XLA Ops:
  2.0 19.9 %all_to_all.30.own = f32[16,80,128]{2,1,0:T(8,128)S(1)} all-to-all(f32[16,80,128]{2,1,0:T(8,128)S(1)} %deal.1), channel_id=1, replica_groups=mesh['tier'=8,'member'=16] {'member'}, dimensions={0} | all-to-all | bytes 1310720 | tf_op jit(solution)/shard_map/all_to_all | solution.py:356
  24.6 3.9 %collective-permute-done = s32[768]{0:T(1024)S(1)} collective-permute-done((s32[768]{0:T(1024)S(1)}, s32[768]{0:T(1024)S(1)}, u32[]{:S(2)}, u32[]{:S(2)}) %collective-permute-start) | collective-permute-done | bytes 3104 | tf_op jit(solution)/shard_map/ppermute | solution.py:26
  28.5 4.2 %collective-permute-start.4 = (f32[16,80,128]{2,1,0:T(8,128)S(1)}, f32[16,80,128]{2,1,0:T(8,128)S(1)}, u32[]{:S(2)}, u32[]{:S(2)}) collective-permute-start(f32[16,80,128]{2,1,0:T(8,128)S(1)} %all_to_all.30.own), channel_id=1, source_target_pairs={{0,32},{16,48},{32,64},{48,80},{64,96},{80,112},{1,33},{17,49},{33... | collective-permute-start | bytes 1966088 | tf_op jit(solution)/shard_map/ppermute | solution.py:26
  34.0 2.8 %pick.5 = f32[16,144,128]{2,1,0:T(8,128)} custom-call(s32[2304]{0:T(1024)S(1)} %pad_add_fusion.table, f32[16,80,128]{2,1,0:T(8,128)S(1)} %all_to_all.30.own), custom_call_target="tpu_custom_call" | custom-call | tf_op jit(solution)/shard_map/pick/pallas_call | solution.py:123
  36.9 3.7 %all-to-all-start.2 = ((f32[16,144,128]{2,1,0:T(8,128)}), f32[16,144,128]{2,1,0:T(8,128)S(1)}, u32[]{:S(2)}, u32[]{:S(2)}) async-start(f32[16,144,128]{2,1,0:T(8,128)} %pick.5), calls=%async_computation.2 | async-start | bytes 2359296 | tf_op jit(solution)/shard_map/all_to_all | solution.py:356
  42.4 4.4 %collective-permute-done.4.below2 = f32[16,80,128]{2,1,0:T(8,128)S(1)} collective-permute-done((f32[16,80,128]{2,1,0:T(8,128)S(1)}, f32[16,80,128]{2,1,0:T(8,128)S(1)}, u32[]{:S(2)}, u32[]{:S(2)}) %collective-permute-start.4) | collective-permute-done | bytes 655392 | tf_op jit(solution)/shard_map/ppermute | solution.py:26
  46.7 4.8 %collective-permute-done.3.above2 = f32[16,80,128]{2,1,0:T(8,128)S(1)} collective-permute-done((f32[16,80,128]{2,1,0:T(8,128)S(1)}, f32[16,80,128]{2,1,0:T(8,128)S(1)}, u32[]{:S(2)}, u32[]{:S(2)}) %collective-permute-start.3) | collective-permute-done | bytes 655392 | tf_op jit(solution)/shard_map/ppermute | solution.py:26
  55.3 2.8 %pick.4 = f32[16,288,128]{2,1,0:T(8,128)S(1)} custom-call(s32[2304]{0:T(1024)S(1)} %pad_add_fusion.table, s32[2]{0:T(128)S(1)} %pad_add_fusion.1.place, f32[16,80,128]{2,1,0:T(8,128)} %collective-permute-done.2.mate, f32[16,80,128]{2,1,0:T(8,128)} %collective-permute-done.5.cross, f32[16,80,128]{2,1,0:T(8,128)S(1)} %collective-permute-done.3.above2, ...), custom_call_target="tpu_custom_call" | custom-call | tf_op jit(solution)/shard_map/pick/pallas_call | solution.py:123
  61.3 3.7 %all-to-all-start.1 = ((f32[16,288,128]{2,1,0:T(8,128)}), f32[16,288,128]{2,1,0:T(8,128)S(1)}, u32[]{:S(2)}, u32[]{:S(2)}) async-start(f32[16,288,128]{2,1,0:T(8,128)} %copy-done), calls=%async_computation.1 | async-start | bytes 4718592 | tf_op jit(solution)/shard_map/all_to_all | solution.py:356
  69.4 5.6 %early.2 = (f32[8,192,128]{2,1,0:T(8,128)}, f32[8,192,128]{2,1,0:T(8,128)}, f32[8,192,128]{2,1,0:T(8,128)}, f32[8,192,128]{2,1,0:T(8,128)}) custom-call(s32[48]{0:T(128)S(1)} %copy-done.9, f32[78]{0:T(128)S(1)} %copy-done.11, f32[8,144,128]{2,1,0:T(8,128)} %bitcast.20, f32[16,144,128]{2,1,0:T(8,128)S(1)} %all-to-all-done.2.near, f32[96,96]{1,0:T(8,128)S(1)} %copy-done.3, ...), custom_call_target="tpu_custom_call" | custom-call | tf_op jit(solution)/shard_map/early/pallas_call | solution.py:315
  75.0 28.6 %all-to-all-done.1.other = f32[16,288,128]{2,1,0:T(8,128)S(1)} async-done(((f32[16,288,128]{2,1,0:T(8,128)}), f32[16,288,128]{2,1,0:T(8,128)S(1)}, u32[]{:S(2)}, u32[]{:S(2)}) %all-to-all-start.1) | async-done | bytes 2359328 | tf_op jit(solution)/shard_map/all_to_all | solution.py:356
  105.1 10.8 %late.2 = (f32[16,72,128]{2,1,0:T(8,128)S(1)}, f32[8,192,128]{2,1,0:T(8,128)}, f32[8,192,128]{2,1,0:T(8,128)}) custom-call(s32[48]{0:T(128)S(1)} %copy-done.10, f32[78]{0:T(128)S(1)} %copy-done.12, f32[16,288,128]{2,1,0:T(8,128)S(1)} %all-to-all-done.1.other, f32[96,96]{1,0:T(8,128)S(1)} %copy-done.4, f32[96,96,96]{2,1,0:T(8,128)} %refs_7_.3, ...), custom_call_target="tpu_custom_call" | custom-call | tf_op jit(solution)/shard_map/late/pallas_call | solution.py:328
  115.9 15.7 %all_to_all.31.own = f32[16,72,128]{2,1,0:T(8,128)S(1)} all-to-all(f32[16,72,128]{2,1,0:T(8,128)S(1)} %get-tuple-element.27), channel_id=1, replica_groups=mesh['tier'=8,'member'=16] {'member'}, dimensions={0} | all-to-all | bytes 1179648 | tf_op jit(solution)/shard_map/all_to_all | solution.py:356
  131.6 5.0 %collective-permute-start.8 = (f32[16,72,128]{2,1,0:T(8,128)S(1)}, f32[16,72,128]{2,1,0:T(8,128)S(1)}, u32[]{:S(2)}, u32[]{:S(2)}) collective-permute-start(f32[16,72,128]{2,1,0:T(8,128)S(1)} %all_to_all.31.own), channel_id=1, source_target_pairs={{0,32},{16,48},{32,64},{48,80},{64,96},{80,112},{1,33},{17,49},{33... | collective-permute-start | bytes 1769480 | tf_op jit(solution)/shard_map/ppermute | solution.py:26
  137.9 2.9 %pick.7 = f32[16,144,128]{2,1,0:T(8,128)} custom-call(s32[2304]{0:T(1024)S(1)} %copy-done.8, f32[16,72,128]{2,1,0:T(8,128)S(1)} %all_to_all.31.own), custom_call_target="tpu_custom_call" | custom-call | tf_op jit(solution)/shard_map/pick/pallas_call | solution.py:123
  140.8 3.7 %all-to-all-start.5 = ((f32[16,144,128]{2,1,0:T(8,128)}), f32[16,144,128]{2,1,0:T(8,128)S(1)}, u32[]{:S(2)}, u32[]{:S(2)}) async-start(f32[16,144,128]{2,1,0:T(8,128)} %pick.7), calls=%async_computation.5 | async-start | bytes 2359296 | tf_op jit(solution)/shard_map/all_to_all | solution.py:356
  144.6 3.2 %collective-permute-done.8.below2 = f32[16,72,128]{2,1,0:T(8,128)S(1)} collective-permute-done((f32[16,72,128]{2,1,0:T(8,128)S(1)}, f32[16,72,128]{2,1,0:T(8,128)S(1)}, u32[]{:S(2)}, u32[]{:S(2)}) %collective-permute-start.8) | collective-permute-done | bytes 589856 | tf_op jit(solution)/shard_map/ppermute | solution.py:26
  147.8 4.1 %collective-permute-done.7.above2 = f32[16,72,128]{2,1,0:T(8,128)S(1)} collective-permute-done((f32[16,72,128]{2,1,0:T(8,128)S(1)}, f32[16,72,128]{2,1,0:T(8,128)S(1)}, u32[]{:S(2)}, u32[]{:S(2)}) %collective-permute-start.7) | collective-permute-done | bytes 589856 | tf_op jit(solution)/shard_map/ppermute | solution.py:26
  154.7 2.2 %pick.6 = f32[16,288,128]{2,1,0:T(8,128)S(1)} custom-call(s32[2304]{0:T(1024)S(1)} %copy-done.8, s32[2]{0:T(128)S(1)} %copy-done.15, f32[16,72,128]{2,1,0:T(8,128)S(1)} %collective-permute-done.6.mate, f32[16,72,128]{2,1,0:T(8,128)S(1)} %collective-permute-done.9.cross, f32[16,72,128]{2,1,0:T(8,128)S(1)} %collective-permute-done.7.above2, ...), custom_call_target="tpu_custom_call" | custom-call | tf_op jit(solution)/shard_map/pick/pallas_call | solution.py:123
  158.3 3.8 %all-to-all-done.5.near = f32[16,144,128]{2,1,0:T(8,128)S(1)} async-done(((f32[16,144,128]{2,1,0:T(8,128)}), f32[16,144,128]{2,1,0:T(8,128)S(1)}, u32[]{:S(2)}, u32[]{:S(2)}) %all-to-all-start.5) | async-done | bytes 1179680 | tf_op jit(solution)/shard_map/all_to_all | solution.py:356
  162.1 3.7 %all-to-all-start.4 = ((f32[16,288,128]{2,1,0:T(8,128)}), f32[16,288,128]{2,1,0:T(8,128)S(1)}, u32[]{:S(2)}, u32[]{:S(2)}) async-start(f32[16,288,128]{2,1,0:T(8,128)} %copy-done.1), calls=%async_computation.4 | async-start | bytes 4718592 | tf_op jit(solution)/shard_map/all_to_all | solution.py:356
  166.7 5.5 %early.3 = (f32[8,192,128]{2,1,0:T(8,128)}, f32[8,192,128]{2,1,0:T(8,128)}, f32[8,192,128]{2,1,0:T(8,128)}) custom-call(s32[48]{0:T(128)S(1)} %copy-done.10, f32[78]{0:T(128)S(1)} %copy-done.13, f32[8,192,128]{2,1,0:T(8,128)} %get-tuple-element.29.state, f32[16,144,128]{2,1,0:T(8,128)S(1)} %all-to-all-done.5.near, f32[96,96]{1,0:T(8,128)S(1)} %copy-done.5, ...), custom_call_target="tpu_custom_call" | custom-call | tf_op jit(solution)/shard_map/early/pallas_call | solution.py:315
  172.2 25.9 %all-to-all-done.4.other = f32[16,288,128]{2,1,0:T(8,128)S(1)} async-done(((f32[16,288,128]{2,1,0:T(8,128)}), f32[16,288,128]{2,1,0:T(8,128)S(1)}, u32[]{:S(2)}, u32[]{:S(2)}) %all-to-all-start.4) | async-done | bytes 2359328 | tf_op jit(solution)/shard_map/all_to_all | solution.py:356
  198.9 10.6 %late.3 = f32[8,144,128]{2,1,0:T(8,128)} custom-call(s32[48]{0:T(128)S(1)} %copy-done.10, f32[78]{0:T(128)S(1)} %copy-done.13, f32[16,288,128]{2,1,0:T(8,128)S(1)} %all-to-all-done.4.other, f32[96,96]{1,0:T(8,128)S(1)} %copy-done.6, f32[96,96,96]{2,1,0:T(8,128)} %refs_7_.3, f32[96,96,96]{2,1,0:T(8,128)} %refs_7_.3, f32[96,96,96]{2,1,0:T(8,128)} %refs_7_.3, ...), custom_call_target="tpu_custom_call" | custom-call | tf_op jit(solution)/shard_map/late/pallas_call | solution.py:328
  (61 shorter events, 27.7 us)
Async XLA Ops:
  0.8 1.1 copy-start.2
  22.0 2.6 %collective-permute-start.1 = (s32[768]{0:T(1024)S(1)}, s32[768]{0:T(1024)S(1)}, u32[]{:S(2)}, u32[]{:S(2)}) collective-permute-start(s32[768]{0:T(1024)S(1)} %convert_element_type.28), channel_id=1, source_target_pairs={{0,16},{16,32},{32,48},{48,64},{64,80},{80,96},{96,112},{1,17},{17... | collective-permute-start | bytes 9224 | tf_op jit(solution)/shard_map/ppermute | solution.py:26
  23.2 5.2 %collective-permute-start = (s32[768]{0:T(1024)S(1)}, s32[768]{0:T(1024)S(1)}, u32[]{:S(2)}, u32[]{:S(2)}) collective-permute-start(s32[768]{0:T(1024)S(1)} %convert_element_type.28), channel_id=1, source_target_pairs={{16,0},{32,16},{48,32},{64,48},{80,64},{96,80},{112,96},{17,1},{33... | collective-permute-start | bytes 9224 | tf_op jit(solution)/shard_map/ppermute | solution.py:26
  28.5 26.8 %copy-start.7 = (s32[2304]{0:T(1024)}, s32[2304]{0:T(1024)S(1)}, u32[]{:S(2)}) copy-start(s32[2304]{0:T(1024)S(1)} %pad_add_fusion.table) | copy-start | bytes 27652
  28.5 18.3 %collective-permute-start.4 = (f32[16,80,128]{2,1,0:T(8,128)S(1)}, f32[16,80,128]{2,1,0:T(8,128)S(1)}, u32[]{:S(2)}, u32[]{:S(2)}) collective-permute-start(f32[16,80,128]{2,1,0:T(8,128)S(1)} %all_to_all.30.own), channel_id=1, source_target_pairs={{0,32},{16,48},{32,64},{48,80},{64,96},{80,112},{1,33},{17,49},{33... | collective-permute-start | bytes 1966088 | tf_op jit(solution)/shard_map/ppermute | solution.py:26
  32.7 18.8 %collective-permute-start.3 = (f32[16,80,128]{2,1,0:T(8,128)S(1)}, f32[16,80,128]{2,1,0:T(8,128)S(1)}, u32[]{:S(2)}, u32[]{:S(2)}) collective-permute-start(f32[16,80,128]{2,1,0:T(8,128)S(1)} %all_to_all.30.own), channel_id=1, source_target_pairs={{32,0},{48,16},{64,32},{80,48},{96,64},{112,80},{33,1},{49,17},{65... | collective-permute-start | bytes 1966088 | tf_op jit(solution)/shard_map/ppermute | solution.py:26
  36.9 24.4 %all-to-all-start.2 = ((f32[16,144,128]{2,1,0:T(8,128)}), f32[16,144,128]{2,1,0:T(8,128)S(1)}, u32[]{:S(2)}, u32[]{:S(2)}) async-start(f32[16,144,128]{2,1,0:T(8,128)} %pick.5), calls=%async_computation.2 | async-start | bytes 2359296 | tf_op jit(solution)/shard_map/all_to_all | solution.py:356
  40.6 12.7 %collective-permute-start.2 = (f32[16,80,128]{2,1,0:T(8,128)S(1)}, f32[16,80,128]{2,1,0:T(8,128)}, u32[]{:S(2)}, u32[]{:S(2)}) collective-permute-start(f32[16,80,128]{2,1,0:T(8,128)S(1)} %all_to_all.30.own), channel_id=1, source_target_pairs={{0,16},{16,0},{32,48},{48,32},{64,80},{80,64},{96,112},{112,96},{1... | collective-permute-start | bytes 1966088 | tf_op jit(solution)/shard_map/ppermute | solution.py:363
  52.4 2.9 %collective-permute-start.5 = (f32[16,80,128]{2,1,0:T(8,128)}, f32[16,80,128]{2,1,0:T(8,128)}, u32[]{:S(2)}, u32[]{:S(2)}) collective-permute-start(f32[16,80,128]{2,1,0:T(8,128)} %broadcast_select_fusion), channel_id=1, source_target_pairs={{0,16},{16,0},{32,48},{48,32},{64,80},{80,64},{96,112},{112,96},{1... | collective-permute-start | bytes 1966088 | tf_op jit(solution)/shard_map/ppermute | solution.py:367
  53.3 4.8 %copy-start.14 = (s32[2]{0:T(128)}, s32[2]{0:T(128)S(1)}, u32[]{:S(2)}) copy-start(s32[2]{0:T(128)S(1)} %pad_add_fusion.1.place) | copy-start | bytes 28
  58.1 1.4 copy-start
  61.3 42.3 %all-to-all-start.1 = ((f32[16,288,128]{2,1,0:T(8,128)}), f32[16,288,128]{2,1,0:T(8,128)S(1)}, u32[]{:S(2)}, u32[]{:S(2)}) async-start(f32[16,288,128]{2,1,0:T(8,128)} %copy-done), calls=%async_computation.1 | async-start | bytes 4718592 | tf_op jit(solution)/shard_map/all_to_all | solution.py:356
  67.3 0.8 copy-start.3
  69.4 34.2 %copy-start.10 = (s32[48]{0:T(128)S(1)}, s32[48]{0:T(128)}, u32[]{:S(2)}) copy-start(s32[48]{0:T(128)} %get-tuple-element.20.mode) | copy-start | bytes 580
  105.1 32.9 %copy-start.8 = (s32[2304]{0:T(1024)S(1)}, s32[2304]{0:T(1024)}, u32[]{:S(2)}) copy-start(s32[2304]{0:T(1024)} %copy-done.7) | copy-start | bytes 27652
  131.6 16.2 %collective-permute-start.8 = (f32[16,72,128]{2,1,0:T(8,128)S(1)}, f32[16,72,128]{2,1,0:T(8,128)S(1)}, u32[]{:S(2)}, u32[]{:S(2)}) collective-permute-start(f32[16,72,128]{2,1,0:T(8,128)S(1)} %all_to_all.31.own), channel_id=1, source_target_pairs={{0,32},{16,48},{32,64},{48,80},{64,96},{80,112},{1,33},{17,49},{33... | collective-permute-start | bytes 1769480 | tf_op jit(solution)/shard_map/ppermute | solution.py:26
  136.6 15.3 %collective-permute-start.7 = (f32[16,72,128]{2,1,0:T(8,128)S(1)}, f32[16,72,128]{2,1,0:T(8,128)S(1)}, u32[]{:S(2)}, u32[]{:S(2)}) collective-permute-start(f32[16,72,128]{2,1,0:T(8,128)S(1)} %all_to_all.31.own), channel_id=1, source_target_pairs={{32,0},{48,16},{64,32},{80,48},{96,64},{112,80},{33,1},{49,17},{65... | collective-permute-start | bytes 1769480 | tf_op jit(solution)/shard_map/ppermute | solution.py:26
  140.8 21.3 %all-to-all-start.5 = ((f32[16,144,128]{2,1,0:T(8,128)}), f32[16,144,128]{2,1,0:T(8,128)S(1)}, u32[]{:S(2)}, u32[]{:S(2)}) async-start(f32[16,144,128]{2,1,0:T(8,128)} %pick.7), calls=%async_computation.5 | async-start | bytes 2359296 | tf_op jit(solution)/shard_map/all_to_all | solution.py:356
  144.5 7.6 %collective-permute-start.6 = (f32[16,72,128]{2,1,0:T(8,128)S(1)}, f32[16,72,128]{2,1,0:T(8,128)S(1)}, u32[]{:S(2)}, u32[]{:S(2)}) collective-permute-start(f32[16,72,128]{2,1,0:T(8,128)S(1)} %all_to_all.31.own), channel_id=1, source_target_pairs={{0,16},{16,0},{32,48},{48,32},{64,80},{80,64},{96,112},{112,96},{1... | collective-permute-start | bytes 1769480 | tf_op jit(solution)/shard_map/ppermute | solution.py:363
  152.0 2.1 collective-permute-start.9
  156.9 1.4 copy-start.1
  158.3 7.6 %copy-start.13 = (f32[78]{0:T(128)S(1)}, f32[78]{0:T(128)}, u32[]{:S(2)}) copy-start(f32[78]{0:T(128)} %get-tuple-element.21.scale) | copy-start | bytes 940
  162.1 35.9 %all-to-all-start.4 = ((f32[16,288,128]{2,1,0:T(8,128)}), f32[16,288,128]{2,1,0:T(8,128)S(1)}, u32[]{:S(2)}, u32[]{:S(2)}) async-start(f32[16,288,128]{2,1,0:T(8,128)} %copy-done.1), calls=%async_computation.4 | async-start | bytes 4718592 | tf_op jit(solution)/shard_map/all_to_all | solution.py:356
  165.9 0.8 copy-start.5
  (6 other events, 4.2 us)

commit v3 on v2

--- a/solution.py
+++ b/solution.py
@@ -125,7 +125,7 @@
         in_specs=[pl.BlockSpec(memory_space=pltpu.SMEM)] * len(scalars)
         + [pl.BlockSpec(memory_space=pltpu.VMEM)] * len(blocks),
         out_specs=pl.BlockSpec(memory_space=pltpu.VMEM),
-        out_shape=jax.ShapeDtypeStruct((MEMBERS, kinds * M * PIECE, 128), F32),
+        out_shape=pltpu.HBM((MEMBERS, kinds * M * PIECE, 128), F32),
         compiler_params=pltpu.CompilerParams(vmem_limit_bytes=16 * 1024 * 1024),
         name="pick",
     )(*scalars, *blocks)
@@ -157,23 +157,25 @@
 
 
 def commuted(*terms):
-    lefts, rights, tall, wide = [], [], [], []
+    lefts, tall, wide_high, wide_low, both, highs = [], [], [], [], [], []
     pad = jnp.zeros((CHUNK - N, 2 * CHUNK), BF16)
-    thin = pad[:, :CHUNK]
     for operator, a, b in terms:
         high, low = split(operator)
         lefts += [high, low, high]
-        rights += [high, thin, high, thin, low, thin]
+        both += [jnp.concatenate([high, low], axis=1), pad]
+        highs += [high, pad[:, :CHUNK]]
         high, low = (jnp.concatenate(piece, axis=1) for piece in a)
         tall += [high, pad, high, pad, low, pad]
         high, low = (jnp.concatenate(piece, axis=0) for piece in b)
-        wide += [high, low, high]
-    from_left = jnp.dot(
-        jnp.concatenate(lefts, axis=1), jnp.concatenate(tall, axis=0), preferred_element_type=F32
-    )
-    from_right = jnp.dot(
-        jnp.concatenate(wide, axis=1), jnp.concatenate(rights, axis=0), preferred_element_type=F32
-    )
+        wide_high.append(high)
+        wide_low.append(low)
+
+    def product(left, right):
+        return jnp.dot(jnp.concatenate(left, axis=1), jnp.concatenate(right, axis=0), preferred_element_type=F32)
+
+    from_left = product(lefts, tall)
+    from_right = product(wide_high, both)
+    from_right = from_right[:, :CHUNK] + from_right[:, CHUNK:] + product(wide_low, highs)
     return jnp.concatenate([from_left[:, CHUNK:] - from_right[N:], from_right[:N] - from_left[:, :CHUNK]], axis=0)
 
 
@@ -204,66 +206,76 @@
 
 
 def early_kernel(last, mode, scale, state, near, core, *refs):
-    ops, refs = refs[: 2 * TOGETHER], refs[2 * TOGETHER :]
-    first, first_up, first_down, raw, plain = refs[-5:]
+    ops, refs = refs[: 4 * TOGETHER], refs[4 * TOGETHER :]
+    part, total, raw, plain = refs[-4:]
+    hamiltonian = widened(STEP * core[...])
     for turn in range(TOGETHER):
         m = pl.program_id(0) * TOGETHER + turn
-        above_op, below_op = ops[2 * turn : 2 * turn + 2]
+        up_op, down_op, above_op, below_op = ops[4 * turn : 4 * turn + 4]
         if last:
-            own = state[turn]
+            assembled(state, m * PIECE, raw.at[turn, 0], plain.at[turn, 0])
         else:
-            unpack(state.at[turn], refs[0].at[turn])
-            own = refs[0][turn]
+            unpack(state.at[turn], plain.at[turn, 0])
         for kind in range(2):
-            assembled(near, (kind * M + m) * PIECE, raw.at[turn, kind], plain.at[turn, kind])
-        first[turn] = commuted(plainly(widened(STEP * core[...]), own)) - scale[6 * M + m] * own
-        first_up[turn] = commuted(
-            with_factor(widened(scale[WEIGHT + 4] * above_op[0]), plain[turn, 0], *factor(scale, 1, m))
+            assembled(near, (kind * M + m) * PIECE, raw.at[turn, 1 + kind], plain.at[turn, 1 + kind])
+        own, up_down, down_up = (plain[turn, place] for place in range(3))
+        first = commuted(plainly(hamiltonian, own)) - scale[6 * M + m] * own
+        first_up = commuted(with_factor(widened(scale[WEIGHT + 4] * above_op[0]), up_down, *factor(scale, 1, m)))
+        first_down = commuted(plainly(widened(scale[WEIGHT + 2] * below_op[0]), down_up))
+        part[turn] = second_of(scale, m, hamiltonian, up_op, down_op, first, first_up, first_down)
+        if last:
+            before, before_first = refs[:2]
+            total[turn] = before[turn] + before_first[turn] + 0.5 * own + (1.0 / 6.0) * first
+        else:
+            total[turn] = own + first
+
+
+def second_of(scale, m, hamiltonian, up_op, down_op, first, first_up, first_down):
+    up_op, down_op = widened(scale[WEIGHT] * up_op[0]), widened(scale[WEIGHT + 3] * down_op[0])
+    return (
+        commuted(
+            plainly(hamiltonian, first), plainly(up_op, first_up), with_factor(down_op, first_down, *factor(scale, 0, m))
         )
-        first_down[turn] = commuted(plainly(widened(scale[WEIGHT + 2] * below_op[0]), plain[turn, 1]))
+        - scale[6 * M + m] * first
+    )
 
 
 def late_kernel(last, mode, scale, other, core, *refs):
-    ops, (base, part, part_up, part_down), refs = refs[: 4 * TOGETHER], refs[4 * TOGETHER :][:4], refs[4 * TOGETHER + 4 :]
+    ops, part, refs = refs[: 4 * TOGETHER], refs[4 * TOGETHER], refs[4 * TOGETHER + 1 :]
     if last:
-        result, raw, plain = refs
+        total, result, raw, plain = refs
     else:
-        result, following, total, raw, plain = refs
+        result, kept_first, raw, plain = refs
+    hamiltonian = widened(STEP * core[...])
     for turn in range(TOGETHER):
         m = pl.program_id(0) * TOGETHER + turn
         up_op, down_op, above_op, below_op = ops[4 * turn : 4 * turn + 4]
         for kind in range(4):
             assembled(other, (turn * 4 + kind) * PIECE, raw.at[turn, kind], plain.at[turn, kind])
         up, down, up2, down2 = (plain[turn, kind] for kind in range(4))
-        hamiltonian = widened(STEP * core[...])
-        up_op, down_op = widened(scale[WEIGHT] * up_op[0]), widened(scale[WEIGHT + 3] * down_op[0])
-        own_factor = factor(scale, 0, m)
         up_pieces = halved(up)
-        first = part[turn] + commuted((up_op, up_pieces, up_pieces), with_factor(down_op, down, *own_factor))
+        first = commuted(
+            (widened(scale[WEIGHT] * up_op[0]), up_pieces, up_pieces),
+            with_factor(widened(scale[WEIGHT + 3] * down_op[0]), down, *factor(scale, 0, m)),
+        )
         first_up = (
-            part_up[turn]
-            + commuted((hamiltonian, up_pieces, up_pieces), plainly(widened(scale[WEIGHT + 1] * above_op[0]), up2))
+            commuted((hamiltonian, up_pieces, up_pieces), plainly(widened(scale[WEIGHT + 1] * above_op[0]), up2))
             - scale[7 * M + m] * up
         )
         first_down = (
-            part_down[turn]
-            + commuted(
+            commuted(
                 plainly(hamiltonian, down),
                 with_factor(widened(scale[WEIGHT + 5] * below_op[0]), down2, *factor(scale, 2, m)),
             )
             - scale[8 * M + m] * down
         )
-        second = (
-            commuted(plainly(hamiltonian, first), plainly(up_op, first_up), with_factor(down_op, first_down, *own_factor))
-            - scale[6 * M + m] * first
-        )
+        second = part[turn] + second_of(scale, m, hamiltonian, up_op, down_op, first, first_up, first_down)
         if last:
-            plain[turn, 0] = base[turn] + (1.0 / 6.0) * first + (1.0 / 24.0) * second
+            plain[turn, 0] = total[turn] + (1.0 / 6.0) * first + (1.0 / 24.0) * second
             pack(plain.at[turn, 0], result.at[turn])
         else:
-            following[turn] = second
+            kept_first[turn] = first
             plain[turn, 0] = second
-            total[turn] = base[turn] + first + 0.5 * second
             pack(plain.at[turn, 0], raw.at[turn, 0])
             for member in range(MEMBERS):
                 result[member, pl.ds(m * PIECE, PIECE), :] = raw[turn, 0, member * PIECE : (member + 1) * PIECE, :]
@@ -307,25 +319,27 @@
     return [pltpu.with_memory_space_constraint(value, pltpu.HBM) for value in values]
 
 
-def early(nodes, state, near, operators, last):
+def early(nodes, state, near, operators, sums):
     hamiltonian, coupling = operators
-    specs = [PLAIN if last else WHOLE, all_of(near.shape), all_of(hamiltonian.shape)] + operator_specs(4, 2)
-    outs = 3 if last else 4
-    call = by_matrix(functools.partial(early_kernel, last), "early", specs, [PLAIN] * outs, [SUMS] * outs, 2, 2)
-    return call(*nodes, *kept(state), near, hamiltonian, *kept(*[coupling] * (2 * TOGETHER)))
-
-
-def late(nodes, other, operators, base, parts, last):
+    last = len(sums) > 0
+    specs = [all_of(state.shape) if last else WHOLE, all_of(near.shape), all_of(hamiltonian.shape)]
+    specs += operator_specs(0, 3, 4, 2) + [PLAIN] * len(sums)
+    call = by_matrix(functools.partial(early_kernel, last), "early", specs, [PLAIN] * 2, [SUMS] * 2, 3, 3)
+    return call(*nodes, state, near, *kept(hamiltonian, *[coupling] * (4 * TOGETHER), *sums))
+
+
+def late(nodes, other, operators, part, total):
     hamiltonian, coupling = operators
+    last = total is not None
     specs = [pl.BlockSpec((MEMBERS, TOGETHER * 4 * PIECE, 128), lambda step, mode, scale: (0, step, 0))]
-    specs += [all_of(hamiltonian.shape)] + operator_specs(0, 3, 1, 5) + [PLAIN] * 4
+    specs += [all_of(hamiltonian.shape)] + operator_specs(0, 3, 1, 5) + [PLAIN] * (1 + last)
     if last:
         outs = [WHOLE], [jax.ShapeDtypeStruct((M, ROWS, 128), F32)]
     else:
         blocks = (MEMBERS, M * PIECE, 128)
-        outs = [all_of(blocks), PLAIN, PLAIN], [jax.ShapeDtypeStruct(blocks, F32), SUMS, SUMS]
+        outs = [all_of(blocks), PLAIN], [pltpu.HBM(blocks, F32), SUMS]
     call = by_matrix(functools.partial(late_kernel, last), "late", specs, *outs, 4, 4)
-    return call(*nodes, other, hamiltonian, *kept(*[coupling] * (4 * TOGETHER), base, *parts))
+    return call(*nodes, other, *kept(hamiltonian, *[coupling] * (4 * TOGETHER), part, *[total] * last))
 
 
 def shards(
@@ -358,16 +372,15 @@
     def link_fields(tier_blocks):
         return tier_blocks[:, M * PIECE, :FIELDS].reshape(-1).astype(jnp.int32)
 
-    def two_steps(own, table, state, operators, nodes, before):
-        last = before is not None
+    def two_steps(own, table, state, operators, nodes, sums):
         mate = lax.ppermute(own, "tier", [(source, source ^ 1) for source in range(TIERS)])
         above2, below2 = passed_along(own, -2), passed_along(own, 2)
         near = swapped(picked(pick_near_kernel, 2, [table], [own]))
         cross = jnp.where(tier % 2 == 0, above2, below2)
         cross = lax.ppermute(cross, "tier", [(source, source ^ 1) for source in range(TIERS)])
         other = swapped(picked(pick_other_kernel, 4, [table, place], [mate, cross, above2, below2]))
-        *base, part, part_up, part_down = early(nodes, state, near, operators, last)
-        return late(nodes, other, operators, before if last else base[0], (part, part_up, part_down), last)
+        part, total = early(nodes, state, near, operators, sums)
+        return total, late(nodes, other, operators, part, total if sums else None)
 
     state = density.reshape(M, 2, ROWS // 2, 128).transpose(0, 2, 1, 3).reshape(M, ROWS, 128)
     own = swapped(dealt(state, links))
@@ -376,8 +389,8 @@
     own, table = lax.optimization_barrier((own, table))
     nodes = make_nodes(table, place, corr_real, corr_imag, decay_rate, weight)
     operators = hamiltonian, coupling
-    blocks, state, total = two_steps(own, table, state, operators, nodes, None)
-    (result,) = two_steps(swapped(blocks), table, state, operators, nodes, total)
+    start, (blocks, first) = two_steps(own, table, state, operators, nodes, ())
+    _, (result,) = two_steps(swapped(blocks), table, blocks, operators, nodes, (start, first))
     return result.reshape(M, ROWS // 2, 2, 128).transpose(0, 2, 1, 3).reshape(M, 2, N * N)
 
 

time: 210 us -> 198 us (0.943)
  waiting for transfers between devices: 84.4 us -> 71.9 us
  local copies, waits for them, and re-layouts: 10.6 us -> 6.62 us
  Pallas kernels: 44.9 us -> 48.4 us
    ppermute x6, waiting for transfers between devices: 20.3 us -> 12.2 us  [passed_along(): lax.ppermute(value, 'tier', [(source, source + steps) for source in range...]
    all_to_all x4, waiting for transfers between devices: 60.1 us -> 55.4 us  [swapped(): lax.all_to_all(blocks, 'member', split_axis=0, concat_axis=0, tiled=True)]
    unnamed x32 -> x24, local copies, waits for them, and re-layouts: 9.65 us -> 5.71 us
    ppermute x6, starting transfers between devices: 14.4 us -> 17.7 us  [passed_along(): lax.ppermute(value, 'tier', [(source, source + steps) for source in range...]
    pallas_call x4, Pallas kernels: 10.7 us -> 13.5 us  [picked(): pl.pallas_call(kernel, in_specs=[pl.BlockSpec(memory_space=pltpu.SMEM)] *...]
  transfers between devices with their start and end apart: 14 -> 14, of which waited for: 11 -> 11; matrix products, arithmetic and copies ran while one was open for 1% -> 1% of each run, Pallas kernels for 11% -> 15%
where the time goes in v3:
time: 198 us; the launch traced here: 197 us
  waiting for transfers between devices  71.9 us (36%)
  Pallas kernels  48.4 us (24%)
  blocking collectives  35.3 us (18%)
  starting transfers between devices  32.8 us (17%)
  local copies, waits for them, and re-layouts  6.62 us (3%)
    all_to_all x4, waiting for transfers between devices, swapped(): lax.all_to_all(blocks, 'member', split_axis=0, concat_axis=0, tiled=True)  55.4 us
    all_to_all x2, blocking collectives, swapped(): lax.all_to_all(blocks, 'member', split_axis=0, concat_axis=0, tiled=True)  35.3 us
    pallas_call x2, Pallas kernels, late(): call(*nodes, other, *kept(hamiltonian, *[coupling] * (4 * TOGETHER), part...  18.3 us
    ppermute x6, starting transfers between devices, passed_along(): lax.ppermute(value, 'tier', [(source, source + steps) for source in range...  17.7 us
    pallas_call x2, Pallas kernels, early(): call(*nodes, state, near, *kept(hamiltonian, *[coupling] * (4 * TOGETHER)...  14.9 us
    all_to_all x4, starting transfers between devices, swapped(): lax.all_to_all(blocks, 'member', split_axis=0, concat_axis=0, tiled=True)  14.8 us
    pallas_call x4, Pallas kernels, picked(): pl.pallas_call(kernel, in_specs=[pl.BlockSpec(memory_space=pltpu.SMEM)] *...  13.5 us
    ppermute x6, waiting for transfers between devices, passed_along(): lax.ppermute(value, 'tier', [(source, source + steps) for source in range...  12.2 us
  transfers between devices with their start and end apart: 14, of which 11 were waited for; matrix products, arithmetic and copies ran while one was open for 1% of the time, Pallas kernels for 15%

profile of v3, /device:TPU:0, one launch (start us, length us, event | category | flops | bytes accessed | tf_op | source)
XLA Modules:
  0.0 197.1 jit_solution(6429309989971401714)
XLA Ops:
  2.0 19.9 %all_to_all.30.own = f32[16,80,128]{2,1,0:T(8,128)S(1)} all-to-all(f32[16,80,128]{2,1,0:T(8,128)S(1)} %deal.1), channel_id=1, replica_groups=mesh['tier'=8,'member'=16] {'member'}, dimensions={0} | all-to-all | bytes 1310720 | tf_op jit(solution)/shard_map/all_to_all | solution.py:370
  23.2 3.0 %collective-permute-start.1 = (s32[768]{0:T(1024)S(1)}, s32[768]{0:T(1024)S(1)}, u32[]{:S(2)}, u32[]{:S(2)}) collective-permute-start(s32[768]{0:T(1024)S(1)} %convert_element_type.28), channel_id=1, source_target_pairs={{0,16},{16,32},{32,48},{48,64},{64,80},{80,96},{96,112},{1,17},{17... | collective-permute-start | bytes 9224 | tf_op jit(solution)/shard_map/ppermute | solution.py:26
  28.4 6.2 %collective-permute-start.4 = (f32[16,80,128]{2,1,0:T(8,128)S(1)}, f32[16,80,128]{2,1,0:T(8,128)S(1)}, u32[]{:S(2)}, u32[]{:S(2)}) collective-permute-start(f32[16,80,128]{2,1,0:T(8,128)S(1)} %all_to_all.30.own), channel_id=1, source_target_pairs={{0,32},{16,48},{32,64},{48,80},{64,96},{80,112},{1,33},{17,49},{33... | collective-permute-start | bytes 1966088 | tf_op jit(solution)/shard_map/ppermute | solution.py:26
  34.6 2.9 %pick.5 = f32[16,144,128]{2,1,0:T(8,128)} custom-call(s32[2304]{0:T(1024)S(1)} %pad_add_fusion.table, f32[16,80,128]{2,1,0:T(8,128)S(1)} %all_to_all.30.own), custom_call_target="tpu_custom_call" | custom-call | tf_op jit(solution)/shard_map/pick/pallas_call | solution.py:123
  37.5 3.7 %all-to-all-start.2 = ((f32[16,144,128]{2,1,0:T(8,128)}), f32[16,144,128]{2,1,0:T(8,128)S(1)}, u32[]{:S(2)}, u32[]{:S(2)}) async-start(f32[16,144,128]{2,1,0:T(8,128)} %pick.5), calls=%async_computation.2 | async-start | bytes 2359296 | tf_op jit(solution)/shard_map/all_to_all | solution.py:370
  41.3 6.0 %collective-permute-done.3.above2 = f32[16,80,128]{2,1,0:T(8,128)S(1)} collective-permute-done((f32[16,80,128]{2,1,0:T(8,128)S(1)}, f32[16,80,128]{2,1,0:T(8,128)S(1)}, u32[]{:S(2)}, u32[]{:S(2)}) %collective-permute-start.3) | collective-permute-done | bytes 655392 | tf_op jit(solution)/shard_map/ppermute | solution.py:26
  49.5 2.4 %collective-permute-done.5.cross = f32[16,80,128]{2,1,0:T(8,128)} collective-permute-done((f32[16,80,128]{2,1,0:T(8,128)}, f32[16,80,128]{2,1,0:T(8,128)}, u32[]{:S(2)}, u32[]{:S(2)}) %collective-permute-start.5) | collective-permute-done | bytes 655392 | tf_op jit(solution)/shard_map/ppermute | solution.py:380
  51.8 4.2 %pick.4 = f32[16,288,128]{2,1,0:T(8,128)} custom-call(s32[2304]{0:T(1024)S(1)} %pad_add_fusion.table, s32[2]{0:T(128)S(1)} %pad_add_fusion.1.place, f32[16,80,128]{2,1,0:T(8,128)} %collective-permute-done.2.mate, f32[16,80,128]{2,1,0:T(8,128)} %collective-permute-done.5.cross, f32[16,80,128]{2,1,0:T(8,128)S(1)} %collective-permute-done.3.above2, ...), custom_call_target="tpu_custom_call" | custom-call | tf_op jit(solution)/shard_map/pick/pallas_call | solution.py:123
  56.0 4.3 %all-to-all-done.2.near = f32[16,144,128]{2,1,0:T(8,128)S(1)} async-done(((f32[16,144,128]{2,1,0:T(8,128)}), f32[16,144,128]{2,1,0:T(8,128)S(1)}, u32[]{:S(2)}, u32[]{:S(2)}) %all-to-all-start.2) | async-done | bytes 1179680 | tf_op jit(solution)/shard_map/all_to_all | solution.py:370
  60.3 3.7 %all-to-all-start.1 = ((f32[16,288,128]{2,1,0:T(8,128)}), f32[16,288,128]{2,1,0:T(8,128)S(1)}, u32[]{:S(2)}, u32[]{:S(2)}) async-start(f32[16,288,128]{2,1,0:T(8,128)} %pick.4), calls=%async_computation.1 | async-start | bytes 4718592 | tf_op jit(solution)/shard_map/all_to_all | solution.py:370
  68.6 7.3 %early.2 = (f32[8,192,128]{2,1,0:T(8,128)}, f32[8,192,128]{2,1,0:T(8,128)}) custom-call(s32[48]{0:T(128)S(1)} %copy-done.5, f32[78]{0:T(128)S(1)} %copy-done.7, f32[8,144,128]{2,1,0:T(8,128)S(1)} %bitcast.21, f32[16,144,128]{2,1,0:T(8,128)S(1)} %all-to-all-done.2.near, f32[96,96]{1,0:T(8,128)} %core.7, f32[96,96,96]{2,1,0:T(8,128)} %refs_7_.7, ...), custom_call_target="tpu_custom_call" | custom-call | tf_op jit(solution)/shard_map/early/pallas_call | solution.py:328
  75.9 21.9 %all-to-all-done.1.other = f32[16,288,128]{2,1,0:T(8,128)S(1)} async-done(((f32[16,288,128]{2,1,0:T(8,128)}), f32[16,288,128]{2,1,0:T(8,128)S(1)}, u32[]{:S(2)}, u32[]{:S(2)}) %all-to-all-start.1) | async-done | bytes 2359328 | tf_op jit(solution)/shard_map/all_to_all | solution.py:370
  98.4 9.2 %late.2 = (f32[16,72,128]{2,1,0:T(8,128)}, f32[8,192,128]{2,1,0:T(8,128)}) custom-call(s32[48]{0:T(128)S(1)} %copy-done.6, f32[78]{0:T(128)S(1)} %copy-done.8, f32[16,288,128]{2,1,0:T(8,128)S(1)} %all-to-all-done.1.other, f32[96,96]{1,0:T(8,128)} %core.7, f32[96,96,96]{2,1,0:T(8,128)} %refs_7_.7, f32[96,96,96]{2,1,0:T(8,128)} %refs_7_.7, ...), custom_call_target="tpu_custom_call" | custom-call | tf_op jit(solution)/shard_map/late/pallas_call | solution.py:342
  107.6 15.5 %all_to_all.31.own = f32[16,72,128]{2,1,0:T(8,128)S(1)} all-to-all(f32[16,72,128]{2,1,0:T(8,128)} %get-tuple-element.20.state), channel_id=1, replica_groups=mesh['tier'=8,'member'=16] {'member'}, dimensions={0} | all-to-all | bytes 1179648 | tf_op jit(solution)/shard_map/all_to_all | solution.py:370
  124.4 4.6 %collective-permute-start.8 = (f32[16,72,128]{2,1,0:T(8,128)S(1)}, f32[16,72,128]{2,1,0:T(8,128)S(1)}, u32[]{:S(2)}, u32[]{:S(2)}) collective-permute-start(f32[16,72,128]{2,1,0:T(8,128)S(1)} %all_to_all.31.own), channel_id=1, source_target_pairs={{0,32},{16,48},{32,64},{48,80},{64,96},{80,112},{1,33},{17,49},{33... | collective-permute-start | bytes 1769480 | tf_op jit(solution)/shard_map/ppermute | solution.py:26
  129.0 2.9 %pick.7 = f32[16,144,128]{2,1,0:T(8,128)} custom-call(s32[2304]{0:T(1024)S(1)} %copy-done.4, f32[16,72,128]{2,1,0:T(8,128)S(1)} %all_to_all.31.own), custom_call_target="tpu_custom_call" | custom-call | tf_op jit(solution)/shard_map/pick/pallas_call | solution.py:123
  131.9 3.7 %all-to-all-start.5 = ((f32[16,144,128]{2,1,0:T(8,128)}), f32[16,144,128]{2,1,0:T(8,128)S(1)}, u32[]{:S(2)}, u32[]{:S(2)}) async-start(f32[16,144,128]{2,1,0:T(8,128)} %pick.7), calls=%async_computation.5 | async-start | bytes 2359296 | tf_op jit(solution)/shard_map/all_to_all | solution.py:370
  135.7 3.0 %collective-permute-done.7.above2 = f32[16,72,128]{2,1,0:T(8,128)S(1)} collective-permute-done((f32[16,72,128]{2,1,0:T(8,128)S(1)}, f32[16,72,128]{2,1,0:T(8,128)S(1)}, u32[]{:S(2)}, u32[]{:S(2)}) %collective-permute-start.7) | collective-permute-done | bytes 589856 | tf_op jit(solution)/shard_map/ppermute | solution.py:26
  142.7 3.6 %pick.6 = f32[16,288,128]{2,1,0:T(8,128)} custom-call(s32[2304]{0:T(1024)S(1)} %copy-done.4, s32[2]{0:T(128)S(1)} %copy-done.11, f32[16,72,128]{2,1,0:T(8,128)S(1)} %collective-permute-done.6.mate, f32[16,72,128]{2,1,0:T(8,128)S(1)} %collective-permute-done.9.cross, f32[16,72,128]{2,1,0:T(8,128)S(1)} %collective-permute-done.7.above2, ...), custom_call_target="tpu_custom_call" | custom-call | tf_op jit(solution)/shard_map/pick/pallas_call | solution.py:123
  146.3 6.8 %all-to-all-done.5.near = f32[16,144,128]{2,1,0:T(8,128)S(1)} async-done(((f32[16,144,128]{2,1,0:T(8,128)}), f32[16,144,128]{2,1,0:T(8,128)S(1)}, u32[]{:S(2)}, u32[]{:S(2)}) %all-to-all-start.5) | async-done | bytes 1179680 | tf_op jit(solution)/shard_map/all_to_all | solution.py:370
  153.0 3.7 %all-to-all-start.4 = ((f32[16,288,128]{2,1,0:T(8,128)}), f32[16,288,128]{2,1,0:T(8,128)S(1)}, u32[]{:S(2)}, u32[]{:S(2)}) async-start(f32[16,288,128]{2,1,0:T(8,128)} %pick.6), calls=%async_computation.4 | async-start | bytes 4718592 | tf_op jit(solution)/shard_map/all_to_all | solution.py:370
  157.8 7.6 %early.3 = (f32[8,192,128]{2,1,0:T(8,128)}, f32[8,192,128]{2,1,0:T(8,128)}) custom-call(s32[48]{0:T(128)S(1)} %copy-done.6, f32[78]{0:T(128)S(1)} %copy-done.9, f32[16,72,128]{2,1,0:T(8,128)S(1)} %copy-done.2, f32[16,144,128]{2,1,0:T(8,128)S(1)} %all-to-all-done.5.near, f32[96,96]{1,0:T(8,128)} %core.7, f32[96,96,96]{2,1,0:T(8,128)} %refs_7_.7, ...), custom_call_target="tpu_custom_call" | custom-call | tf_op jit(solution)/shard_map/early/pallas_call | solution.py:328
  165.4 22.6 %all-to-all-done.4.other = f32[16,288,128]{2,1,0:T(8,128)S(1)} async-done(((f32[16,288,128]{2,1,0:T(8,128)}), f32[16,288,128]{2,1,0:T(8,128)S(1)}, u32[]{:S(2)}, u32[]{:S(2)}) %all-to-all-start.4) | async-done | bytes 2359328 | tf_op jit(solution)/shard_map/all_to_all | solution.py:370
  188.0 9.1 %late.3 = f32[8,144,128]{2,1,0:T(8,128)} custom-call(s32[48]{0:T(128)S(1)} %copy-done.6, f32[78]{0:T(128)S(1)} %copy-done.9, f32[16,288,128]{2,1,0:T(8,128)S(1)} %all-to-all-done.4.other, f32[96,96]{1,0:T(8,128)} %core.7, f32[96,96,96]{2,1,0:T(8,128)} %refs_7_.7, f32[96,96,96]{2,1,0:T(8,128)} %refs_7_.7, f32[96,96,96]{2,1,0:T(8,128)} %refs_7_.7, ...), custom_call_target="tpu_custom_call" | custom-call | tf_op jit(solution)/shard_map/late/pallas_call | solution.py:342
  (53 shorter events, 19.4 us)
Async XLA Ops:
  0.8 1.1 copy-start
  22.0 4.3 %collective-permute-start = (s32[768]{0:T(1024)S(1)}, s32[768]{0:T(1024)S(1)}, u32[]{:S(2)}, u32[]{:S(2)}) collective-permute-start(s32[768]{0:T(1024)S(1)} %convert_element_type.28), channel_id=1, source_target_pairs={{16,0},{32,16},{48,32},{64,48},{80,64},{96,80},{112,96},{17,1},{33... | collective-permute-start | bytes 9224 | tf_op jit(solution)/shard_map/ppermute | solution.py:26
  23.2 3.8 %collective-permute-start.1 = (s32[768]{0:T(1024)S(1)}, s32[768]{0:T(1024)S(1)}, u32[]{:S(2)}, u32[]{:S(2)}) collective-permute-start(s32[768]{0:T(1024)S(1)} %convert_element_type.28), channel_id=1, source_target_pairs={{0,16},{16,32},{32,48},{48,64},{64,80},{80,96},{96,112},{1,17},{17... | collective-permute-start | bytes 9224 | tf_op jit(solution)/shard_map/ppermute | solution.py:26
  27.1 24.7 %copy-start.3 = (s32[2304]{0:T(1024)}, s32[2304]{0:T(1024)S(1)}, u32[]{:S(2)}) copy-start(s32[2304]{0:T(1024)S(1)} %pad_add_fusion.table) | copy-start | bytes 27652
  27.1 20.2 %collective-permute-start.3 = (f32[16,80,128]{2,1,0:T(8,128)S(1)}, f32[16,80,128]{2,1,0:T(8,128)S(1)}, u32[]{:S(2)}, u32[]{:S(2)}) collective-permute-start(f32[16,80,128]{2,1,0:T(8,128)S(1)} %all_to_all.30.own), channel_id=1, source_target_pairs={{32,0},{48,16},{64,32},{80,48},{96,64},{112,80},{33,1},{49,17},{65... | collective-permute-start | bytes 1966088 | tf_op jit(solution)/shard_map/ppermute | solution.py:26
  28.4 20.1 %collective-permute-start.4 = (f32[16,80,128]{2,1,0:T(8,128)S(1)}, f32[16,80,128]{2,1,0:T(8,128)S(1)}, u32[]{:S(2)}, u32[]{:S(2)}) collective-permute-start(f32[16,80,128]{2,1,0:T(8,128)S(1)} %all_to_all.30.own), channel_id=1, source_target_pairs={{0,32},{16,48},{32,64},{48,80},{64,96},{80,112},{1,33},{17,49},{33... | collective-permute-start | bytes 1966088 | tf_op jit(solution)/shard_map/ppermute | solution.py:26
  37.5 22.8 %all-to-all-start.2 = ((f32[16,144,128]{2,1,0:T(8,128)}), f32[16,144,128]{2,1,0:T(8,128)S(1)}, u32[]{:S(2)}, u32[]{:S(2)}) async-start(f32[16,144,128]{2,1,0:T(8,128)} %pick.5), calls=%async_computation.2 | async-start | bytes 2359296 | tf_op jit(solution)/shard_map/all_to_all | solution.py:370
  41.2 8.3 %collective-permute-start.2 = (f32[16,80,128]{2,1,0:T(8,128)S(1)}, f32[16,80,128]{2,1,0:T(8,128)}, u32[]{:S(2)}, u32[]{:S(2)}) collective-permute-start(f32[16,80,128]{2,1,0:T(8,128)S(1)} %all_to_all.30.own), channel_id=1, source_target_pairs={{0,16},{16,0},{32,48},{48,32},{64,80},{80,64},{96,112},{112,96},{1... | collective-permute-start | bytes 1966088 | tf_op jit(solution)/shard_map/ppermute | solution.py:376
  49.4 2.4 %collective-permute-start.5 = (f32[16,80,128]{2,1,0:T(8,128)}, f32[16,80,128]{2,1,0:T(8,128)}, u32[]{:S(2)}, u32[]{:S(2)}) collective-permute-start(f32[16,80,128]{2,1,0:T(8,128)} %broadcast_select_fusion), channel_id=1, source_target_pairs={{0,16},{16,0},{32,48},{48,32},{64,80},{80,64},{96,112},{112,96},{1... | collective-permute-start | bytes 1966088 | tf_op jit(solution)/shard_map/ppermute | solution.py:380
  49.5 6.5 %copy-start.10 = (s32[2]{0:T(128)}, s32[2]{0:T(128)S(1)}, u32[]{:S(2)}) copy-start(s32[2]{0:T(128)S(1)} %pad_add_fusion.1.place) | copy-start | bytes 28
  60.3 37.5 %all-to-all-start.1 = ((f32[16,288,128]{2,1,0:T(8,128)}), f32[16,288,128]{2,1,0:T(8,128)S(1)}, u32[]{:S(2)}, u32[]{:S(2)}) async-start(f32[16,288,128]{2,1,0:T(8,128)} %pick.4), calls=%async_computation.1 | async-start | bytes 4718592 | tf_op jit(solution)/shard_map/all_to_all | solution.py:370
  66.3 1.1 copy-start.1
  67.4 0.6 copy-start.5
  68.6 29.2 %copy-start.6 = (s32[48]{0:T(128)S(1)}, s32[48]{0:T(128)}, u32[]{:S(2)}) copy-start(s32[48]{0:T(128)} %get-tuple-element.16.mode) | copy-start | bytes 580
  98.4 30.6 %copy-start.4 = (s32[2304]{0:T(1024)S(1)}, s32[2304]{0:T(1024)}, u32[]{:S(2)}) copy-start(s32[2304]{0:T(1024)} %copy-done.3) | copy-start | bytes 27652
  123.1 15.6 %collective-permute-start.7 = (f32[16,72,128]{2,1,0:T(8,128)S(1)}, f32[16,72,128]{2,1,0:T(8,128)S(1)}, u32[]{:S(2)}, u32[]{:S(2)}) collective-permute-start(f32[16,72,128]{2,1,0:T(8,128)S(1)} %all_to_all.31.own), channel_id=1, source_target_pairs={{32,0},{48,16},{64,32},{80,48},{96,64},{112,80},{33,1},{49,17},{65... | collective-permute-start | bytes 1769480 | tf_op jit(solution)/shard_map/ppermute | solution.py:26
  124.4 15.5 %collective-permute-start.8 = (f32[16,72,128]{2,1,0:T(8,128)S(1)}, f32[16,72,128]{2,1,0:T(8,128)S(1)}, u32[]{:S(2)}, u32[]{:S(2)}) collective-permute-start(f32[16,72,128]{2,1,0:T(8,128)S(1)} %all_to_all.31.own), channel_id=1, source_target_pairs={{0,32},{16,48},{32,64},{48,80},{64,96},{80,112},{1,33},{17,49},{33... | collective-permute-start | bytes 1769480 | tf_op jit(solution)/shard_map/ppermute | solution.py:26
  131.9 21.1 %all-to-all-start.5 = ((f32[16,144,128]{2,1,0:T(8,128)}), f32[16,144,128]{2,1,0:T(8,128)S(1)}, u32[]{:S(2)}, u32[]{:S(2)}) async-start(f32[16,144,128]{2,1,0:T(8,128)} %pick.7), calls=%async_computation.5 | async-start | bytes 2359296 | tf_op jit(solution)/shard_map/all_to_all | solution.py:370
  135.6 4.4 %collective-permute-start.6 = (f32[16,72,128]{2,1,0:T(8,128)S(1)}, f32[16,72,128]{2,1,0:T(8,128)S(1)}, u32[]{:S(2)}, u32[]{:S(2)}) collective-permute-start(f32[16,72,128]{2,1,0:T(8,128)S(1)} %all_to_all.31.own), channel_id=1, source_target_pairs={{0,16},{16,0},{32,48},{48,32},{64,80},{80,64},{96,112},{112,96},{1... | collective-permute-start | bytes 1769480 | tf_op jit(solution)/shard_map/ppermute | solution.py:376
  139.9 2.1 %collective-permute-start.9 = (f32[16,72,128]{2,1,0:T(8,128)S(1)}, f32[16,72,128]{2,1,0:T(8,128)S(1)}, u32[]{:S(2)}, u32[]{:S(2)}) collective-permute-start(f32[16,72,128]{2,1,0:T(8,128)S(1)} %broadcast_select_fusion.1), channel_id=1, source_target_pairs={{0,16},{16,0},{32,48},{48,32},{64,80},{80,64},{96,112},{112,96},{1... | collective-permute-start | bytes 1769480 | tf_op jit(solution)/shard_map/ppermute | solution.py:380
  142.0 0.7 copy-start.11
  146.3 10.5 %copy-start.9 = (f32[78]{0:T(128)S(1)}, f32[78]{0:T(128)}, u32[]{:S(2)}) copy-start(f32[78]{0:T(128)} %get-tuple-element.17.scale) | copy-start | bytes 940
  153.0 34.9 %all-to-all-start.4 = ((f32[16,288,128]{2,1,0:T(8,128)}), f32[16,288,128]{2,1,0:T(8,128)S(1)}, u32[]{:S(2)}, u32[]{:S(2)}) async-start(f32[16,288,128]{2,1,0:T(8,128)} %pick.6), calls=%async_computation.4 | async-start | bytes 4718592 | tf_op jit(solution)/shard_map/all_to_all | solution.py:370
  156.8 1.1 copy-start.2
  (2 other events, 1.2 us)

commit v4 on v3

--- a/solution.py
+++ b/solution.py
@@ -30,7 +30,7 @@
     return table[(level * MEMBERS + member) * FIELDS + field * M + slot]
 
 
-def nodes_kernel(table, place, corr_real, corr_imag, decay, weight, mode, scale):
+def nodes_kernel(table, place, corr_real, corr_imag, decay, weight, mode, scale, lists):
     tier, member = place[0], place[1]
     level = tier.astype(F32)
 
@@ -56,14 +56,28 @@
     for kind in range(6):
         scale[WEIGHT + kind] = weight[kind]
 
+    def note(member, carry):
+        for m in range(M):
+            for kind in range(2):
+                for far in range(3):
+                    who, slot = chased(table, member, m, kind, far)
+                    lists[(member * M + m) * 6 + kind * 3 + far] = who * M + slot
+        return carry
+
+    lax.fori_loop(0, MEMBERS, note, 0)
+
 
 def make_nodes(table, place, corr_real, corr_imag, decay, weight):
     smem = pl.BlockSpec(memory_space=pltpu.SMEM)
     return pl.pallas_call(
         nodes_kernel,
         in_specs=[smem] * 6,
-        out_specs=[smem, smem],
-        out_shape=[jax.ShapeDtypeStruct((6 * M,), jnp.int32), jax.ShapeDtypeStruct((WEIGHT + 6,), F32)],
+        out_specs=[smem] * 3,
+        out_shape=[
+            jax.ShapeDtypeStruct((6 * M,), jnp.int32),
+            jax.ShapeDtypeStruct((WEIGHT + 6,), F32),
+            jax.ShapeDtypeStruct((MEMBERS * M * 6,), jnp.int32),
+        ],
         name="nodes",
     )(table, place, corr_real, corr_imag, decay, weight)
 
@@ -89,43 +103,68 @@
     )(state, links)
 
 
-def pick_near_kernel(table, own, out):
+def chased(table, member, m, kind, far):
+    first = 3 * kind
+    who, slot = entry(table, 0, member, first, m), entry(table, 0, member, first + 1, m)
+    if far:
+        then = first if far == 1 else 3 - first
+        who, slot = (entry(table, kind + 1, who, then + field, slot) for field in range(2))
+    return who, slot
+
+
+def listed(lists, member, m, kind, far):
+    place = lists[(member * M + m) * 6 + kind * 3 + far]
+    return lax.shift_right_logical(place, 3), jnp.bitwise_and(place, M - 1)
+
+
+def sent_out(held, out, done, member):
+    return pltpu.make_async_copy(held.at[member], out.at[member], done.at[member])
+
+
+def pick_near_kernel(find, links, own, out, held, done):
     def one(member, carry):
         for m in range(M):
-            for kind, first in ((0, 0), (1, 3)):
-                who, slot = entry(table, 0, member, first, m), entry(table, 0, member, first + 1, m)
-                who, slot = (entry(table, kind + 1, who, 3 - first + field, slot) for field in range(2))
+            for kind in range(2):
+                who, slot = find(links, member, m, kind, 2)
                 row = (kind * M + m) * PIECE
-                out[member, row : row + PIECE, :] = own[who, pl.ds(slot * PIECE, PIECE), :]
+                held[member, row : row + PIECE, :] = own[who, pl.ds(slot * PIECE, PIECE), :]
+        sent_out(held, out, done, member).start()
         return carry
 
     lax.fori_loop(0, MEMBERS, one, 0)
-
-
-def pick_other_kernel(table, place, mate, cross, above2, below2, out):
+    for member in range(MEMBERS):
+        sent_out(held, out, done, member).wait()
+
+
+def pick_other_kernel(find, links, place, mate, cross, above2, below2, out, held, done):
     def one(above, below, member, carry):
         for m in range(M):
-            for kind, source, source2, first in ((0, above, above2, 0), (1, below, below2, 3)):
-                who, slot = entry(table, 0, member, first, m), entry(table, 0, member, first + 1, m)
+            for kind, source, source2 in ((0, above, above2), (1, below, below2)):
+                who, slot = find(links, member, m, kind, 0)
                 row = (m * 4 + kind) * PIECE
-                out[member, row : row + PIECE, :] = source[who, pl.ds(slot * PIECE, PIECE), :]
-                who, slot = (entry(table, kind + 1, who, first + field, slot) for field in range(2))
+                held[member, row : row + PIECE, :] = source[who, pl.ds(slot * PIECE, PIECE), :]
+                who, slot = find(links, member, m, kind, 1)
                 row += 2 * PIECE
-                out[member, row : row + PIECE, :] = source2[who, pl.ds(slot * PIECE, PIECE), :]
+                held[member, row : row + PIECE, :] = source2[who, pl.ds(slot * PIECE, PIECE), :]
+        sent_out(held, out, done, member).start()
         return carry
 
     lower_core = jnp.bitwise_and(place[0], 1) == 0
     pl.when(lower_core)(lambda: lax.fori_loop(0, MEMBERS, functools.partial(one, mate, cross), None))
     pl.when(jnp.logical_not(lower_core))(lambda: lax.fori_loop(0, MEMBERS, functools.partial(one, cross, mate), None))
+    for member in range(MEMBERS):
+        sent_out(held, out, done, member).wait()
 
 
 def picked(kernel, kinds, scalars, blocks):
+    shape = (MEMBERS, kinds * M * PIECE, 128)
     return pl.pallas_call(
         kernel,
         in_specs=[pl.BlockSpec(memory_space=pltpu.SMEM)] * len(scalars)
         + [pl.BlockSpec(memory_space=pltpu.VMEM)] * len(blocks),
-        out_specs=pl.BlockSpec(memory_space=pltpu.VMEM),
-        out_shape=pltpu.HBM((MEMBERS, kinds * M * PIECE, 128), F32),
+        out_specs=pl.BlockSpec(memory_space=pl.ANY),
+        out_shape=pltpu.HBM(shape, F32),
+        scratch_shapes=[pltpu.VMEM(shape, F32), pltpu.SemaphoreType.DMA((MEMBERS,))],
         compiler_params=pltpu.CompilerParams(vmem_limit_bytes=16 * 1024 * 1024),
         name="pick",
     )(*scalars, *blocks)
@@ -160,7 +199,7 @@
     lefts, tall, wide_high, wide_low, both, highs = [], [], [], [], [], []
     pad = jnp.zeros((CHUNK - N, 2 * CHUNK), BF16)
     for operator, a, b in terms:
-        high, low = split(operator)
+        high, low = operator[0], operator[1]
         lefts += [high, low, high]
         both += [jnp.concatenate([high, low], axis=1), pad]
         highs += [high, pad[:, :CHUNK]]
@@ -179,10 +218,6 @@
     return jnp.concatenate([from_left[:, CHUNK:] - from_right[N:], from_right[:N] - from_left[:, :CHUNK]], axis=0)
 
 
-def widened(operator):
-    return jnp.concatenate([operator, jnp.zeros((N, CHUNK - N), F32)], axis=1)
-
-
 def plainly(operator, value):
     pieces = halved(value)
     return operator, pieces, pieces
@@ -201,14 +236,42 @@
     unpack(raw, target)
 
 
+def operators_kernel(mode, scale, hamiltonian, coupling, out, held, done):
+    copies = [pltpu.make_async_copy(coupling.at[mode[at]], held.at[at], done.at[at]) for at in range(6 * M)]
+    for copy in copies:
+        copy.start()
+
+    def keep(at, operator):
+        operator = jnp.concatenate([operator, jnp.zeros((N, CHUNK - N), F32)], axis=1)
+        out[at, 0], out[at, 1] = split(operator)
+
+    keep(6 * M, STEP * hamiltonian[...])
+    for at, copy in enumerate(copies):
+        copy.wait()
+        keep(at, scale[WEIGHT + at // M] * held[at])
+
+
+def make_operators(mode, scale, hamiltonian, coupling):
+    smem, vmem = pl.BlockSpec(memory_space=pltpu.SMEM), pl.BlockSpec(memory_space=pltpu.VMEM)
+    return pl.pallas_call(
+        operators_kernel,
+        in_specs=[smem, smem, vmem, pl.BlockSpec(memory_space=pl.ANY)],
+        out_specs=vmem,
+        out_shape=pltpu.HBM((6 * M + 1, 2, N, CHUNK), BF16),
+        scratch_shapes=[pltpu.VMEM((6 * M, N, N), F32), pltpu.SemaphoreType.DMA((6 * M,))],
+        compiler_params=pltpu.CompilerParams(vmem_limit_bytes=16 * 1024 * 1024),
+        name="operators",
+    )(mode, scale, hamiltonian, coupling)
+
+
 def factor(scale, kind, m):
     return scale[kind * M + m], scale[3 * M + kind * M + m]
 
 
-def early_kernel(last, mode, scale, state, near, core, *refs):
+def early_kernel(last, scale, state, near, core, *refs):
     ops, refs = refs[: 4 * TOGETHER], refs[4 * TOGETHER :]
     part, total, raw, plain = refs[-4:]
-    hamiltonian = widened(STEP * core[...])
+    hamiltonian = core[0]
     for turn in range(TOGETHER):
         m = pl.program_id(0) * TOGETHER + turn
         up_op, down_op, above_op, below_op = ops[4 * turn : 4 * turn + 4]
@@ -220,8 +283,8 @@
             assembled(near, (kind * M + m) * PIECE, raw.at[turn, 1 + kind], plain.at[turn, 1 + kind])
         own, up_down, down_up = (plain[turn, place] for place in range(3))
         first = commuted(plainly(hamiltonian, own)) - scale[6 * M + m] * own
-        first_up = commuted(with_factor(widened(scale[WEIGHT + 4] * above_op[0]), up_down, *factor(scale, 1, m)))
-        first_down = commuted(plainly(widened(scale[WEIGHT + 2] * below_op[0]), down_up))
+        first_up = commuted(with_factor(above_op[0], up_down, *factor(scale, 1, m)))
+        first_down = commuted(plainly(below_op[0], down_up))
         part[turn] = second_of(scale, m, hamiltonian, up_op, down_op, first, first_up, first_down)
         if last:
             before, before_first = refs[:2]
@@ -231,22 +294,23 @@
 
 
 def second_of(scale, m, hamiltonian, up_op, down_op, first, first_up, first_down):
-    up_op, down_op = widened(scale[WEIGHT] * up_op[0]), widened(scale[WEIGHT + 3] * down_op[0])
     return (
         commuted(
-            plainly(hamiltonian, first), plainly(up_op, first_up), with_factor(down_op, first_down, *factor(scale, 0, m))
+            plainly(hamiltonian, first),
+            plainly(up_op[0], first_up),
+            with_factor(down_op[0], first_down, *factor(scale, 0, m)),
         )
         - scale[6 * M + m] * first
     )
 
 
-def late_kernel(last, mode, scale, other, core, *refs):
+def late_kernel(last, scale, other, core, *refs):
     ops, part, refs = refs[: 4 * TOGETHER], refs[4 * TOGETHER], refs[4 * TOGETHER + 1 :]
     if last:
         total, result, raw, plain = refs
     else:
         result, kept_first, raw, plain = refs
-    hamiltonian = widened(STEP * core[...])
+    hamiltonian = core[0]
     for turn in range(TOGETHER):
         m = pl.program_id(0) * TOGETHER + turn
         up_op, down_op, above_op, below_op = ops[4 * turn : 4 * turn + 4]
@@ -255,17 +319,17 @@
         up, down, up2, down2 = (plain[turn, kind] for kind in range(4))
         up_pieces = halved(up)
         first = commuted(
-            (widened(scale[WEIGHT] * up_op[0]), up_pieces, up_pieces),
-            with_factor(widened(scale[WEIGHT + 3] * down_op[0]), down, *factor(scale, 0, m)),
+            (up_op[0], up_pieces, up_pieces),
+            with_factor(down_op[0], down, *factor(scale, 0, m)),
         )
         first_up = (
-            commuted((hamiltonian, up_pieces, up_pieces), plainly(widened(scale[WEIGHT + 1] * above_op[0]), up2))
+            commuted((hamiltonian, up_pieces, up_pieces), plainly(above_op[0], up2))
             - scale[7 * M + m] * up
         )
         first_down = (
             commuted(
                 plainly(hamiltonian, down),
-                with_factor(widened(scale[WEIGHT + 5] * below_op[0]), down2, *factor(scale, 2, m)),
+                with_factor(below_op[0], down2, *factor(scale, 2, m)),
             )
             - scale[8 * M + m] * down
         )
@@ -282,18 +346,18 @@
 
 
 TOGETHER = 2
-PLAIN = pl.BlockSpec((TOGETHER, 2 * N, 128), lambda step, mode, scale: (step, 0, 0))
-WHOLE = pl.BlockSpec((TOGETHER, ROWS, 128), lambda step, mode, scale: (step, 0, 0))
+PLAIN = pl.BlockSpec((TOGETHER, 2 * N, 128), lambda step, scale: (step, 0, 0))
+WHOLE = pl.BlockSpec((TOGETHER, ROWS, 128), lambda step, scale: (step, 0, 0))
 SUMS = pltpu.HBM((M, 2 * N, 128), F32)
 
 
 def all_of(shape):
-    return pl.BlockSpec(shape, lambda step, mode, scale: (0,) * len(shape))
+    return pl.BlockSpec(shape, lambda step, scale: (0,) * len(shape))
 
 
 def operator_specs(*lists):
     return [
-        pl.BlockSpec((1, N, N), lambda step, mode, scale, at=at * M + turn: (mode[step * TOGETHER + at], 0, 0))
+        pl.BlockSpec((1, 2, N, CHUNK), lambda step, scale, at=at * M + turn: (step * TOGETHER + at, 0, 0, 0))
         for turn in range(TOGETHER)
         for at in lists
     ]
@@ -303,7 +367,7 @@
     return pl.pallas_call(
         kernel,
         grid_spec=pltpu.PrefetchScalarGridSpec(
-            num_scalar_prefetch=2,
+            num_scalar_prefetch=1,
             grid=(M // TOGETHER,),
             in_specs=in_specs,
             out_specs=out_specs,
@@ -315,31 +379,32 @@
     )
 
 
+HAMILTONIAN = pl.BlockSpec((1, 2, N, CHUNK), lambda step, scale: (6 * M, 0, 0, 0))
+
+
 def kept(*values):
     return [pltpu.with_memory_space_constraint(value, pltpu.HBM) for value in values]
 
 
-def early(nodes, state, near, operators, sums):
-    hamiltonian, coupling = operators
+def early(scale, state, near, operators, sums):
     last = len(sums) > 0
-    specs = [all_of(state.shape) if last else WHOLE, all_of(near.shape), all_of(hamiltonian.shape)]
+    specs = [all_of(state.shape) if last else WHOLE, all_of(near.shape), HAMILTONIAN]
     specs += operator_specs(0, 3, 4, 2) + [PLAIN] * len(sums)
     call = by_matrix(functools.partial(early_kernel, last), "early", specs, [PLAIN] * 2, [SUMS] * 2, 3, 3)
-    return call(*nodes, state, near, *kept(hamiltonian, *[coupling] * (4 * TOGETHER), *sums))
-
-
-def late(nodes, other, operators, part, total):
-    hamiltonian, coupling = operators
+    return call(scale, state, near, *kept(*[operators] * (4 * TOGETHER + 1), *sums))
+
+
+def late(scale, other, operators, part, total):
     last = total is not None
-    specs = [pl.BlockSpec((MEMBERS, TOGETHER * 4 * PIECE, 128), lambda step, mode, scale: (0, step, 0))]
-    specs += [all_of(hamiltonian.shape)] + operator_specs(0, 3, 1, 5) + [PLAIN] * (1 + last)
+    specs = [pl.BlockSpec((MEMBERS, TOGETHER * 4 * PIECE, 128), lambda step, scale: (0, step, 0))]
+    specs += [HAMILTONIAN] + operator_specs(0, 3, 1, 5) + [PLAIN] * (1 + last)
     if last:
         outs = [WHOLE], [jax.ShapeDtypeStruct((M, ROWS, 128), F32)]
     else:
         blocks = (MEMBERS, M * PIECE, 128)
         outs = [all_of(blocks), PLAIN], [pltpu.HBM(blocks, F32), SUMS]
     call = by_matrix(functools.partial(late_kernel, last), "late", specs, *outs, 4, 4)
-    return call(*nodes, other, *kept(hamiltonian, *[coupling] * (4 * TOGETHER), part, *[total] * last))
+    return call(scale, other, *kept(*[operators] * (4 * TOGETHER + 1), part, *[total] * last))
 
 
 def shards(
@@ -372,25 +437,25 @@
     def link_fields(tier_blocks):
         return tier_blocks[:, M * PIECE, :FIELDS].reshape(-1).astype(jnp.int32)
 
-    def two_steps(own, table, state, operators, nodes, sums):
+    def two_steps(own, find, links, state, operators, scale, sums):
         mate = lax.ppermute(own, "tier", [(source, source ^ 1) for source in range(TIERS)])
         above2, below2 = passed_along(own, -2), passed_along(own, 2)
-        near = swapped(picked(pick_near_kernel, 2, [table], [own]))
+        near = swapped(picked(functools.partial(pick_near_kernel, find), 2, [links], [own]))
         cross = jnp.where(tier % 2 == 0, above2, below2)
         cross = lax.ppermute(cross, "tier", [(source, source ^ 1) for source in range(TIERS)])
-        other = swapped(picked(pick_other_kernel, 4, [table, place], [mate, cross, above2, below2]))
-        part, total = early(nodes, state, near, operators, sums)
-        return total, late(nodes, other, operators, part, total if sums else None)
+        other = swapped(picked(functools.partial(pick_other_kernel, find), 4, [links, place], [mate, cross, above2, below2]))
+        part, total = early(scale, state, near, operators, sums)
+        return total, late(scale, other, operators, part, total if sums else None)
 
     state = density.reshape(M, 2, ROWS // 2, 128).transpose(0, 2, 1, 3).reshape(M, ROWS, 128)
     own = swapped(dealt(state, links))
     table = link_fields(own)
     table = jnp.concatenate([table, passed_along(table, -1), passed_along(table, 1)])
     own, table = lax.optimization_barrier((own, table))
-    nodes = make_nodes(table, place, corr_real, corr_imag, decay_rate, weight)
-    operators = hamiltonian, coupling
-    start, (blocks, first) = two_steps(own, table, state, operators, nodes, ())
-    _, (result,) = two_steps(swapped(blocks), table, blocks, operators, nodes, (start, first))
+    mode, scale, lists = make_nodes(table, place, corr_real, corr_imag, decay_rate, weight)
+    operators = make_operators(mode, scale, hamiltonian, coupling)
+    start, (blocks, first) = two_steps(own, chased, table, state, operators, scale, ())
+    _, (result,) = two_steps(swapped(blocks), listed, lists, blocks, operators, scale, (start, first))
     return result.reshape(M, ROWS // 2, 2, 128).transpose(0, 2, 1, 3).reshape(M, 2, N * N)
 
 

time: 198 us -> 196 us (0.990)
  waiting for transfers between devices: 71.9 us -> 63 us
  Pallas kernels: 48.4 us -> 54.7 us
    all_to_all x4, waiting for transfers between devices: 55.4 us -> 45.6 us  [swapped(): lax.all_to_all(blocks, 'member', split_axis=0, concat_axis=0, tiled=True)]
    pallas_call x5 -> x6, Pallas kernels: 34.8 us -> 43.5 us  [the longest x2 18.2 us: late(): call(scale, other, *kept(*[operators] * (4 * TOGETHER + 1), part, *[total...]
    pallas_call x4, Pallas kernels: 13.5 us -> 11.1 us  [picked(): pl.pallas_call(kernel, in_specs=[pl.BlockSpec(memory_space=pltpu.SMEM)] *...]
  transfers between devices with their start and end apart: 14 -> 14, of which waited for: 11 -> 11; matrix products, arithmetic and copies ran while one was open for 1% -> 1% of each run, Pallas kernels for 15% -> 19%
where the time goes in v4:
time: 196 us; the launch traced here: 195 us
  waiting for transfers between devices  63 us (32%)
  Pallas kernels  54.7 us (28%)
  blocking collectives  35.3 us (18%)
  starting transfers between devices  32.8 us (17%)
  local copies, waits for them, and re-layouts  7.47 us (4%)
    all_to_all x4, waiting for transfers between devices, swapped(): lax.all_to_all(blocks, 'member', split_axis=0, concat_axis=0, tiled=True)  45.6 us
    all_to_all x2, blocking collectives, swapped(): lax.all_to_all(blocks, 'member', split_axis=0, concat_axis=0, tiled=True)  35.3 us
    pallas_call x2, Pallas kernels, late(): call(scale, other, *kept(*[operators] * (4 * TOGETHER + 1), part, *[total...  18.2 us
    ppermute x6, starting transfers between devices, passed_along(): lax.ppermute(value, 'tier', [(source, source + steps) for source in range...  17.7 us
    all_to_all x4, starting transfers between devices, swapped(): lax.all_to_all(blocks, 'member', split_axis=0, concat_axis=0, tiled=True)  14.9 us
    pallas_call x2, Pallas kernels, early(): call(scale, state, near, *kept(*[operators] * (4 * TOGETHER + 1), *sums))  14.7 us
    ppermute x6, waiting for transfers between devices, passed_along(): lax.ppermute(value, 'tier', [(source, source + steps) for source in range...  13.1 us
    pallas_call x4, Pallas kernels, picked(): pl.pallas_call(kernel, in_specs=[pl.BlockSpec(memory_space=pltpu.SMEM)] *...  11.1 us
  transfers between devices with their start and end apart: 14, of which 11 were waited for; matrix products, arithmetic and copies ran while one was open for 1% of the time, Pallas kernels for 19%

profile of v4, /device:TPU:0, one launch (start us, length us, event | category | flops | bytes accessed | tf_op | source)
XLA Modules:
  0.0 195.4 jit_solution(4941601826880100306)
XLA Ops:
  2.0 19.9 %all_to_all.30.own = f32[16,80,128]{2,1,0:T(8,128)S(1)} all-to-all(f32[16,80,128]{2,1,0:T(8,128)S(1)} %deal.1), channel_id=1, replica_groups=mesh['tier'=8,'member'=16] {'member'}, dimensions={0} | all-to-all | bytes 1310720 | tf_op jit(solution)/shard_map/all_to_all | solution.py:435
  23.2 3.0 %collective-permute-start.1 = (s32[768]{0:T(1024)S(1)}, s32[768]{0:T(1024)S(1)}, u32[]{:S(2)}, u32[]{:S(2)}) collective-permute-start(s32[768]{0:T(1024)S(1)} %convert_element_type.28), channel_id=1, source_target_pairs={{0,16},{16,32},{32,48},{48,64},{64,80},{80,96},{96,112},{1,17},{17... | collective-permute-start | bytes 9224 | tf_op jit(solution)/shard_map/ppermute | solution.py:26
  28.4 6.2 %collective-permute-start.4 = (f32[16,80,128]{2,1,0:T(8,128)S(1)}, f32[16,80,128]{2,1,0:T(8,128)S(1)}, u32[]{:S(2)}, u32[]{:S(2)}) collective-permute-start(f32[16,80,128]{2,1,0:T(8,128)S(1)} %all_to_all.30.own), channel_id=1, source_target_pairs={{0,32},{16,48},{32,64},{48,80},{64,96},{80,112},{1,33},{17,49},{33... | collective-permute-start | bytes 1966088 | tf_op jit(solution)/shard_map/ppermute | solution.py:26
  34.6 2.6 %pick.5 = f32[16,144,128]{2,1,0:T(8,128)} custom-call(s32[2304]{0:T(1024)S(1)} %pad_add_fusion.table.links, f32[16,80,128]{2,1,0:T(8,128)S(1)} %all_to_all.30.own), custom_call_target="tpu_custom_call" | custom-call | tf_op jit(solution)/shard_map/pick/pallas_call | solution.py:161
  37.2 3.7 %all-to-all-start.2 = ((f32[16,144,128]{2,1,0:T(8,128)}), f32[16,144,128]{2,1,0:T(8,128)S(1)}, u32[]{:S(2)}, u32[]{:S(2)}) async-start(f32[16,144,128]{2,1,0:T(8,128)} %pick.5), calls=%async_computation.2 | async-start | bytes 2359296 | tf_op jit(solution)/shard_map/all_to_all | solution.py:435
  41.1 6.2 %collective-permute-done.3.above2 = f32[16,80,128]{2,1,0:T(8,128)S(1)} collective-permute-done((f32[16,80,128]{2,1,0:T(8,128)S(1)}, f32[16,80,128]{2,1,0:T(8,128)S(1)}, u32[]{:S(2)}, u32[]{:S(2)}) %collective-permute-start.3) | collective-permute-done | bytes 655392 | tf_op jit(solution)/shard_map/ppermute | solution.py:26
  51.8 3.7 %pick.4 = f32[16,288,128]{2,1,0:T(8,128)} custom-call(s32[2304]{0:T(1024)S(1)} %pad_add_fusion.table.links, s32[2]{0:T(128)S(1)} %pad_add_fusion.1.place, f32[16,80,128]{2,1,0:T(8,128)} %collective-permute-done.2.mate, f32[16,80,128]{2,1,0:T(8,128)} %collective-permute-done.5.cross, f32[16,80,128]{2,1,0:T(8,128)S(1)} %collective-permute-done.3.above2, ...), custom_call_target="tpu_custom_call" | custom-call | tf_op jit(solution)/shard_map/pick/pallas_call | solution.py:161
  55.6 4.5 %all-to-all-done.2.near = f32[16,144,128]{2,1,0:T(8,128)S(1)} async-done(((f32[16,144,128]{2,1,0:T(8,128)}), f32[16,144,128]{2,1,0:T(8,128)S(1)}, u32[]{:S(2)}, u32[]{:S(2)}) %all-to-all-start.2) | async-done | bytes 1179680 | tf_op jit(solution)/shard_map/all_to_all | solution.py:435
  60.1 3.7 %all-to-all-start.1 = ((f32[16,288,128]{2,1,0:T(8,128)}), f32[16,288,128]{2,1,0:T(8,128)S(1)}, u32[]{:S(2)}, u32[]{:S(2)}) async-start(f32[16,288,128]{2,1,0:T(8,128)} %pick.4), calls=%async_computation.1 | async-start | bytes 4718592 | tf_op jit(solution)/shard_map/all_to_all | solution.py:435
  64.5 4.2 %nodes.1 = (s32[48]{0:T(128)}, f32[78]{0:T(128)}, s32[768]{0:T(1024)}) custom-call(s32[2304]{0:T(1024)} %copy-done.4, s32[2]{0:T(128)} %copy-done.9, f32[96]{0:T(128)} %corr_real.1, f32[96]{0:T(128)} %corr_imag.1, f32[96]{0:T(128)} %decay.1, f32[6]{0:T(128)} %maximum_multiply_fusion.weight), custom_call_target="tpu_custom_call" | custom-call | tf_op jit(solution)/shard_map/nodes/pallas_call | solution.py:72
  73.2 6.3 %operators.1.core.refs_0_.refs_1_.refs_2_.refs_3_.refs_4_.refs_5_.refs_6_.refs_7_ = bf16[49,2,96,128]{3,2,1,0:T(8,128)(2,1)} custom-call(s32[48]{0:T(128)S(1)} %copy-done.11, f32[78]{0:T(128)S(1)} %copy-done.7, f32[96,96]{1,0:T(8,128)S(1)} %copy-done.5, f32[96,96,96]{2,1,0:T(8,128)S(1)} %copy-done), custom_call_target="tpu_custom_call" | custom-call | tf_op jit(solution)/shard_map/operators/pallas_call | solution.py:256
  79.5 7.2 %early.2 = (f32[8,192,128]{2,1,0:T(8,128)}, f32[8,192,128]{2,1,0:T(8,128)}) custom-call(f32[78]{0:T(128)S(1)} %copy-done.8, f32[8,144,128]{2,1,0:T(8,128)S(1)} %bitcast.21, f32[16,144,128]{2,1,0:T(8,128)S(1)} %all-to-all-done.2.near, bf16[49,2,96,128]{3,2,1,0:T(8,128)(2,1)} %operators.1.core.refs_0_.refs_1_.refs_2_.refs_3_.refs_4_.refs_5_.refs_6_.refs_7_, ...), custom_call_target="tpu_custom_call" | custom-call | tf_op jit(solution)/shard_map/early/pallas_call | solution.py:394
  86.8 10.8 %all-to-all-done.1.other = f32[16,288,128]{2,1,0:T(8,128)S(1)} async-done(((f32[16,288,128]{2,1,0:T(8,128)}), f32[16,288,128]{2,1,0:T(8,128)S(1)}, u32[]{:S(2)}, u32[]{:S(2)}) %all-to-all-start.1) | async-done | bytes 2359328 | tf_op jit(solution)/shard_map/all_to_all | solution.py:435
  97.6 9.2 %late.2 = (f32[16,72,128]{2,1,0:T(8,128)}, f32[8,192,128]{2,1,0:T(8,128)}) custom-call(f32[78]{0:T(128)S(1)} %copy-done.8, f32[16,288,128]{2,1,0:T(8,128)S(1)} %all-to-all-done.1.other, bf16[49,2,96,128]{3,2,1,0:T(8,128)(2,1)} %operators.1.core.refs_0_.refs_1_.refs_2_.refs_3_.refs_4_.refs_5_.refs_6_.refs_7_, ...), custom_call_target="tpu_custom_call" | custom-call | tf_op jit(solution)/shard_map/late/pallas_call | solution.py:407
  106.8 15.5 %all_to_all.31.own = f32[16,72,128]{2,1,0:T(8,128)S(1)} all-to-all(f32[16,72,128]{2,1,0:T(8,128)} %get-tuple-element.22.state), channel_id=1, replica_groups=mesh['tier'=8,'member'=16] {'member'}, dimensions={0} | all-to-all | bytes 1179648 | tf_op jit(solution)/shard_map/all_to_all | solution.py:435
  123.6 4.6 %collective-permute-start.8 = (f32[16,72,128]{2,1,0:T(8,128)S(1)}, f32[16,72,128]{2,1,0:T(8,128)S(1)}, u32[]{:S(2)}, u32[]{:S(2)}) collective-permute-start(f32[16,72,128]{2,1,0:T(8,128)S(1)} %all_to_all.31.own), channel_id=1, source_target_pairs={{0,32},{16,48},{32,64},{48,80},{64,96},{80,112},{1,33},{17,49},{33... | collective-permute-start | bytes 1769480 | tf_op jit(solution)/shard_map/ppermute | solution.py:26
  130.2 3.7 %all-to-all-start.5 = ((f32[16,144,128]{2,1,0:T(8,128)}), f32[16,144,128]{2,1,0:T(8,128)S(1)}, u32[]{:S(2)}, u32[]{:S(2)}) async-start(f32[16,144,128]{2,1,0:T(8,128)} %pick.7), calls=%async_computation.5 | async-start | bytes 2359296 | tf_op jit(solution)/shard_map/all_to_all | solution.py:435
  134.1 3.8 %collective-permute-done.7.above2 = f32[16,72,128]{2,1,0:T(8,128)S(1)} collective-permute-done((f32[16,72,128]{2,1,0:T(8,128)S(1)}, f32[16,72,128]{2,1,0:T(8,128)S(1)}, u32[]{:S(2)}, u32[]{:S(2)}) %collective-permute-start.7) | collective-permute-done | bytes 589856 | tf_op jit(solution)/shard_map/ppermute | solution.py:26
  141.2 2.7 %pick.6 = f32[16,288,128]{2,1,0:T(8,128)} custom-call(s32[768]{0:T(1024)S(1)} %copy-done.6, s32[2]{0:T(128)S(1)} %copy-done.10, f32[16,72,128]{2,1,0:T(8,128)S(1)} %collective-permute-done.6.mate, f32[16,72,128]{2,1,0:T(8,128)S(1)} %collective-permute-done.9.cross, f32[16,72,128]{2,1,0:T(8,128)S(1)} %collective-permute-done.7.above2, ...), custom_call_target="tpu_custom_call" | custom-call | tf_op jit(solution)/shard_map/pick/pallas_call | solution.py:161
  143.8 7.5 %all-to-all-done.5.near = f32[16,144,128]{2,1,0:T(8,128)S(1)} async-done(((f32[16,144,128]{2,1,0:T(8,128)}), f32[16,144,128]{2,1,0:T(8,128)S(1)}, u32[]{:S(2)}, u32[]{:S(2)}) %all-to-all-start.5) | async-done | bytes 1179680 | tf_op jit(solution)/shard_map/all_to_all | solution.py:435
  151.4 3.7 %all-to-all-start.4 = ((f32[16,288,128]{2,1,0:T(8,128)}), f32[16,288,128]{2,1,0:T(8,128)S(1)}, u32[]{:S(2)}, u32[]{:S(2)}) async-start(f32[16,288,128]{2,1,0:T(8,128)} %pick.6), calls=%async_computation.4 | async-start | bytes 4718592 | tf_op jit(solution)/shard_map/all_to_all | solution.py:435
  156.2 7.5 %early.3 = (f32[8,192,128]{2,1,0:T(8,128)}, f32[8,192,128]{2,1,0:T(8,128)}) custom-call(f32[78]{0:T(128)S(1)} %copy-done.8, f32[16,72,128]{2,1,0:T(8,128)S(1)} %copy-done.3, f32[16,144,128]{2,1,0:T(8,128)S(1)} %all-to-all-done.5.near, bf16[49,2,96,128]{3,2,1,0:T(8,128)(2,1)} %operators.1.core.refs_0_.refs_1_.refs_2_.refs_3_.refs_4_.refs_5_.refs_6_.refs_7_, ...), custom_call_target="tpu_custom_call" | custom-call | tf_op jit(solution)/shard_map/early/pallas_call | solution.py:394
  163.6 22.7 %all-to-all-done.4.other = f32[16,288,128]{2,1,0:T(8,128)S(1)} async-done(((f32[16,288,128]{2,1,0:T(8,128)}), f32[16,288,128]{2,1,0:T(8,128)S(1)}, u32[]{:S(2)}, u32[]{:S(2)}) %all-to-all-start.4) | async-done | bytes 2359328 | tf_op jit(solution)/shard_map/all_to_all | solution.py:435
  186.3 9.1 %late.3 = f32[8,144,128]{2,1,0:T(8,128)} custom-call(f32[78]{0:T(128)S(1)} %copy-done.8, f32[16,288,128]{2,1,0:T(8,128)S(1)} %all-to-all-done.4.other, bf16[49,2,96,128]{3,2,1,0:T(8,128)(2,1)} %operators.1.core.refs_0_.refs_1_.refs_2_.refs_3_.refs_4_.refs_5_.refs_6_.refs_7_, ...), custom_call_target="tpu_custom_call" | custom-call | tf_op jit(solution)/shard_map/late/pallas_call | solution.py:407
  (54 shorter events, 23.0 us)
Async XLA Ops:
  0.8 1.1 copy-start.1
  22.0 4.3 %collective-permute-start = (s32[768]{0:T(1024)S(1)}, s32[768]{0:T(1024)S(1)}, u32[]{:S(2)}, u32[]{:S(2)}) collective-permute-start(s32[768]{0:T(1024)S(1)} %convert_element_type.28), channel_id=1, source_target_pairs={{16,0},{32,16},{48,32},{64,48},{80,64},{96,80},{112,96},{17,1},{33... | collective-permute-start | bytes 9224 | tf_op jit(solution)/shard_map/ppermute | solution.py:26
  23.2 3.8 %collective-permute-start.1 = (s32[768]{0:T(1024)S(1)}, s32[768]{0:T(1024)S(1)}, u32[]{:S(2)}, u32[]{:S(2)}) collective-permute-start(s32[768]{0:T(1024)S(1)} %convert_element_type.28), channel_id=1, source_target_pairs={{0,16},{16,32},{32,48},{48,64},{64,80},{80,96},{96,112},{1,17},{17... | collective-permute-start | bytes 9224 | tf_op jit(solution)/shard_map/ppermute | solution.py:26
  27.1 24.7 %copy-start.4 = (s32[2304]{0:T(1024)}, s32[2304]{0:T(1024)S(1)}, u32[]{:S(2)}) copy-start(s32[2304]{0:T(1024)S(1)} %pad_add_fusion.table.links) | copy-start | bytes 27652
  27.1 20.2 %collective-permute-start.3 = (f32[16,80,128]{2,1,0:T(8,128)S(1)}, f32[16,80,128]{2,1,0:T(8,128)S(1)}, u32[]{:S(2)}, u32[]{:S(2)}) collective-permute-start(f32[16,80,128]{2,1,0:T(8,128)S(1)} %all_to_all.30.own), channel_id=1, source_target_pairs={{32,0},{48,16},{64,32},{80,48},{96,64},{112,80},{33,1},{49,17},{65... | collective-permute-start | bytes 1966088 | tf_op jit(solution)/shard_map/ppermute | solution.py:26
  28.4 20.1 %collective-permute-start.4 = (f32[16,80,128]{2,1,0:T(8,128)S(1)}, f32[16,80,128]{2,1,0:T(8,128)S(1)}, u32[]{:S(2)}, u32[]{:S(2)}) collective-permute-start(f32[16,80,128]{2,1,0:T(8,128)S(1)} %all_to_all.30.own), channel_id=1, source_target_pairs={{0,32},{16,48},{32,64},{48,80},{64,96},{80,112},{1,33},{17,49},{33... | collective-permute-start | bytes 1966088 | tf_op jit(solution)/shard_map/ppermute | solution.py:26
  37.2 22.8 %all-to-all-start.2 = ((f32[16,144,128]{2,1,0:T(8,128)}), f32[16,144,128]{2,1,0:T(8,128)S(1)}, u32[]{:S(2)}, u32[]{:S(2)}) async-start(f32[16,144,128]{2,1,0:T(8,128)} %pick.5), calls=%async_computation.2 | async-start | bytes 2359296 | tf_op jit(solution)/shard_map/all_to_all | solution.py:435
  41.0 8.5 %collective-permute-start.2 = (f32[16,80,128]{2,1,0:T(8,128)S(1)}, f32[16,80,128]{2,1,0:T(8,128)}, u32[]{:S(2)}, u32[]{:S(2)}) collective-permute-start(f32[16,80,128]{2,1,0:T(8,128)S(1)} %all_to_all.30.own), channel_id=1, source_target_pairs={{0,16},{16,0},{32,48},{48,32},{64,80},{80,64},{96,112},{112,96},{1... | collective-permute-start | bytes 1966088 | tf_op jit(solution)/shard_map/ppermute | solution.py:441
  49.4 2.4 %collective-permute-start.5 = (f32[16,80,128]{2,1,0:T(8,128)}, f32[16,80,128]{2,1,0:T(8,128)}, u32[]{:S(2)}, u32[]{:S(2)}) collective-permute-start(f32[16,80,128]{2,1,0:T(8,128)} %broadcast_select_fusion), channel_id=1, source_target_pairs={{0,16},{16,0},{32,48},{48,32},{64,80},{80,64},{96,112},{112,96},{1... | collective-permute-start | bytes 1966088 | tf_op jit(solution)/shard_map/ppermute | solution.py:445
  49.4 6.1 %copy-start.9 = (s32[2]{0:T(128)}, s32[2]{0:T(128)S(1)}, u32[]{:S(2)}) copy-start(s32[2]{0:T(128)S(1)} %pad_add_fusion.1.place) | copy-start | bytes 28
  60.1 37.5 %all-to-all-start.1 = ((f32[16,288,128]{2,1,0:T(8,128)}), f32[16,288,128]{2,1,0:T(8,128)S(1)}, u32[]{:S(2)}, u32[]{:S(2)}) async-start(f32[16,288,128]{2,1,0:T(8,128)} %pick.4), calls=%async_computation.1 | async-start | bytes 4718592 | tf_op jit(solution)/shard_map/all_to_all | solution.py:435
  68.7 2.3 %copy-start = (f32[96,96,96]{2,1,0:T(8,128)S(1)}, f32[96,96,96]{2,1,0:T(8,128)}, u32[]{:S(2)}) copy-start(f32[96,96,96]{2,1,0:T(8,128)} %coupling.1) | copy-start | bytes 10616836
  71.1 0.8 copy-start.5
  73.2 6.3 %copy-start.2 = (f32[8,2,9216]{2,1,0:T(2,128)S(1)}, f32[8,2,9216]{2,1,0:T(2,128)}, u32[]{:S(2)}) copy-start(f32[8,2,9216]{2,1,0:T(2,128)} %param.12) | copy-start | bytes 1769476
  73.2 6.4 %copy-start.8 = (f32[78]{0:T(128)S(1)}, f32[78]{0:T(128)}, u32[]{:S(2)}) copy-start(f32[78]{0:T(128)} %get-tuple-element.17.scale) | copy-start | bytes 940
  97.6 30.5 %copy-start.6 = (s32[768]{0:T(1024)S(1)}, s32[768]{0:T(1024)}, u32[]{:S(2)}) copy-start(s32[768]{0:T(1024)} %get-tuple-element.18.links) | copy-start | bytes 9220
  122.3 15.6 %collective-permute-start.7 = (f32[16,72,128]{2,1,0:T(8,128)S(1)}, f32[16,72,128]{2,1,0:T(8,128)S(1)}, u32[]{:S(2)}, u32[]{:S(2)}) collective-permute-start(f32[16,72,128]{2,1,0:T(8,128)S(1)} %all_to_all.31.own), channel_id=1, source_target_pairs={{32,0},{48,16},{64,32},{80,48},{96,64},{112,80},{33,1},{49,17},{65... | collective-permute-start | bytes 1769480 | tf_op jit(solution)/shard_map/ppermute | solution.py:26
  123.6 15.5 %collective-permute-start.8 = (f32[16,72,128]{2,1,0:T(8,128)S(1)}, f32[16,72,128]{2,1,0:T(8,128)S(1)}, u32[]{:S(2)}, u32[]{:S(2)}) collective-permute-start(f32[16,72,128]{2,1,0:T(8,128)S(1)} %all_to_all.31.own), channel_id=1, source_target_pairs={{0,32},{16,48},{32,64},{48,80},{64,96},{80,112},{1,33},{17,49},{33... | collective-permute-start | bytes 1769480 | tf_op jit(solution)/shard_map/ppermute | solution.py:26
  130.2 10.9 %copy-start.10 = (s32[2]{0:T(128)S(1)}, s32[2]{0:T(128)}, u32[]{:S(2)}) copy-start(s32[2]{0:T(128)} %copy-done.9) | copy-start | bytes 28
  130.2 21.1 %all-to-all-start.5 = ((f32[16,144,128]{2,1,0:T(8,128)}), f32[16,144,128]{2,1,0:T(8,128)S(1)}, u32[]{:S(2)}, u32[]{:S(2)}) async-start(f32[16,144,128]{2,1,0:T(8,128)} %pick.7), calls=%async_computation.5 | async-start | bytes 2359296 | tf_op jit(solution)/shard_map/all_to_all | solution.py:435
  134.0 5.2 %collective-permute-start.6 = (f32[16,72,128]{2,1,0:T(8,128)S(1)}, f32[16,72,128]{2,1,0:T(8,128)S(1)}, u32[]{:S(2)}, u32[]{:S(2)}) collective-permute-start(f32[16,72,128]{2,1,0:T(8,128)S(1)} %all_to_all.31.own), channel_id=1, source_target_pairs={{0,16},{16,0},{32,48},{48,32},{64,80},{80,64},{96,112},{112,96},{1... | collective-permute-start | bytes 1769480 | tf_op jit(solution)/shard_map/ppermute | solution.py:441
  139.1 2.1 %collective-permute-start.9 = (f32[16,72,128]{2,1,0:T(8,128)S(1)}, f32[16,72,128]{2,1,0:T(8,128)S(1)}, u32[]{:S(2)}, u32[]{:S(2)}) collective-permute-start(f32[16,72,128]{2,1,0:T(8,128)S(1)} %broadcast_select_fusion.1), channel_id=1, source_target_pairs={{0,16},{16,0},{32,48},{48,32},{64,80},{80,64},{96,112},{112,96},{1... | collective-permute-start | bytes 1769480 | tf_op jit(solution)/shard_map/ppermute | solution.py:445
  151.4 34.9 %all-to-all-start.4 = ((f32[16,288,128]{2,1,0:T(8,128)}), f32[16,288,128]{2,1,0:T(8,128)S(1)}, u32[]{:S(2)}, u32[]{:S(2)}) async-start(f32[16,288,128]{2,1,0:T(8,128)} %pick.6), calls=%async_computation.4 | async-start | bytes 4718592 | tf_op jit(solution)/shard_map/all_to_all | solution.py:435
  155.1 1.1 copy-start.3
  (2 other events, 1.3 us)

commit v5 on v4

--- a/solution.py
+++ b/solution.py
@@ -278,10 +278,11 @@
         if last:
             assembled(state, m * PIECE, raw.at[turn, 0], plain.at[turn, 0])
         else:
-            unpack(state.at[turn], plain.at[turn, 0])
+            raw[turn, 0, 0:ROWS, :] = state[turn]
+            unpack(raw.at[turn, 0], plain.at[turn, 0])
         for kind in range(2):
             assembled(near, (kind * M + m) * PIECE, raw.at[turn, 1 + kind], plain.at[turn, 1 + kind])
-        own, up_down, down_up = (plain[turn, place] for place in range(3))
+        own, up_down, down_up = (plain[turn, place, 0 : 2 * N, :] for place in range(3))
         first = commuted(plainly(hamiltonian, own)) - scale[6 * M + m] * own
         first_up = commuted(with_factor(above_op[0], up_down, *factor(scale, 1, m)))
         first_down = commuted(plainly(below_op[0], down_up))
@@ -316,7 +317,7 @@
         up_op, down_op, above_op, below_op = ops[4 * turn : 4 * turn + 4]
         for kind in range(4):
             assembled(other, (turn * 4 + kind) * PIECE, raw.at[turn, kind], plain.at[turn, kind])
-        up, down, up2, down2 = (plain[turn, kind] for kind in range(4))
+        up, down, up2, down2 = (plain[turn, kind, 0 : 2 * N, :] for kind in range(4))
         up_pieces = halved(up)
         first = commuted(
             (up_op[0], up_pieces, up_pieces),
@@ -335,11 +336,12 @@
         )
         second = part[turn] + second_of(scale, m, hamiltonian, up_op, down_op, first, first_up, first_down)
         if last:
-            plain[turn, 0] = total[turn] + (1.0 / 6.0) * first + (1.0 / 24.0) * second
-            pack(plain.at[turn, 0], result.at[turn])
+            plain[turn, 0, 0 : 2 * N, :] = total[turn] + (1.0 / 6.0) * first + (1.0 / 24.0) * second
+            pack(plain.at[turn, 0], raw.at[turn, 0])
+            result[turn] = raw[turn, 0, 0:ROWS, :]
         else:
             kept_first[turn] = first
-            plain[turn, 0] = second
+            plain[turn, 0, 0 : 2 * N, :] = second
             pack(plain.at[turn, 0], raw.at[turn, 0])
             for member in range(MEMBERS):
                 result[member, pl.ds(m * PIECE, PIECE), :] = raw[turn, 0, member * PIECE : (member + 1) * PIECE, :]
@@ -371,7 +373,7 @@
             grid=(M // TOGETHER,),
             in_specs=in_specs,
             out_specs=out_specs,
-            scratch_shapes=[pltpu.VMEM((TOGETHER, raws, ROWS, 128), F32), pltpu.VMEM((TOGETHER, plains, 2 * N, 128), F32)],
+            scratch_shapes=[pltpu.VMEM((TOGETHER, raws, ROWS + 8, 128), F32), pltpu.VMEM((TOGETHER, plains, 2 * N + 8, 128), F32)],
         ),
         out_shape=out_shape,
         compiler_params=pltpu.CompilerParams(vmem_limit_bytes=32 * 1024 * 1024),

time: 196 us -> 197 us (level)
  no operation moved by 1% of the time
where the time goes in v5:
time: 197 us; the launch traced here: 195 us
  waiting for transfers between devices  63 us (32%)
  Pallas kernels  54.8 us (28%)
  blocking collectives  35.3 us (18%)
  starting transfers between devices  32.8 us (17%)
  local copies, waits for them, and re-layouts  7.47 us (4%)
    all_to_all x4, waiting for transfers between devices, swapped(): lax.all_to_all(blocks, 'member', split_axis=0, concat_axis=0, tiled=True)  45.5 us
    all_to_all x2, blocking collectives, swapped(): lax.all_to_all(blocks, 'member', split_axis=0, concat_axis=0, tiled=True)  35.3 us
    pallas_call x2, Pallas kernels, late(): call(scale, other, *kept(*[operators] * (4 * TOGETHER + 1), part, *[total...  18.3 us
    ppermute x6, starting transfers between devices, passed_along(): lax.ppermute(value, 'tier', [(source, source + steps) for source in range...  17.7 us
    all_to_all x4, starting transfers between devices, swapped(): lax.all_to_all(blocks, 'member', split_axis=0, concat_axis=0, tiled=True)  14.9 us
    pallas_call x2, Pallas kernels, early(): call(scale, state, near, *kept(*[operators] * (4 * TOGETHER + 1), *sums))  14.7 us
    ppermute x6, waiting for transfers between devices, passed_along(): lax.ppermute(value, 'tier', [(source, source + steps) for source in range...  13.1 us
    pallas_call x4, Pallas kernels, picked(): pl.pallas_call(kernel, in_specs=[pl.BlockSpec(memory_space=pltpu.SMEM)] *...  11.1 us
  transfers between devices with their start and end apart: 14, of which 11 were waited for; matrix products, arithmetic and copies ran while one was open for 1% of the time, Pallas kernels for 19%

profile of v5, /device:TPU:0, one launch (start us, length us, event | category | flops | bytes accessed | tf_op | source)
XLA Modules:
  0.0 195.5 jit_solution(17381391741065907687)
XLA Ops:
  2.0 19.9 %all_to_all.30.own = f32[16,80,128]{2,1,0:T(8,128)S(1)} all-to-all(f32[16,80,128]{2,1,0:T(8,128)S(1)} %deal.1), channel_id=1, replica_groups=mesh['tier'=8,'member'=16] {'member'}, dimensions={0} | all-to-all | bytes 1310720 | tf_op jit(solution)/shard_map/all_to_all | solution.py:437
  23.2 3.0 %collective-permute-start.1 = (s32[768]{0:T(1024)S(1)}, s32[768]{0:T(1024)S(1)}, u32[]{:S(2)}, u32[]{:S(2)}) collective-permute-start(s32[768]{0:T(1024)S(1)} %convert_element_type.28), channel_id=1, source_target_pairs={{0,16},{16,32},{32,48},{48,64},{64,80},{80,96},{96,112},{1,17},{17... | collective-permute-start | bytes 9224 | tf_op jit(solution)/shard_map/ppermute | solution.py:26
  28.4 6.2 %collective-permute-start.4 = (f32[16,80,128]{2,1,0:T(8,128)S(1)}, f32[16,80,128]{2,1,0:T(8,128)S(1)}, u32[]{:S(2)}, u32[]{:S(2)}) collective-permute-start(f32[16,80,128]{2,1,0:T(8,128)S(1)} %all_to_all.30.own), channel_id=1, source_target_pairs={{0,32},{16,48},{32,64},{48,80},{64,96},{80,112},{1,33},{17,49},{33... | collective-permute-start | bytes 1966088 | tf_op jit(solution)/shard_map/ppermute | solution.py:26
  34.6 2.6 %pick.5 = f32[16,144,128]{2,1,0:T(8,128)} custom-call(s32[2304]{0:T(1024)S(1)} %pad_add_fusion.table.links, f32[16,80,128]{2,1,0:T(8,128)S(1)} %all_to_all.30.own), custom_call_target="tpu_custom_call" | custom-call | tf_op jit(solution)/shard_map/pick/pallas_call | solution.py:161
  37.2 3.7 %all-to-all-start.2 = ((f32[16,144,128]{2,1,0:T(8,128)}), f32[16,144,128]{2,1,0:T(8,128)S(1)}, u32[]{:S(2)}, u32[]{:S(2)}) async-start(f32[16,144,128]{2,1,0:T(8,128)} %pick.5), calls=%async_computation.2 | async-start | bytes 2359296 | tf_op jit(solution)/shard_map/all_to_all | solution.py:437
  41.1 6.2 %collective-permute-done.3.above2 = f32[16,80,128]{2,1,0:T(8,128)S(1)} collective-permute-done((f32[16,80,128]{2,1,0:T(8,128)S(1)}, f32[16,80,128]{2,1,0:T(8,128)S(1)}, u32[]{:S(2)}, u32[]{:S(2)}) %collective-permute-start.3) | collective-permute-done | bytes 655392 | tf_op jit(solution)/shard_map/ppermute | solution.py:26
  51.8 3.7 %pick.4 = f32[16,288,128]{2,1,0:T(8,128)} custom-call(s32[2304]{0:T(1024)S(1)} %pad_add_fusion.table.links, s32[2]{0:T(128)S(1)} %pad_add_fusion.1.place, f32[16,80,128]{2,1,0:T(8,128)} %collective-permute-done.2.mate, f32[16,80,128]{2,1,0:T(8,128)} %collective-permute-done.5.cross, f32[16,80,128]{2,1,0:T(8,128)S(1)} %collective-permute-done.3.above2, ...), custom_call_target="tpu_custom_call" | custom-call | tf_op jit(solution)/shard_map/pick/pallas_call | solution.py:161
  55.6 4.5 %all-to-all-done.2.near = f32[16,144,128]{2,1,0:T(8,128)S(1)} async-done(((f32[16,144,128]{2,1,0:T(8,128)}), f32[16,144,128]{2,1,0:T(8,128)S(1)}, u32[]{:S(2)}, u32[]{:S(2)}) %all-to-all-start.2) | async-done | bytes 1179680 | tf_op jit(solution)/shard_map/all_to_all | solution.py:437
  60.1 3.7 %all-to-all-start.1 = ((f32[16,288,128]{2,1,0:T(8,128)}), f32[16,288,128]{2,1,0:T(8,128)S(1)}, u32[]{:S(2)}, u32[]{:S(2)}) async-start(f32[16,288,128]{2,1,0:T(8,128)} %pick.4), calls=%async_computation.1 | async-start | bytes 4718592 | tf_op jit(solution)/shard_map/all_to_all | solution.py:437
  64.5 4.2 %nodes.1 = (s32[48]{0:T(128)}, f32[78]{0:T(128)}, s32[768]{0:T(1024)}) custom-call(s32[2304]{0:T(1024)} %copy-done.4, s32[2]{0:T(128)} %copy-done.9, f32[96]{0:T(128)} %corr_real.1, f32[96]{0:T(128)} %corr_imag.1, f32[96]{0:T(128)} %decay.1, f32[6]{0:T(128)} %maximum_multiply_fusion.weight), custom_call_target="tpu_custom_call" | custom-call | tf_op jit(solution)/shard_map/nodes/pallas_call | solution.py:72
  73.2 6.3 %operators.1.core.refs_0_.refs_1_.refs_2_.refs_3_.refs_4_.refs_5_.refs_6_.refs_7_ = bf16[49,2,96,128]{3,2,1,0:T(8,128)(2,1)} custom-call(s32[48]{0:T(128)S(1)} %copy-done.11, f32[78]{0:T(128)S(1)} %copy-done.7, f32[96,96]{1,0:T(8,128)S(1)} %copy-done.5, f32[96,96,96]{2,1,0:T(8,128)S(1)} %copy-done), custom_call_target="tpu_custom_call" | custom-call | tf_op jit(solution)/shard_map/operators/pallas_call | solution.py:256
  79.5 7.3 %early.2 = (f32[8,192,128]{2,1,0:T(8,128)}, f32[8,192,128]{2,1,0:T(8,128)}) custom-call(f32[78]{0:T(128)S(1)} %copy-done.8, f32[8,144,128]{2,1,0:T(8,128)S(1)} %bitcast.21, f32[16,144,128]{2,1,0:T(8,128)S(1)} %all-to-all-done.2.near, bf16[49,2,96,128]{3,2,1,0:T(8,128)(2,1)} %operators.1.core.refs_0_.refs_1_.refs_2_.refs_3_.refs_4_.refs_5_.refs_6_.refs_7_, ...), custom_call_target="tpu_custom_call" | custom-call | tf_op jit(solution)/shard_map/early/pallas_call | solution.py:396
  86.8 10.8 %all-to-all-done.1.other = f32[16,288,128]{2,1,0:T(8,128)S(1)} async-done(((f32[16,288,128]{2,1,0:T(8,128)}), f32[16,288,128]{2,1,0:T(8,128)S(1)}, u32[]{:S(2)}, u32[]{:S(2)}) %all-to-all-start.1) | async-done | bytes 2359328 | tf_op jit(solution)/shard_map/all_to_all | solution.py:437
  97.6 9.2 %late.2 = (f32[16,72,128]{2,1,0:T(8,128)}, f32[8,192,128]{2,1,0:T(8,128)}) custom-call(f32[78]{0:T(128)S(1)} %copy-done.8, f32[16,288,128]{2,1,0:T(8,128)S(1)} %all-to-all-done.1.other, bf16[49,2,96,128]{3,2,1,0:T(8,128)(2,1)} %operators.1.core.refs_0_.refs_1_.refs_2_.refs_3_.refs_4_.refs_5_.refs_6_.refs_7_, ...), custom_call_target="tpu_custom_call" | custom-call | tf_op jit(solution)/shard_map/late/pallas_call | solution.py:409
  106.8 15.5 %all_to_all.31.own = f32[16,72,128]{2,1,0:T(8,128)S(1)} all-to-all(f32[16,72,128]{2,1,0:T(8,128)} %get-tuple-element.22.state), channel_id=1, replica_groups=mesh['tier'=8,'member'=16] {'member'}, dimensions={0} | all-to-all | bytes 1179648 | tf_op jit(solution)/shard_map/all_to_all | solution.py:437
  123.6 4.6 %collective-permute-start.8 = (f32[16,72,128]{2,1,0:T(8,128)S(1)}, f32[16,72,128]{2,1,0:T(8,128)S(1)}, u32[]{:S(2)}, u32[]{:S(2)}) collective-permute-start(f32[16,72,128]{2,1,0:T(8,128)S(1)} %all_to_all.31.own), channel_id=1, source_target_pairs={{0,32},{16,48},{32,64},{48,80},{64,96},{80,112},{1,33},{17,49},{33... | collective-permute-start | bytes 1769480 | tf_op jit(solution)/shard_map/ppermute | solution.py:26
  130.2 3.7 %all-to-all-start.5 = ((f32[16,144,128]{2,1,0:T(8,128)}), f32[16,144,128]{2,1,0:T(8,128)S(1)}, u32[]{:S(2)}, u32[]{:S(2)}) async-start(f32[16,144,128]{2,1,0:T(8,128)} %pick.7), calls=%async_computation.5 | async-start | bytes 2359296 | tf_op jit(solution)/shard_map/all_to_all | solution.py:437
  134.1 3.8 %collective-permute-done.7.above2 = f32[16,72,128]{2,1,0:T(8,128)S(1)} collective-permute-done((f32[16,72,128]{2,1,0:T(8,128)S(1)}, f32[16,72,128]{2,1,0:T(8,128)S(1)}, u32[]{:S(2)}, u32[]{:S(2)}) %collective-permute-start.7) | collective-permute-done | bytes 589856 | tf_op jit(solution)/shard_map/ppermute | solution.py:26
  141.2 2.7 %pick.6 = f32[16,288,128]{2,1,0:T(8,128)} custom-call(s32[768]{0:T(1024)S(1)} %copy-done.6, s32[2]{0:T(128)S(1)} %copy-done.10, f32[16,72,128]{2,1,0:T(8,128)S(1)} %collective-permute-done.6.mate, f32[16,72,128]{2,1,0:T(8,128)S(1)} %collective-permute-done.9.cross, f32[16,72,128]{2,1,0:T(8,128)S(1)} %collective-permute-done.7.above2, ...), custom_call_target="tpu_custom_call" | custom-call | tf_op jit(solution)/shard_map/pick/pallas_call | solution.py:161
  143.8 7.5 %all-to-all-done.5.near = f32[16,144,128]{2,1,0:T(8,128)S(1)} async-done(((f32[16,144,128]{2,1,0:T(8,128)}), f32[16,144,128]{2,1,0:T(8,128)S(1)}, u32[]{:S(2)}, u32[]{:S(2)}) %all-to-all-start.5) | async-done | bytes 1179680 | tf_op jit(solution)/shard_map/all_to_all | solution.py:437
  151.4 3.7 %all-to-all-start.4 = ((f32[16,288,128]{2,1,0:T(8,128)}), f32[16,288,128]{2,1,0:T(8,128)S(1)}, u32[]{:S(2)}, u32[]{:S(2)}) async-start(f32[16,288,128]{2,1,0:T(8,128)} %pick.6), calls=%async_computation.4 | async-start | bytes 4718592 | tf_op jit(solution)/shard_map/all_to_all | solution.py:437
  156.2 7.5 %early.3 = (f32[8,192,128]{2,1,0:T(8,128)}, f32[8,192,128]{2,1,0:T(8,128)}) custom-call(f32[78]{0:T(128)S(1)} %copy-done.8, f32[16,72,128]{2,1,0:T(8,128)S(1)} %copy-done.3, f32[16,144,128]{2,1,0:T(8,128)S(1)} %all-to-all-done.5.near, bf16[49,2,96,128]{3,2,1,0:T(8,128)(2,1)} %operators.1.core.refs_0_.refs_1_.refs_2_.refs_3_.refs_4_.refs_5_.refs_6_.refs_7_, ...), custom_call_target="tpu_custom_call" | custom-call | tf_op jit(solution)/shard_map/early/pallas_call | solution.py:396
  163.6 22.7 %all-to-all-done.4.other = f32[16,288,128]{2,1,0:T(8,128)S(1)} async-done(((f32[16,288,128]{2,1,0:T(8,128)}), f32[16,288,128]{2,1,0:T(8,128)S(1)}, u32[]{:S(2)}, u32[]{:S(2)}) %all-to-all-start.4) | async-done | bytes 2359328 | tf_op jit(solution)/shard_map/all_to_all | solution.py:437
  186.3 9.1 %late.3 = f32[8,144,128]{2,1,0:T(8,128)} custom-call(f32[78]{0:T(128)S(1)} %copy-done.8, f32[16,288,128]{2,1,0:T(8,128)S(1)} %all-to-all-done.4.other, bf16[49,2,96,128]{3,2,1,0:T(8,128)(2,1)} %operators.1.core.refs_0_.refs_1_.refs_2_.refs_3_.refs_4_.refs_5_.refs_6_.refs_7_, ...), custom_call_target="tpu_custom_call" | custom-call | tf_op jit(solution)/shard_map/late/pallas_call | solution.py:409
  (54 shorter events, 23.0 us)
Async XLA Ops:
  0.8 1.1 copy-start.1
  22.0 4.3 %collective-permute-start = (s32[768]{0:T(1024)S(1)}, s32[768]{0:T(1024)S(1)}, u32[]{:S(2)}, u32[]{:S(2)}) collective-permute-start(s32[768]{0:T(1024)S(1)} %convert_element_type.28), channel_id=1, source_target_pairs={{16,0},{32,16},{48,32},{64,48},{80,64},{96,80},{112,96},{17,1},{33... | collective-permute-start | bytes 9224 | tf_op jit(solution)/shard_map/ppermute | solution.py:26
  23.2 3.8 %collective-permute-start.1 = (s32[768]{0:T(1024)S(1)}, s32[768]{0:T(1024)S(1)}, u32[]{:S(2)}, u32[]{:S(2)}) collective-permute-start(s32[768]{0:T(1024)S(1)} %convert_element_type.28), channel_id=1, source_target_pairs={{0,16},{16,32},{32,48},{48,64},{64,80},{80,96},{96,112},{1,17},{17... | collective-permute-start | bytes 9224 | tf_op jit(solution)/shard_map/ppermute | solution.py:26
  27.1 24.7 %copy-start.4 = (s32[2304]{0:T(1024)}, s32[2304]{0:T(1024)S(1)}, u32[]{:S(2)}) copy-start(s32[2304]{0:T(1024)S(1)} %pad_add_fusion.table.links) | copy-start | bytes 27652
  27.1 20.2 %collective-permute-start.3 = (f32[16,80,128]{2,1,0:T(8,128)S(1)}, f32[16,80,128]{2,1,0:T(8,128)S(1)}, u32[]{:S(2)}, u32[]{:S(2)}) collective-permute-start(f32[16,80,128]{2,1,0:T(8,128)S(1)} %all_to_all.30.own), channel_id=1, source_target_pairs={{32,0},{48,16},{64,32},{80,48},{96,64},{112,80},{33,1},{49,17},{65... | collective-permute-start | bytes 1966088 | tf_op jit(solution)/shard_map/ppermute | solution.py:26
  28.4 20.1 %collective-permute-start.4 = (f32[16,80,128]{2,1,0:T(8,128)S(1)}, f32[16,80,128]{2,1,0:T(8,128)S(1)}, u32[]{:S(2)}, u32[]{:S(2)}) collective-permute-start(f32[16,80,128]{2,1,0:T(8,128)S(1)} %all_to_all.30.own), channel_id=1, source_target_pairs={{0,32},{16,48},{32,64},{48,80},{64,96},{80,112},{1,33},{17,49},{33... | collective-permute-start | bytes 1966088 | tf_op jit(solution)/shard_map/ppermute | solution.py:26
  37.2 22.8 %all-to-all-start.2 = ((f32[16,144,128]{2,1,0:T(8,128)}), f32[16,144,128]{2,1,0:T(8,128)S(1)}, u32[]{:S(2)}, u32[]{:S(2)}) async-start(f32[16,144,128]{2,1,0:T(8,128)} %pick.5), calls=%async_computation.2 | async-start | bytes 2359296 | tf_op jit(solution)/shard_map/all_to_all | solution.py:437
  41.0 8.5 %collective-permute-start.2 = (f32[16,80,128]{2,1,0:T(8,128)S(1)}, f32[16,80,128]{2,1,0:T(8,128)}, u32[]{:S(2)}, u32[]{:S(2)}) collective-permute-start(f32[16,80,128]{2,1,0:T(8,128)S(1)} %all_to_all.30.own), channel_id=1, source_target_pairs={{0,16},{16,0},{32,48},{48,32},{64,80},{80,64},{96,112},{112,96},{1... | collective-permute-start | bytes 1966088 | tf_op jit(solution)/shard_map/ppermute | solution.py:443
  49.4 2.4 %collective-permute-start.5 = (f32[16,80,128]{2,1,0:T(8,128)}, f32[16,80,128]{2,1,0:T(8,128)}, u32[]{:S(2)}, u32[]{:S(2)}) collective-permute-start(f32[16,80,128]{2,1,0:T(8,128)} %broadcast_select_fusion), channel_id=1, source_target_pairs={{0,16},{16,0},{32,48},{48,32},{64,80},{80,64},{96,112},{112,96},{1... | collective-permute-start | bytes 1966088 | tf_op jit(solution)/shard_map/ppermute | solution.py:447
  49.4 6.1 %copy-start.9 = (s32[2]{0:T(128)}, s32[2]{0:T(128)S(1)}, u32[]{:S(2)}) copy-start(s32[2]{0:T(128)S(1)} %pad_add_fusion.1.place) | copy-start | bytes 28
  60.1 37.5 %all-to-all-start.1 = ((f32[16,288,128]{2,1,0:T(8,128)}), f32[16,288,128]{2,1,0:T(8,128)S(1)}, u32[]{:S(2)}, u32[]{:S(2)}) async-start(f32[16,288,128]{2,1,0:T(8,128)} %pick.4), calls=%async_computation.1 | async-start | bytes 4718592 | tf_op jit(solution)/shard_map/all_to_all | solution.py:437
  68.7 2.3 %copy-start = (f32[96,96,96]{2,1,0:T(8,128)S(1)}, f32[96,96,96]{2,1,0:T(8,128)}, u32[]{:S(2)}) copy-start(f32[96,96,96]{2,1,0:T(8,128)} %coupling.1) | copy-start | bytes 10616836
  71.1 0.8 copy-start.5
  73.2 6.3 %copy-start.2 = (f32[8,2,9216]{2,1,0:T(2,128)S(1)}, f32[8,2,9216]{2,1,0:T(2,128)}, u32[]{:S(2)}) copy-start(f32[8,2,9216]{2,1,0:T(2,128)} %param.12) | copy-start | bytes 1769476
  73.2 6.4 %copy-start.8 = (f32[78]{0:T(128)S(1)}, f32[78]{0:T(128)}, u32[]{:S(2)}) copy-start(f32[78]{0:T(128)} %get-tuple-element.17.scale) | copy-start | bytes 940
  97.6 30.6 %copy-start.6 = (s32[768]{0:T(1024)S(1)}, s32[768]{0:T(1024)}, u32[]{:S(2)}) copy-start(s32[768]{0:T(1024)} %get-tuple-element.18.links) | copy-start | bytes 9220
  122.3 15.6 %collective-permute-start.7 = (f32[16,72,128]{2,1,0:T(8,128)S(1)}, f32[16,72,128]{2,1,0:T(8,128)S(1)}, u32[]{:S(2)}, u32[]{:S(2)}) collective-permute-start(f32[16,72,128]{2,1,0:T(8,128)S(1)} %all_to_all.31.own), channel_id=1, source_target_pairs={{32,0},{48,16},{64,32},{80,48},{96,64},{112,80},{33,1},{49,17},{65... | collective-permute-start | bytes 1769480 | tf_op jit(solution)/shard_map/ppermute | solution.py:26
  123.6 15.5 %collective-permute-start.8 = (f32[16,72,128]{2,1,0:T(8,128)S(1)}, f32[16,72,128]{2,1,0:T(8,128)S(1)}, u32[]{:S(2)}, u32[]{:S(2)}) collective-permute-start(f32[16,72,128]{2,1,0:T(8,128)S(1)} %all_to_all.31.own), channel_id=1, source_target_pairs={{0,32},{16,48},{32,64},{48,80},{64,96},{80,112},{1,33},{17,49},{33... | collective-permute-start | bytes 1769480 | tf_op jit(solution)/shard_map/ppermute | solution.py:26
  130.2 10.9 %copy-start.10 = (s32[2]{0:T(128)S(1)}, s32[2]{0:T(128)}, u32[]{:S(2)}) copy-start(s32[2]{0:T(128)} %copy-done.9) | copy-start | bytes 28
  130.2 21.1 %all-to-all-start.5 = ((f32[16,144,128]{2,1,0:T(8,128)}), f32[16,144,128]{2,1,0:T(8,128)S(1)}, u32[]{:S(2)}, u32[]{:S(2)}) async-start(f32[16,144,128]{2,1,0:T(8,128)} %pick.7), calls=%async_computation.5 | async-start | bytes 2359296 | tf_op jit(solution)/shard_map/all_to_all | solution.py:437
  134.0 5.2 %collective-permute-start.6 = (f32[16,72,128]{2,1,0:T(8,128)S(1)}, f32[16,72,128]{2,1,0:T(8,128)S(1)}, u32[]{:S(2)}, u32[]{:S(2)}) collective-permute-start(f32[16,72,128]{2,1,0:T(8,128)S(1)} %all_to_all.31.own), channel_id=1, source_target_pairs={{0,16},{16,0},{32,48},{48,32},{64,80},{80,64},{96,112},{112,96},{1... | collective-permute-start | bytes 1769480 | tf_op jit(solution)/shard_map/ppermute | solution.py:443
  139.1 2.1 %collective-permute-start.9 = (f32[16,72,128]{2,1,0:T(8,128)S(1)}, f32[16,72,128]{2,1,0:T(8,128)S(1)}, u32[]{:S(2)}, u32[]{:S(2)}) collective-permute-start(f32[16,72,128]{2,1,0:T(8,128)S(1)} %broadcast_select_fusion.1), channel_id=1, source_target_pairs={{0,16},{16,0},{32,48},{48,32},{64,80},{80,64},{96,112},{112,96},{1... | collective-permute-start | bytes 1769480 | tf_op jit(solution)/shard_map/ppermute | solution.py:447
  151.4 34.9 %all-to-all-start.4 = ((f32[16,288,128]{2,1,0:T(8,128)}), f32[16,288,128]{2,1,0:T(8,128)S(1)}, u32[]{:S(2)}, u32[]{:S(2)}) async-start(f32[16,288,128]{2,1,0:T(8,128)} %pick.6), calls=%async_computation.4 | async-start | bytes 4718592 | tf_op jit(solution)/shard_map/all_to_all | solution.py:437
  155.1 1.1 copy-start.3
  (2 other events, 1.3 us)

commit v6 on v5

--- a/solution.py
+++ b/solution.py
@@ -316,7 +316,7 @@
         m = pl.program_id(0) * TOGETHER + turn
         up_op, down_op, above_op, below_op = ops[4 * turn : 4 * turn + 4]
         for kind in range(4):
-            assembled(other, (turn * 4 + kind) * PIECE, raw.at[turn, kind], plain.at[turn, kind])
+            assembled(other, (m * 4 + kind) * PIECE, raw.at[turn, kind], plain.at[turn, kind])
         up, down, up2, down2 = (plain[turn, kind, 0 : 2 * N, :] for kind in range(4))
         up_pieces = halved(up)
         first = commuted(
@@ -347,7 +347,7 @@
                 result[member, pl.ds(m * PIECE, PIECE), :] = raw[turn, 0, member * PIECE : (member + 1) * PIECE, :]
 
 
-TOGETHER = 2
+TOGETHER = 4
 PLAIN = pl.BlockSpec((TOGETHER, 2 * N, 128), lambda step, scale: (step, 0, 0))
 WHOLE = pl.BlockSpec((TOGETHER, ROWS, 128), lambda step, scale: (step, 0, 0))
 SUMS = pltpu.HBM((M, 2 * N, 128), F32)
@@ -398,7 +398,7 @@
 
 def late(scale, other, operators, part, total):
     last = total is not None
-    specs = [pl.BlockSpec((MEMBERS, TOGETHER * 4 * PIECE, 128), lambda step, scale: (0, step, 0))]
+    specs = [pl.BlockSpec(memory_space=pltpu.VMEM)]
     specs += [HAMILTONIAN] + operator_specs(0, 3, 1, 5) + [PLAIN] * (1 + last)
     if last:
         outs = [WHOLE], [jax.ShapeDtypeStruct((M, ROWS, 128), F32)]

time: 197 us -> 196 us (level)
  no operation moved by 1% of the time
where the time goes in v6:
time: 196 us; the launch traced here: 195 us
  waiting for transfers between devices  63.2 us (32%)
  Pallas kernels  53.4 us (27%)
  blocking collectives  35.3 us (18%)
  starting transfers between devices  33 us (17%)
  local copies, waits for them, and re-layouts  7.47 us (4%)
    all_to_all x4, waiting for transfers between devices, swapped(): lax.all_to_all(blocks, 'member', split_axis=0, concat_axis=0, tiled=True)  45.7 us
    all_to_all x2, blocking collectives, swapped(): lax.all_to_all(blocks, 'member', split_axis=0, concat_axis=0, tiled=True)  35.3 us
    ppermute x6, starting transfers between devices, passed_along(): lax.ppermute(value, 'tier', [(source, source + steps) for source in range...  17.7 us
    pallas_call x2, Pallas kernels, late(): call(scale, other, *kept(*[operators] * (4 * TOGETHER + 1), part, *[total...  17.3 us
    all_to_all x4, starting transfers between devices, swapped(): lax.all_to_all(blocks, 'member', split_axis=0, concat_axis=0, tiled=True)  15.1 us
    pallas_call x2, Pallas kernels, early(): call(scale, state, near, *kept(*[operators] * (4 * TOGETHER + 1), *sums))  14.4 us
    ppermute x6, waiting for transfers between devices, passed_along(): lax.ppermute(value, 'tier', [(source, source + steps) for source in range...  13.1 us
    pallas_call x4, Pallas kernels, picked(): pl.pallas_call(kernel, in_specs=[pl.BlockSpec(memory_space=pltpu.SMEM)] *...  11.1 us
  transfers between devices with their start and end apart: 14, of which 11 were waited for; matrix products, arithmetic and copies ran while one was open for 1% of the time, Pallas kernels for 19%

profile of v6, /device:TPU:0, one launch (start us, length us, event | category | flops | bytes accessed | tf_op | source)
XLA Modules:
  0.0 194.6 jit_solution(12534007304177586805)
XLA Ops:
  2.0 19.9 %all_to_all.30.own = f32[16,80,128]{2,1,0:T(8,128)S(1)} all-to-all(f32[16,80,128]{2,1,0:T(8,128)S(1)} %deal.1), channel_id=1, replica_groups=mesh['tier'=8,'member'=16] {'member'}, dimensions={0} | all-to-all | bytes 1310720 | tf_op jit(solution)/shard_map/all_to_all | solution.py:437
  23.2 3.0 %collective-permute-start.1 = (s32[768]{0:T(1024)S(1)}, s32[768]{0:T(1024)S(1)}, u32[]{:S(2)}, u32[]{:S(2)}) collective-permute-start(s32[768]{0:T(1024)S(1)} %convert_element_type.28), channel_id=1, source_target_pairs={{0,16},{16,32},{32,48},{48,64},{64,80},{80,96},{96,112},{1,17},{17... | collective-permute-start | bytes 9224 | tf_op jit(solution)/shard_map/ppermute | solution.py:26
  28.4 6.2 %collective-permute-start.4 = (f32[16,80,128]{2,1,0:T(8,128)S(1)}, f32[16,80,128]{2,1,0:T(8,128)S(1)}, u32[]{:S(2)}, u32[]{:S(2)}) collective-permute-start(f32[16,80,128]{2,1,0:T(8,128)S(1)} %all_to_all.30.own), channel_id=1, source_target_pairs={{0,32},{16,48},{32,64},{48,80},{64,96},{80,112},{1,33},{17,49},{33... | collective-permute-start | bytes 1966088 | tf_op jit(solution)/shard_map/ppermute | solution.py:26
  34.6 2.6 %pick.5 = f32[16,144,128]{2,1,0:T(8,128)} custom-call(s32[2304]{0:T(1024)S(1)} %pad_add_fusion.table.links, f32[16,80,128]{2,1,0:T(8,128)S(1)} %all_to_all.30.own), custom_call_target="tpu_custom_call" | custom-call | tf_op jit(solution)/shard_map/pick/pallas_call | solution.py:161
  37.2 3.7 %all-to-all-start.2 = ((f32[16,144,128]{2,1,0:T(8,128)}), f32[16,144,128]{2,1,0:T(8,128)S(1)}, u32[]{:S(2)}, u32[]{:S(2)}) async-start(f32[16,144,128]{2,1,0:T(8,128)} %pick.5), calls=%async_computation.2 | async-start | bytes 2359296 | tf_op jit(solution)/shard_map/all_to_all | solution.py:437
  41.1 6.2 %collective-permute-done.3.above2 = f32[16,80,128]{2,1,0:T(8,128)S(1)} collective-permute-done((f32[16,80,128]{2,1,0:T(8,128)S(1)}, f32[16,80,128]{2,1,0:T(8,128)S(1)}, u32[]{:S(2)}, u32[]{:S(2)}) %collective-permute-start.3) | collective-permute-done | bytes 655392 | tf_op jit(solution)/shard_map/ppermute | solution.py:26
  51.8 3.7 %pick.4 = f32[16,288,128]{2,1,0:T(8,128)} custom-call(s32[2304]{0:T(1024)S(1)} %pad_add_fusion.table.links, s32[2]{0:T(128)S(1)} %pad_add_fusion.1.place, f32[16,80,128]{2,1,0:T(8,128)} %collective-permute-done.2.mate, f32[16,80,128]{2,1,0:T(8,128)} %collective-permute-done.5.cross, f32[16,80,128]{2,1,0:T(8,128)S(1)} %collective-permute-done.3.above2, ...), custom_call_target="tpu_custom_call" | custom-call | tf_op jit(solution)/shard_map/pick/pallas_call | solution.py:161
  55.6 4.5 %all-to-all-done.2.near = f32[16,144,128]{2,1,0:T(8,128)S(1)} async-done(((f32[16,144,128]{2,1,0:T(8,128)}), f32[16,144,128]{2,1,0:T(8,128)S(1)}, u32[]{:S(2)}, u32[]{:S(2)}) %all-to-all-start.2) | async-done | bytes 1179680 | tf_op jit(solution)/shard_map/all_to_all | solution.py:437
  60.1 3.7 %all-to-all-start.1 = ((f32[16,288,128]{2,1,0:T(8,128)}), f32[16,288,128]{2,1,0:T(8,128)S(1)}, u32[]{:S(2)}, u32[]{:S(2)}) async-start(f32[16,288,128]{2,1,0:T(8,128)} %pick.4), calls=%async_computation.1 | async-start | bytes 4718592 | tf_op jit(solution)/shard_map/all_to_all | solution.py:437
  64.5 4.2 %nodes.1 = (s32[48]{0:T(128)}, f32[78]{0:T(128)}, s32[768]{0:T(1024)}) custom-call(s32[2304]{0:T(1024)} %copy-done.4, s32[2]{0:T(128)} %copy-done.9, f32[96]{0:T(128)} %corr_real.1, f32[96]{0:T(128)} %corr_imag.1, f32[96]{0:T(128)} %decay.1, f32[6]{0:T(128)} %maximum_multiply_fusion.weight), custom_call_target="tpu_custom_call" | custom-call | tf_op jit(solution)/shard_map/nodes/pallas_call | solution.py:72
  73.2 6.3 %operators.1.core.refs_0_.refs_1_.refs_2_.refs_3_.refs_4_.refs_5_.refs_6_.refs_7_.refs_8_.refs_9_.refs_10_.refs_11_.refs_12_.refs_13_.refs_14_.refs_15_ = bf16[49,2,96,128]{3,2,1,0:T(8,128)(2,1)} custom-call(s32[48]{0:T(128)S(1)} %copy-done.11, f32[78]{0:T(128)S(1)} %copy-done.7, f32[96,96]{1,0:T(8,128)S(1)} %copy-done.5, f32[96,96,96]{2,1,0:T(8,128)S(1)} %copy-done), custom_call_target="tpu_custom_call" | custom-call | tf_op jit(solution)/shard_map/operators/pallas_call | solution.py:256
  79.5 7.1 %early.2 = (f32[8,192,128]{2,1,0:T(8,128)}, f32[8,192,128]{2,1,0:T(8,128)}) custom-call(f32[78]{0:T(128)S(1)} %copy-done.8, f32[8,144,128]{2,1,0:T(8,128)S(1)} %bitcast.21, f32[16,144,128]{2,1,0:T(8,128)S(1)} %all-to-all-done.2.near, ...), custom_call_target="tpu_custom_call" | custom-call | tf_op jit(solution)/shard_map/early/pallas_call | solution.py:396
  86.6 11.0 %all-to-all-done.1.other = f32[16,288,128]{2,1,0:T(8,128)S(1)} async-done(((f32[16,288,128]{2,1,0:T(8,128)}), f32[16,288,128]{2,1,0:T(8,128)S(1)}, u32[]{:S(2)}, u32[]{:S(2)}) %all-to-all-start.1) | async-done | bytes 2359328 | tf_op jit(solution)/shard_map/all_to_all | solution.py:437
  97.6 8.7 %late.2 = (f32[16,72,128]{2,1,0:T(8,128)}, f32[8,192,128]{2,1,0:T(8,128)}) custom-call(f32[78]{0:T(128)S(1)} %copy-done.8, f32[16,288,128]{2,1,0:T(8,128)S(1)} %all-to-all-done.1.other, ...), custom_call_target="tpu_custom_call" | custom-call | tf_op jit(solution)/shard_map/late/pallas_call | solution.py:409
  106.3 15.5 %all_to_all.31.own = f32[16,72,128]{2,1,0:T(8,128)S(1)} all-to-all(f32[16,72,128]{2,1,0:T(8,128)} %get-tuple-element.22.state), channel_id=1, replica_groups=mesh['tier'=8,'member'=16] {'member'}, dimensions={0} | all-to-all | bytes 1179648 | tf_op jit(solution)/shard_map/all_to_all | solution.py:437
  123.0 4.6 %collective-permute-start.8 = (f32[16,72,128]{2,1,0:T(8,128)S(1)}, f32[16,72,128]{2,1,0:T(8,128)S(1)}, u32[]{:S(2)}, u32[]{:S(2)}) collective-permute-start(f32[16,72,128]{2,1,0:T(8,128)S(1)} %all_to_all.31.own), channel_id=1, source_target_pairs={{0,32},{16,48},{32,64},{48,80},{64,96},{80,112},{1,33},{17,49},{33... | collective-permute-start | bytes 1769480 | tf_op jit(solution)/shard_map/ppermute | solution.py:26
  129.7 3.7 %all-to-all-start.5 = ((f32[16,144,128]{2,1,0:T(8,128)}), f32[16,144,128]{2,1,0:T(8,128)S(1)}, u32[]{:S(2)}, u32[]{:S(2)}) async-start(f32[16,144,128]{2,1,0:T(8,128)} %pick.7), calls=%async_computation.5 | async-start | bytes 2359296 | tf_op jit(solution)/shard_map/all_to_all | solution.py:437
  133.5 3.8 %collective-permute-done.7.above2 = f32[16,72,128]{2,1,0:T(8,128)S(1)} collective-permute-done((f32[16,72,128]{2,1,0:T(8,128)S(1)}, f32[16,72,128]{2,1,0:T(8,128)S(1)}, u32[]{:S(2)}, u32[]{:S(2)}) %collective-permute-start.7) | collective-permute-done | bytes 589856 | tf_op jit(solution)/shard_map/ppermute | solution.py:26
  140.7 2.7 %pick.6 = f32[16,288,128]{2,1,0:T(8,128)} custom-call(s32[768]{0:T(1024)S(1)} %copy-done.6, s32[2]{0:T(128)S(1)} %copy-done.10, f32[16,72,128]{2,1,0:T(8,128)S(1)} %collective-permute-done.6.mate, f32[16,72,128]{2,1,0:T(8,128)S(1)} %collective-permute-done.9.cross, f32[16,72,128]{2,1,0:T(8,128)S(1)} %collective-permute-done.7.above2, ...), custom_call_target="tpu_custom_call" | custom-call | tf_op jit(solution)/shard_map/pick/pallas_call | solution.py:161
  143.3 7.5 %all-to-all-done.5.near = f32[16,144,128]{2,1,0:T(8,128)S(1)} async-done(((f32[16,144,128]{2,1,0:T(8,128)}), f32[16,144,128]{2,1,0:T(8,128)S(1)}, u32[]{:S(2)}, u32[]{:S(2)}) %all-to-all-start.5) | async-done | bytes 1179680 | tf_op jit(solution)/shard_map/all_to_all | solution.py:437
  150.9 3.9 %all-to-all-start.4 = ((f32[16,288,128]{2,1,0:T(8,128)}), f32[16,288,128]{2,1,0:T(8,128)S(1)}, u32[]{:S(2)}, u32[]{:S(2)}) async-start(f32[16,288,128]{2,1,0:T(8,128)} %pick.6), calls=%async_computation.4 | async-start | bytes 4718592 | tf_op jit(solution)/shard_map/all_to_all | solution.py:437
  155.8 7.3 %early.3 = (f32[8,192,128]{2,1,0:T(8,128)}, f32[8,192,128]{2,1,0:T(8,128)}) custom-call(f32[78]{0:T(128)S(1)} %copy-done.8, f32[16,72,128]{2,1,0:T(8,128)S(1)} %copy-done.3, f32[16,144,128]{2,1,0:T(8,128)S(1)} %all-to-all-done.5.near, ...), custom_call_target="tpu_custom_call" | custom-call | tf_op jit(solution)/shard_map/early/pallas_call | solution.py:396
  163.2 22.6 %all-to-all-done.4.other = f32[16,288,128]{2,1,0:T(8,128)S(1)} async-done(((f32[16,288,128]{2,1,0:T(8,128)}), f32[16,288,128]{2,1,0:T(8,128)S(1)}, u32[]{:S(2)}, u32[]{:S(2)}) %all-to-all-start.4) | async-done | bytes 2359328 | tf_op jit(solution)/shard_map/all_to_all | solution.py:437
  185.8 8.6 %late.3 = f32[8,144,128]{2,1,0:T(8,128)} custom-call(f32[78]{0:T(128)S(1)} %copy-done.8, f32[16,288,128]{2,1,0:T(8,128)S(1)} %all-to-all-done.4.other, bf16[49,2,96,128]{3,2,1,0:T(8,128)(2,1)} %operators.1.core.refs_0_.refs_1_.refs_2_.refs_3_.refs_4_.refs_5_.refs_6_.refs_7_.refs_8_.refs_9_.refs_10_.refs_11_.refs_12_.refs_13_.refs_14_.refs_15_, ...), custom_call_target="tpu_custom_call" | custom-call | tf_op jit(solution)/shard_map/late/pallas_call | solution.py:409
  (54 shorter events, 23.0 us)
Async XLA Ops:
  0.8 1.1 copy-start.1
  22.0 4.3 %collective-permute-start = (s32[768]{0:T(1024)S(1)}, s32[768]{0:T(1024)S(1)}, u32[]{:S(2)}, u32[]{:S(2)}) collective-permute-start(s32[768]{0:T(1024)S(1)} %convert_element_type.28), channel_id=1, source_target_pairs={{16,0},{32,16},{48,32},{64,48},{80,64},{96,80},{112,96},{17,1},{33... | collective-permute-start | bytes 9224 | tf_op jit(solution)/shard_map/ppermute | solution.py:26
  23.2 3.8 %collective-permute-start.1 = (s32[768]{0:T(1024)S(1)}, s32[768]{0:T(1024)S(1)}, u32[]{:S(2)}, u32[]{:S(2)}) collective-permute-start(s32[768]{0:T(1024)S(1)} %convert_element_type.28), channel_id=1, source_target_pairs={{0,16},{16,32},{32,48},{48,64},{64,80},{80,96},{96,112},{1,17},{17... | collective-permute-start | bytes 9224 | tf_op jit(solution)/shard_map/ppermute | solution.py:26
  27.1 24.7 %copy-start.4 = (s32[2304]{0:T(1024)}, s32[2304]{0:T(1024)S(1)}, u32[]{:S(2)}) copy-start(s32[2304]{0:T(1024)S(1)} %pad_add_fusion.table.links) | copy-start | bytes 27652
  27.1 20.2 %collective-permute-start.3 = (f32[16,80,128]{2,1,0:T(8,128)S(1)}, f32[16,80,128]{2,1,0:T(8,128)S(1)}, u32[]{:S(2)}, u32[]{:S(2)}) collective-permute-start(f32[16,80,128]{2,1,0:T(8,128)S(1)} %all_to_all.30.own), channel_id=1, source_target_pairs={{32,0},{48,16},{64,32},{80,48},{96,64},{112,80},{33,1},{49,17},{65... | collective-permute-start | bytes 1966088 | tf_op jit(solution)/shard_map/ppermute | solution.py:26
  28.4 20.1 %collective-permute-start.4 = (f32[16,80,128]{2,1,0:T(8,128)S(1)}, f32[16,80,128]{2,1,0:T(8,128)S(1)}, u32[]{:S(2)}, u32[]{:S(2)}) collective-permute-start(f32[16,80,128]{2,1,0:T(8,128)S(1)} %all_to_all.30.own), channel_id=1, source_target_pairs={{0,32},{16,48},{32,64},{48,80},{64,96},{80,112},{1,33},{17,49},{33... | collective-permute-start | bytes 1966088 | tf_op jit(solution)/shard_map/ppermute | solution.py:26
  37.2 22.8 %all-to-all-start.2 = ((f32[16,144,128]{2,1,0:T(8,128)}), f32[16,144,128]{2,1,0:T(8,128)S(1)}, u32[]{:S(2)}, u32[]{:S(2)}) async-start(f32[16,144,128]{2,1,0:T(8,128)} %pick.5), calls=%async_computation.2 | async-start | bytes 2359296 | tf_op jit(solution)/shard_map/all_to_all | solution.py:437
  41.0 8.5 %collective-permute-start.2 = (f32[16,80,128]{2,1,0:T(8,128)S(1)}, f32[16,80,128]{2,1,0:T(8,128)}, u32[]{:S(2)}, u32[]{:S(2)}) collective-permute-start(f32[16,80,128]{2,1,0:T(8,128)S(1)} %all_to_all.30.own), channel_id=1, source_target_pairs={{0,16},{16,0},{32,48},{48,32},{64,80},{80,64},{96,112},{112,96},{1... | collective-permute-start | bytes 1966088 | tf_op jit(solution)/shard_map/ppermute | solution.py:443
  49.4 2.4 %collective-permute-start.5 = (f32[16,80,128]{2,1,0:T(8,128)}, f32[16,80,128]{2,1,0:T(8,128)}, u32[]{:S(2)}, u32[]{:S(2)}) collective-permute-start(f32[16,80,128]{2,1,0:T(8,128)} %broadcast_select_fusion), channel_id=1, source_target_pairs={{0,16},{16,0},{32,48},{48,32},{64,80},{80,64},{96,112},{112,96},{1... | collective-permute-start | bytes 1966088 | tf_op jit(solution)/shard_map/ppermute | solution.py:447
  49.4 6.1 %copy-start.9 = (s32[2]{0:T(128)}, s32[2]{0:T(128)S(1)}, u32[]{:S(2)}) copy-start(s32[2]{0:T(128)S(1)} %pad_add_fusion.1.place) | copy-start | bytes 28
  60.1 37.5 %all-to-all-start.1 = ((f32[16,288,128]{2,1,0:T(8,128)}), f32[16,288,128]{2,1,0:T(8,128)S(1)}, u32[]{:S(2)}, u32[]{:S(2)}) async-start(f32[16,288,128]{2,1,0:T(8,128)} %pick.4), calls=%async_computation.1 | async-start | bytes 4718592 | tf_op jit(solution)/shard_map/all_to_all | solution.py:437
  68.7 2.3 %copy-start = (f32[96,96,96]{2,1,0:T(8,128)S(1)}, f32[96,96,96]{2,1,0:T(8,128)}, u32[]{:S(2)}) copy-start(f32[96,96,96]{2,1,0:T(8,128)} %coupling.1) | copy-start | bytes 10616836
  71.1 0.8 copy-start.5
  73.2 6.3 %copy-start.2 = (f32[8,2,9216]{2,1,0:T(2,128)S(1)}, f32[8,2,9216]{2,1,0:T(2,128)}, u32[]{:S(2)}) copy-start(f32[8,2,9216]{2,1,0:T(2,128)} %param.12) | copy-start | bytes 1769476
  73.2 6.4 %copy-start.8 = (f32[78]{0:T(128)S(1)}, f32[78]{0:T(128)}, u32[]{:S(2)}) copy-start(f32[78]{0:T(128)} %get-tuple-element.17.scale) | copy-start | bytes 940
  97.6 30.0 %copy-start.6 = (s32[768]{0:T(1024)S(1)}, s32[768]{0:T(1024)}, u32[]{:S(2)}) copy-start(s32[768]{0:T(1024)} %get-tuple-element.18.links) | copy-start | bytes 9220
  121.8 15.6 %collective-permute-start.7 = (f32[16,72,128]{2,1,0:T(8,128)S(1)}, f32[16,72,128]{2,1,0:T(8,128)S(1)}, u32[]{:S(2)}, u32[]{:S(2)}) collective-permute-start(f32[16,72,128]{2,1,0:T(8,128)S(1)} %all_to_all.31.own), channel_id=1, source_target_pairs={{32,0},{48,16},{64,32},{80,48},{96,64},{112,80},{33,1},{49,17},{65... | collective-permute-start | bytes 1769480 | tf_op jit(solution)/shard_map/ppermute | solution.py:26
  123.0 15.5 %collective-permute-start.8 = (f32[16,72,128]{2,1,0:T(8,128)S(1)}, f32[16,72,128]{2,1,0:T(8,128)S(1)}, u32[]{:S(2)}, u32[]{:S(2)}) collective-permute-start(f32[16,72,128]{2,1,0:T(8,128)S(1)} %all_to_all.31.own), channel_id=1, source_target_pairs={{0,32},{16,48},{32,64},{48,80},{64,96},{80,112},{1,33},{17,49},{33... | collective-permute-start | bytes 1769480 | tf_op jit(solution)/shard_map/ppermute | solution.py:26
  129.7 10.9 %copy-start.10 = (s32[2]{0:T(128)S(1)}, s32[2]{0:T(128)}, u32[]{:S(2)}) copy-start(s32[2]{0:T(128)} %copy-done.9) | copy-start | bytes 28
  129.7 21.1 %all-to-all-start.5 = ((f32[16,144,128]{2,1,0:T(8,128)}), f32[16,144,128]{2,1,0:T(8,128)S(1)}, u32[]{:S(2)}, u32[]{:S(2)}) async-start(f32[16,144,128]{2,1,0:T(8,128)} %pick.7), calls=%async_computation.5 | async-start | bytes 2359296 | tf_op jit(solution)/shard_map/all_to_all | solution.py:437
  133.4 5.2 %collective-permute-start.6 = (f32[16,72,128]{2,1,0:T(8,128)S(1)}, f32[16,72,128]{2,1,0:T(8,128)S(1)}, u32[]{:S(2)}, u32[]{:S(2)}) collective-permute-start(f32[16,72,128]{2,1,0:T(8,128)S(1)} %all_to_all.31.own), channel_id=1, source_target_pairs={{0,16},{16,0},{32,48},{48,32},{64,80},{80,64},{96,112},{112,96},{1... | collective-permute-start | bytes 1769480 | tf_op jit(solution)/shard_map/ppermute | solution.py:443
  138.6 2.1 %collective-permute-start.9 = (f32[16,72,128]{2,1,0:T(8,128)S(1)}, f32[16,72,128]{2,1,0:T(8,128)S(1)}, u32[]{:S(2)}, u32[]{:S(2)}) collective-permute-start(f32[16,72,128]{2,1,0:T(8,128)S(1)} %broadcast_select_fusion.1), channel_id=1, source_target_pairs={{0,16},{16,0},{32,48},{48,32},{64,80},{80,64},{96,112},{112,96},{1... | collective-permute-start | bytes 1769480 | tf_op jit(solution)/shard_map/ppermute | solution.py:447
  150.9 34.9 %all-to-all-start.4 = ((f32[16,288,128]{2,1,0:T(8,128)}), f32[16,288,128]{2,1,0:T(8,128)S(1)}, u32[]{:S(2)}, u32[]{:S(2)}) async-start(f32[16,288,128]{2,1,0:T(8,128)} %pick.6), calls=%async_computation.4 | async-start | bytes 4718592 | tf_op jit(solution)/shard_map/all_to_all | solution.py:437
  154.8 1.1 copy-start.3
  (2 other events, 1.3 us)
